TPU v7x, 128 devices: a whole 4x4x4 slice. The times are simulated.
128 devices in a mesh: rows: 4 (over y_lo, core), img: 32 (over x, z, y_hi).
Axes of the slice: x: 4, y: 4 (y_hi: 2, y_lo: 2; y = y_hi * 2 + y_lo), z: 4, core: 2. Of those that a mesh axis runs over, the one named last changes fastest.
Arguments:
- features: bfloat16 [32, 8, 72, 2048], P('img', 'rows')
- image_size: int32 [32, 2], replicated, may hold values from 4 to 72, as said below
- reduce_weight: bfloat16 [2048, 512], P('img'), may hold values from -0.125 to 0.125
- dilated_weight: bfloat16 [512, 4608], P('img'), may hold values from -0.09375 to 0.09375
- expand_weight: bfloat16 [512, 2048], P('img'), may hold values from -0.25 to 0.25
- head_weight: bfloat16 [4, 2048, 4608], P(None, 'img'), may hold values from -0.046875 to 0.046875
- message_weight: bfloat16 [4, 512, 4608], P(None, 'img'), may hold values from -0.09375 to 0.09375
- gate_weight: bfloat16 [4, 512, 512], P(None, 'img'), may hold values from -0.25 to 0.25
- bottleneck_gain: float32 [2, 512], replicated, may hold values from 0.25 to 1.75
- bottleneck_bias: float32 [2, 512], replicated, may hold values from -2.5 to 2.5
- expand_gain: float32 [2048], replicated, may hold values from 0.25 to 1.75
- expand_bias: float32 [2048], replicated, may hold values from -2.5 to 2.5
- head_gain: float32 [4, 512], replicated, may hold values from 0.25 to 1.75
- head_bias: float32 [4, 512], replicated, may hold values from -2.5 to 2.5
- depth_cotangent: bfloat16 [32, 8, 72, 512], P('img', 'rows'), may hold values from -6 to 6
- seg_cotangent: bfloat16 [32, 8, 72, 512], P('img', 'rows'), may hold values from -6 to 6
Outputs:
- depth_stream: float32 [32, 8, 72, 512], P('img', 'rows')
- seg_stream: float32 [32, 8, 72, 512], P('img', 'rows')
- input_grad: float32 [32, 8, 72, 2048], P('img', 'rows')
- reduce_grad: float32 [2048, 512], P('img')
- dilated_grad: float32 [512, 4608], P('img')
- expand_grad: float32 [512, 2048], P('img')
- head_grad: float32 [4, 2048, 4608], P(None, 'img')
- message_grad: float32 [4, 512, 4608], P(None, 'img')
- gate_grad: float32 [4, 512, 512], P(None, 'img')
- bottleneck_gain_grad: float32 [2, 512], replicated
- bottleneck_bias_grad: float32 [2, 512], replicated
- expand_gain_grad: float32 [2048], replicated
- expand_bias_grad: float32 [2048], replicated
- head_gain_grad: float32 [4, 512], replicated
- head_bias_grad: float32 [4, 512], replicated
Inputs may be any that keep to these rules, and one draw needn't show every extreme that they name: `image_size`: each image's map is either full-size, 8 rows by 72 columns, or half-size, 4 rows by 36 columns; image 0 is full-size and image 1 half-size.
All inputs are finite; a program needn't handle non-finite values.
Results may differ from a plain program's by a relative error of at most 0.028.
Values may be sent and summed in bfloat16 or wider, within the bound.
No kernel may reach another device: no remote copies, remote signals or barrier semaphores. Data moves between devices by JAX's collectives and lax.ppermute only.
A program may use at most 384 MiB of HBM per device.

v0:
```python
import jax
import jax.numpy as jnp
from jax import lax
from jax.sharding import PartitionSpec as P

EPS = 1e-05


def together(arrays, axis):
    ends = [0]
    for a in arrays:
        ends.append(ends[-1] + a.size)
    running = lax.psum(jnp.concatenate([a.ravel() for a in arrays]), axis)
    return tuple((running[b:e].reshape(a.shape) for a, b, e in zip(arrays, ends, ends[1:])))


def padded_2(value, sides, width):
    for axis, dim in sides:
        count, length = (lax.axis_size(axis), value.shape[dim])
        up = [(i, (i + 1) % count) for i in range(count - 1)]
        down = [(j, i) for i, j in up]
        last = lax.slice_in_dim(value, length - width, length, axis=dim)
        leading = lax.slice_in_dim(value, 0, width, axis=dim)
        before = lax.ppermute(last, axis, up)
        after = lax.ppermute(leading, axis, down)
        value = jnp.concatenate([before, value, after], axis=dim)
    return value


def sent_together(arrays, axis, dim, along):
    widths = [a.shape[along] for a in arrays]
    both = jnp.concatenate(arrays, axis=along)
    result = lax.all_gather(both, axis, axis=dim, tiled=True)
    return tuple(jnp.split(result, [sum(widths[:k]) for k in range(1, len(widths))], axis=along))


def sent_together_2(arrays, axis, dim, along):
    ends, at = ([], 0)
    for a in arrays[:-1]:
        at += a.shape[along]
        ends.append(at)
    both = jnp.concatenate(arrays, axis=along)
    return tuple(
        jnp.split(lax.psum_scatter(both, axis, scatter_dimension=dim, tiled=True), ends, axis=along)
    )


def pad_cols(tensor, dilation):
    margins = [(0, 0)] * (tensor.ndim - 2) + [(dilation, dilation), (0, 0)]
    return jnp.pad(tensor, margins)


def conv_taps(padded, weight, dilation, strip_rows, strip_cols, pattern):
    out_width = weight.shape[-1] // 9
    summed = None
    for tap_row in range(3):
        for tap_col in range(3):
            tap_index = tap_row * 3 + tap_col
            window = padded[
                ...,
                tap_row * dilation : tap_row * dilation + strip_rows,
                tap_col * dilation : tap_col * dilation + strip_cols,
                :,
            ]
            product = jnp.einsum(
                pattern,
                window,
                weight[..., tap_index * out_width : (tap_index + 1) * out_width],
                preferred_element_type=jnp.float32,
            )
            summed = product if summed is None else summed + product
    return summed


def conv_input(padded, weight, dilation, strip_rows, strip_cols, pattern):
    out_width = weight.shape[-1] // 9
    summed = None
    for tap_row in range(3):
        for tap_col in range(3):
            tap_index = tap_row * 3 + tap_col
            row_from = (2 - tap_row) * dilation
            col_from = (2 - tap_col) * dilation
            window = padded[
                ..., row_from : row_from + strip_rows, col_from : col_from + strip_cols, :
            ]
            product = jnp.einsum(
                pattern,
                window,
                weight[..., tap_index * out_width : (tap_index + 1) * out_width],
                preferred_element_type=jnp.float32,
            )
            summed = product if summed is None else summed + product
    return summed


def conv_weight(padded, upstream, dilation, strip_rows, strip_cols, pattern):
    blocks = []
    for tap_row in range(3):
        for tap_col in range(3):
            window = padded[
                ...,
                tap_row * dilation : tap_row * dilation + strip_rows,
                tap_col * dilation : tap_col * dilation + strip_cols,
                :,
            ]
            blocks.append(jnp.einsum(pattern, window, upstream, preferred_element_type=jnp.float32))
    return jnp.concatenate(blocks, axis=-1)


def norm_forward(tensor, inside, gains_in, shift_bias, pixel_count):
    pixel_axes = (-4, -3, -2)
    firsts = jnp.sum(tensor * inside, axis=pixel_axes, keepdims=True)
    seconds = jnp.sum(tensor * tensor * inside, axis=pixel_axes, keepdims=True)
    firsts, seconds = together((firsts, seconds), ("rows", "img"))
    average = firsts / pixel_count
    inverse = lax.rsqrt(seconds / pixel_count - average * average + EPS)
    centred = (tensor - average) * inverse
    return (gains_in * centred + shift_bias, centred, inverse)


def norm_backward(upstream, centred, inverse, gains_in, inside, pixel_count):
    pixel_axes = (-4, -3, -2)
    gain_sum = jnp.sum(upstream * centred, axis=pixel_axes, keepdims=True)
    bias_sum = jnp.sum(upstream, axis=pixel_axes, keepdims=True)
    gain_sum, bias_sum = together((gain_sum, bias_sum), ("rows", "img"))
    lowered = (
        inside * gains_in * inverse * (upstream - (bias_sum + centred * gain_sum) / pixel_count)
    )
    return (lowered, gain_sum, bias_sum)


def gelu_back(before, upstream):
    unused, pullback = jax.vjp(jax.nn.gelu, before)
    return pullback(upstream)[0]


def extend_heads(stacked):
    return padded_2(stacked, (("rows", 2),), 1)


def extend_back(stacked):
    return padded_2(stacked, (("rows", 2),), 1)


def shards(
    features,
    image_size,
    reduce_weight,
    dilated_weight,
    expand_weight,
    head_weight,
    message_weight,
    gate_weight,
    bottleneck_gain,
    bottleneck_bias,
    expand_gain,
    expand_bias,
    head_gain,
    head_bias,
    depth_cotangent,
    seg_cotangent,
):
    images_here, strip_rows, strip_cols, width_in = features.shape
    first_image = lax.axis_index("img") * images_here
    sizes_here = lax.dynamic_slice_in_dim(image_size, first_image, images_here, 0)
    row_ids = lax.axis_index("rows") * strip_rows + jnp.arange(strip_rows, dtype=jnp.int32)
    col_ids = jnp.arange(strip_cols, dtype=jnp.int32)
    valid = (row_ids[None, :, None] < sizes_here[:, 0, None, None]) & (
        col_ids[None, None, :] < sizes_here[:, 1, None, None]
    )
    inside = valid.astype(jnp.float32)[..., None]
    pixel_count = jnp.sum(
        image_size[:, 0].astype(jnp.float32) * image_size[:, 1].astype(jnp.float32)
    )
    whole_reduce, whole_dilated, whole_expand, whole_head, whole_message, whole_gate = (
        lax.all_gather(reduce_weight, "img", axis=0, tiled=True),
        *sent_together((dilated_weight, expand_weight), "img", 0, 1),
        lax.all_gather(head_weight, "img", axis=1, tiled=True),
        *sent_together((message_weight, gate_weight), "img", 1, 2),
    )
    base_in = features * inside.astype(jnp.bfloat16)
    pre_one = jnp.einsum("irwc,cm->irwm", base_in, whole_reduce, preferred_element_type=jnp.float32)
    norm_one, centred_one, inverse_one = norm_forward(
        pre_one, inside, bottleneck_gain[0], bottleneck_bias[0], pixel_count
    )
    act_one = (jax.nn.gelu(norm_one) * inside).astype(jnp.bfloat16)
    padded_one = pad_cols(padded_2(act_one, (("rows", 1),), 2), 2)
    pre_two = conv_taps(padded_one, whole_dilated, 2, strip_rows, strip_cols, "irwc,co->irwo")
    norm_two, centred_two, inverse_two = norm_forward(
        pre_two, inside, bottleneck_gain[1], bottleneck_bias[1], pixel_count
    )
    act_two = (jax.nn.gelu(norm_two) * inside).astype(jnp.bfloat16)
    pre_three = jnp.einsum(
        "irwm,mc->irwc", act_two, whole_expand, preferred_element_type=jnp.float32
    )
    norm_three, centred_three, inverse_three = norm_forward(
        pre_three, inside, expand_gain, expand_bias, pixel_count
    )
    joined = norm_three + base_in.astype(jnp.float32)
    trunk = (jax.nn.gelu(joined) * inside).astype(jnp.bfloat16)
    padded_trunk = pad_cols(extend_heads(trunk[None]), 1)[0]
    pre_head = conv_taps(padded_trunk, whole_head, 1, strip_rows, strip_cols, "irwc,kco->kirwo")
    head_gains = head_gain[:, None, None, None, :]
    norm_head, centred_head, inverse_head = norm_forward(
        pre_head, inside, head_gains, head_bias[:, None, None, None, :], pixel_count
    )
    task = (jax.nn.gelu(norm_head) * inside).astype(jnp.bfloat16)
    head_count = task.shape[0]
    padded_task = pad_cols(extend_heads(task), 1)
    message = conv_taps(padded_task, whole_message, 1, strip_rows, strip_cols, "kirwc,kco->kirwo")
    gate = jax.nn.sigmoid(
        jnp.einsum("kirwc,kcd->kirwd", task, whole_gate, preferred_element_type=jnp.float32)
    )
    gated_msg = gate * message
    task_wide = task.astype(jnp.float32)
    depth_out = (task_wide[0] + gated_msg[1] + gated_msg[2] + gated_msg[3]) * inside
    seg_out = (task_wide[1] + gated_msg[0] + gated_msg[2] + gated_msg[3]) * inside
    cot_depth = depth_cotangent.astype(jnp.float32) * inside
    cot_seg = seg_cotangent.astype(jnp.float32) * inside
    cot_both = cot_depth + cot_seg
    receive = jnp.stack([cot_seg, cot_depth, cot_both, cot_both])
    zeros_map = jnp.zeros_like(cot_depth)
    direct = jnp.stack([cot_depth, cot_seg, zeros_map, zeros_map])
    d_logit = (receive * message * gate * (1.0 - gate)).astype(jnp.bfloat16)
    d_message = (receive * gate).astype(jnp.bfloat16)
    padded_dmsg = pad_cols(extend_back(d_message), 1)
    d_task = direct + jnp.einsum(
        "kirwd,kcd->kirwc", d_logit, whole_gate, preferred_element_type=jnp.float32
    )
    d_task = d_task + conv_input(
        padded_dmsg, whole_message, 1, strip_rows, strip_cols, "kirwo,kco->kirwc"
    )
    d_norm_head = gelu_back(norm_head, d_task * inside)
    d_pre_head, head_gain_sum, head_bias_sum = norm_backward(
        d_norm_head, centred_head, inverse_head, head_gains, inside, pixel_count
    )
    d_pre_head = d_pre_head.astype(jnp.bfloat16)
    padded_dhead = pad_cols(extend_back(d_pre_head), 1)
    head_shares = []
    for head_index in range(head_count):
        grad_head_one = conv_weight(
            padded_trunk, d_pre_head[head_index], 1, strip_rows, strip_cols, "irwc,irwo->co"
        )
        grad_message_one = conv_weight(
            padded_task[head_index],
            d_message[head_index],
            1,
            strip_rows,
            strip_cols,
            "irwc,irwo->co",
        )
        grad_gate_one = jnp.einsum(
            "irwc,irwd->cd",
            task[head_index],
            d_logit[head_index],
            preferred_element_type=jnp.float32,
        )
        shares_now = (
            lax.psum_scatter(
                grad_head_one.astype(jnp.bfloat16), "img", scatter_dimension=0, tiled=True
            ).astype(jnp.float32),
            *tuple(
                (
                    part.astype(jnp.float32)
                    for part in sent_together_2(
                        (grad_message_one.astype(jnp.bfloat16), grad_gate_one.astype(jnp.bfloat16)),
                        "img",
                        0,
                        1,
                    )
                )
            ),
        )
        head_shares.append(shares_now)
    d_trunk = conv_input(padded_dhead, whole_head, 1, strip_rows, strip_cols, "kirwo,kco->irwc")
    d_joined = gelu_back(joined, d_trunk * inside)
    d_pre_three, expand_gain_sum, expand_bias_sum = norm_backward(
        d_joined, centred_three, inverse_three, expand_gain, inside, pixel_count
    )
    d_pre_three = d_pre_three.astype(jnp.bfloat16)
    grad_expand = jnp.einsum(
        "irwm,irwc->mc", act_two, d_pre_three, preferred_element_type=jnp.float32
    )
    d_act_two = jnp.einsum(
        "irwc,mc->irwm", d_pre_three, whole_expand, preferred_element_type=jnp.float32
    )
    d_norm_two = gelu_back(norm_two, d_act_two * inside)
    d_pre_two, second_gain_sum, second_bias_sum = norm_backward(
        d_norm_two, centred_two, inverse_two, bottleneck_gain[1], inside, pixel_count
    )
    d_pre_two = d_pre_two.astype(jnp.bfloat16)
    padded_dtwo = pad_cols(padded_2(d_pre_two, (("rows", 1),), 2), 2)
    grad_dilated = conv_weight(padded_one, d_pre_two, 2, strip_rows, strip_cols, "irwc,irwo->co")
    d_act_one = conv_input(padded_dtwo, whole_dilated, 2, strip_rows, strip_cols, "irwo,co->irwc")
    d_norm_one = gelu_back(norm_one, d_act_one * inside)
    d_pre_one, first_gain_sum, first_bias_sum = norm_backward(
        d_norm_one, centred_one, inverse_one, bottleneck_gain[0], inside, pixel_count
    )
    d_pre_one = d_pre_one.astype(jnp.bfloat16)
    grad_reduce = jnp.einsum(
        "irwc,irwm->cm", base_in, d_pre_one, preferred_element_type=jnp.float32
    )
    d_base = d_joined + jnp.einsum(
        "irwm,cm->irwc", d_pre_one, whole_reduce, preferred_element_type=jnp.float32
    )
    input_grad = d_base * inside
    trunk_shares = (
        lax.psum_scatter(
            grad_reduce.astype(jnp.bfloat16), "img", scatter_dimension=0, tiled=True
        ).astype(jnp.float32),
        lax.psum_scatter(
            grad_dilated.astype(jnp.bfloat16), "img", scatter_dimension=0, tiled=True
        ).astype(jnp.float32),
        lax.psum_scatter(
            grad_expand.astype(jnp.bfloat16), "img", scatter_dimension=0, tiled=True
        ).astype(jnp.float32),
    )
    stacked_head = jnp.stack([entry[0] for entry in head_shares])
    stacked_message = jnp.stack([entry[1] for entry in head_shares])
    stacked_gate = jnp.stack([entry[2] for entry in head_shares])
    sum_reduce, sum_dilated, sum_expand, sum_head, sum_message, sum_gate = tuple(
        (
            part.astype(jnp.float32)
            for part in together(
                (
                    trunk_shares[0].astype(jnp.bfloat16),
                    trunk_shares[1].astype(jnp.bfloat16),
                    trunk_shares[2].astype(jnp.bfloat16),
                    stacked_head.astype(jnp.bfloat16),
                    stacked_message.astype(jnp.bfloat16),
                    stacked_gate.astype(jnp.bfloat16),
                ),
                "rows",
            )
        )
    )
    bottleneck_gain_grad = jnp.stack([first_gain_sum.reshape(-1), second_gain_sum.reshape(-1)])
    bottleneck_bias_grad = jnp.stack([first_bias_sum.reshape(-1), second_bias_sum.reshape(-1)])
    return (
        depth_out,
        seg_out,
        input_grad,
        sum_reduce,
        sum_dilated,
        sum_expand,
        sum_head,
        sum_message,
        sum_gate,
        bottleneck_gain_grad,
        bottleneck_bias_grad,
        expand_gain_sum.reshape(-1),
        expand_bias_sum.reshape(-1),
        head_gain_sum.reshape(head_count, -1),
        head_bias_sum.reshape(head_count, -1),
    )


def solution(mesh):
    placed = (
        P("img", "rows", None, None),
        P(),
        P("img", None),
        P("img", None),
        P("img", None),
        P(None, "img", None),
        P(None, "img", None),
        P(None, "img", None),
        P(),
        P(),
        P(),
        P(),
        P(),
        P(),
        P("img", "rows", None, None),
        P("img", "rows", None, None),
    )
    return jax.shard_map(
        shards,
        mesh=mesh,
        in_specs=placed,
        out_specs=(
            P("img", "rows", None, None),
            P("img", "rows", None, None),
            P("img", "rows", None, None),
            P("img", None),
            P("img", None),
            P("img", None),
            P(None, "img", None),
            P(None, "img", None),
            P(None, "img", None),
            P(),
            P(),
            P(),
            P(),
            P(),
            P(),
        ),
        check_vma=False,
    )
```

profile of v0, /device:TPU:1, one launch (start us, length us, event | category | flops | bytes accessed | tf_op | source)
XLA Modules:
  0.0 3749.8 jit_solution(6092920002098132178)
XLA Ops:
  14.1 69.7 %all-gather.5.cloned.1.call-done = bf16[2048,512]{1,0:T(8,128)(2,1)} async-done(((bf16[64,512]{1,0:T(8,128)(2,1)}), bf16[2048,512]{1,0:T(8,128)(2,1)}) %all-gather.5.cloned.1.call-update) | async-done | bytes 2097168 | tf_op jit(solution)/shard_map/all_gather | solution.py:176
  86.0 65.7 %psum.63 = f32[1024]{0:T(1024)S(1)} all-reduce(f32[1024]{0:T(1024)S(1)} %pad_maximum_fusion.16), channel_id=1, replica_groups=mesh['rows'=4,'img'=32] {'rows','img'}, use_global_device_ids=true, to_apply=%region_2.0 | all-reduce | flops 1024 | bytes 8192 | tf_op jit(solution)/shard_map/psum | solution.py:13
  152.5 22.0 collective-permute-start.1
  193.3 120.6 %psum.64 = f32[1024]{0:T(1024)S(1)} all-reduce(f32[1024]{0:T(1024)S(1)} %pad_maximum_fusion.17), channel_id=1, replica_groups=mesh['rows'=4,'img'=32] {'rows','img'}, use_global_device_ids=true, to_apply=%region_6.7 | all-reduce | flops 1024 | bytes 8192 | tf_op jit(solution)/shard_map/psum | solution.py:13
  317.1 69.8 %psum.65 = f32[4096]{0:T(1024)S(1)} all-reduce(f32[4096]{0:T(1024)S(1)} %pad_maximum_fusion.12), channel_id=1, replica_groups=mesh['rows'=4,'img'=32] {'rows','img'}, use_global_device_ids=true, to_apply=%region_9.10 | all-reduce | flops 4096 | bytes 32768 | tf_op jit(solution)/shard_map/psum | solution.py:13
  388.4 14.2 collective-permute-start.3
  405.0 9.5 collective-permute-done.2
  414.9 295.9 %all-gather.9.cloned.1.call-done = bf16[4,2048,4608]{2,1,0:T(8,128)(2,1)} async-done(((bf16[4,64,4608]{2,1,0:T(8,128)(2,1)}), bf16[4,2048,4608]{2,1,0:T(8,128)(2,1)}) %all-gather.9.cloned.1.call-update) | async-done | bytes 75497488 | tf_op jit(solution)/shard_map/all_gather | solution.py:178
  754.8 121.6 %psum.66 = f32[4096]{0:T(1024)S(1)} all-reduce(f32[4096]{0:T(1024)S(1)} %pad_maximum_fusion.13), channel_id=1, replica_groups=mesh['rows'=4,'img'=32] {'rows','img'}, use_global_device_ids=true, to_apply=%region_12.13 | all-reduce | flops 4096 | bytes 32768 | tf_op jit(solution)/shard_map/psum | solution.py:13
  934.0 64.3 %psum.67 = f32[4096]{0:T(1024)S(1)} all-reduce(f32[4096]{0:T(1024)S(1)} %pad_maximum_fusion.14), channel_id=1, replica_groups=mesh['rows'=4,'img'=32] {'rows','img'}, use_global_device_ids=true, to_apply=%region_15.16 | all-reduce | flops 4096 | bytes 32768 | tf_op jit(solution)/shard_map/psum | solution.py:13
  1057.8 8.5 fusion.264
  1066.3 62.4 %psum.68 = f32[4096]{0:T(1024)S(1)} all-reduce(f32[4096]{0:T(1024)S(1)} %pad_maximum_fusion.15), channel_id=1, replica_groups=mesh['rows'=4,'img'=32] {'rows','img'}, use_global_device_ids=true, to_apply=%region_18.19 | all-reduce | flops 4096 | bytes 32768 | tf_op jit(solution)/shard_map/psum | solution.py:13
  1137.9 65.6 %psum.69 = f32[1024]{0:T(1024)S(1)} all-reduce(f32[1024]{0:T(1024)S(1)} %pad_maximum_fusion.18), channel_id=1, replica_groups=mesh['rows'=4,'img'=32] {'rows','img'}, use_global_device_ids=true, to_apply=%region_21.22 | all-reduce | flops 1024 | bytes 8192 | tf_op jit(solution)/shard_map/psum | solution.py:13
  1226.7 67.1 %psum.70 = f32[1024]{0:T(1024)S(1)} all-reduce(f32[1024]{0:T(1024)S(1)} %pad_maximum_fusion.19), channel_id=1, replica_groups=mesh['rows'=4,'img'=32] {'rows','img'}, use_global_device_ids=true, to_apply=%region_24.25 | all-reduce | flops 1024 | bytes 8192 | tf_op jit(solution)/shard_map/psum | solution.py:13
  1332.5 8.0 copy.232
  1353.3 7.8 copy.230
  1374.0 7.9 copy.228
  1393.9 8.0 copy.226
  1422.7 23.1 copy.224
  1465.6 24.7 copy.222
  1510.3 24.8 copy.220
  1555.0 24.9 copy.218
  1582.6 148.3 %reduce-scatter.34.cloned.1.call-done = bf16[16,4608]{1,0:T(8,128)(2,1)} async-done(((bf16[512,4608]{1,0:T(8,128)(2,1)}), bf16[16,4608]{1,0:T(8,128)(2,1)}) %reduce-scatter.34.cloned.1.call-update) | async-done | bytes 147472 | tf_op jit(solution)/shard_map/reduce_scatter | solution.py:311
  1733.3 171.5 %reduce-scatter.50.cloned.1.call-done = bf16[16,5120]{1,0:T(8,128)(2,1)} async-done(((bf16[512,5120]{1,0:T(8,128)(2,1)}), bf16[16,5120]{1,0:T(8,128)(2,1)}) %reduce-scatter.50.cloned.1.call-update) | async-done | bytes 163856
  1906.7 190.4 %reduce-scatter.48.cloned.1.call-done = bf16[16,5120]{1,0:T(8,128)(2,1)} async-done(((bf16[512,5120]{1,0:T(8,128)(2,1)}), bf16[16,5120]{1,0:T(8,128)(2,1)}) %reduce-scatter.48.cloned.1.call-update) | async-done | bytes 163856
  2098.9 191.0 %reduce-scatter.46.cloned.1.call-done = bf16[16,5120]{1,0:T(8,128)(2,1)} async-done(((bf16[512,5120]{1,0:T(8,128)(2,1)}), bf16[16,5120]{1,0:T(8,128)(2,1)}) %reduce-scatter.46.cloned.1.call-update) | async-done | bytes 163856
  2291.6 190.9 %reduce-scatter.44.cloned.1.call-done = bf16[16,5120]{1,0:T(8,128)(2,1)} async-done(((bf16[512,5120]{1,0:T(8,128)(2,1)}), bf16[16,5120]{1,0:T(8,128)(2,1)}) %reduce-scatter.44.cloned.1.call-update) | async-done | bytes 163856
  2487.5 298.4 %reduce-scatter.42.cloned.1.call-done = bf16[64,4608]{1,0:T(8,128)(2,1)} async-done(((bf16[2048,4608]{1,0:T(8,128)(2,1)}), bf16[64,4608]{1,0:T(8,128)(2,1)}) %reduce-scatter.42.cloned.1.call-update) | async-done | bytes 589840
  2787.5 280.1 %reduce-scatter.40.cloned.1.call-done = bf16[64,4608]{1,0:T(8,128)(2,1)} async-done(((bf16[2048,4608]{1,0:T(8,128)(2,1)}), bf16[64,4608]{1,0:T(8,128)(2,1)}) %reduce-scatter.40.cloned.1.call-update) | async-done | bytes 589840
  3069.3 281.2 %reduce-scatter.38.cloned.1.call-done = bf16[64,4608]{1,0:T(8,128)(2,1)} async-done(((bf16[2048,4608]{1,0:T(8,128)(2,1)}), bf16[64,4608]{1,0:T(8,128)(2,1)}) %reduce-scatter.38.cloned.1.call-update) | async-done | bytes 589840
  3352.1 279.8 %reduce-scatter.36.cloned.1.call-done = bf16[64,4608]{1,0:T(8,128)(2,1)} async-done(((bf16[2048,4608]{1,0:T(8,128)(2,1)}), bf16[64,4608]{1,0:T(8,128)(2,1)}) %reduce-scatter.36.cloned.1.call-update) | async-done | bytes 589840
  3656.2 70.6 %all-reduce.8.cloned.1.call-done = bf16[1646592]{0:T(1024)(128)(2,1)} async-done(((bf16[1646592]{0:T(1024)(128)(2,1)}), bf16[1646592]{0:T(1024)(128)(2,1)}) %all-reduce.8.cloned.1.call-update) | async-done | bytes 3293200 | tf_op jit(solution)/shard_map/psum | solution.py:13
  (453 shorter events, 445.7 us)
Async XLA Ops:
  7.2 76.6 %all-gather.5.cloned.1.call-start = ((), (), s32[]{:S(2)}) async-start(), calls=%async_computation.11 | async-start | bytes 2162688 | tf_op jit(solution)/shard_map/all_gather | solution.py:176
  7.9 173.6 %all-gather.7.cloned.1.call-start = ((), (), s32[]{:S(2)}) async-start(), calls=%async_computation.12 | async-start | bytes 7028736 | tf_op jit(solution)/shard_map/all_gather | solution.py:33
  9.7 701.1 %all-gather.9.cloned.1.call-start = ((), (), s32[]{:S(2)}) async-start(), calls=%async_computation.13 | async-start | bytes 77856768 | tf_op jit(solution)/shard_map/all_gather | solution.py:178
  10.4 885.4 %all-gather.11.cloned.1.call-start = ((), (), s32[]{:S(2)}) async-start(), calls=%async_computation.14 | async-start | bytes 21626880 | tf_op jit(solution)/shard_map/all_gather | solution.py:33
  11.4 1568.8 %reduce-scatter.32.cloned.1.call-start = ((), (), s32[]{:S(2)}) async-start(), calls=%async_computation.16 | async-start | bytes 2162688 | tf_op jit(solution)/shard_map/reduce_scatter | solution.py:314
  14.1 1043.7 %copy-start.58 = (bf16[2,72]{1,0:T(2,128)(2,1)}, bf16[2,72]{1,0:T(2,128)(2,1)S(1)}, u32[]{:S(2)}) copy-start(bf16[2,72]{1,0:T(2,128)(2,1)S(1)} %get-tuple-element.131) | copy-start | bytes 868
  14.1 1292.7 %copy-start.37 = (f32[2,72]{1,0:T(2,128)}, f32[2,72]{1,0:T(2,128)S(1)}, u32[]{:S(2)}) copy-start(f32[2,72]{1,0:T(2,128)S(1)} %get-tuple-element.132) | copy-start | bytes 1732
  152.5 23.9 collective-permute-start.1
  174.5 4.0 collective-permute-start
  388.4 16.6 collective-permute-start.3
  402.6 11.9 collective-permute-start.2
  414.9 334.9 %copy-start.25 = (bf16[1,4,74,2048]{3,2,1,0:T(8,128)(2,1)}, bf16[1,4,74,2048]{3,2,1,0:T(8,128)(2,1)S(1)}, u32[]{:S(2)}) copy-start(bf16[1,4,74,2048]{3,2,1,0:T(8,128)(2,1)S(1)} %fusion.143) | copy-start | bytes 3637252
  749.8 127.3 %copy-start.42 = (f32[4,512]{1,0:T(4,128)S(1)}, f32[4,512]{1,0:T(4,128)}, u32[]{:S(2)}) copy-start(f32[4,512]{1,0:T(4,128)} %param.28) | copy-start | bytes 24580
  878.9 8.4 collective-permute-start.5
  881.4 6.8 collective-permute-start.4
  914.0 8.0 collective-permute-start.7
  917.0 6.1 collective-permute-start.6
  1001.2 18.5 collective-permute-start.9
  1004.0 9.4 collective-permute-start.8
  1134.4 446.7 %reduce-scatter.30.cloned.1.call-start = ((), (), s32[]{:S(2)}) async-start(), calls=%async_computation.15 | async-start | bytes 2162688 | tf_op jit(solution)/shard_map/reduce_scatter | solution.py:308
  1205.3 7.8 collective-permute-start.11
  1208.6 4.6 collective-permute-start.10
  1300.0 430.9 %reduce-scatter.34.cloned.1.call-start = ((), (), s32[]{:S(2)}) async-start(), calls=%async_computation.18 | async-start | bytes 4866048 | tf_op jit(solution)/shard_map/reduce_scatter | solution.py:311
  1319.6 585.3 %reduce-scatter.50.cloned.1.call-start = ((), (), s32[]{:S(2)}) async-start(), calls=%async_computation.26 | async-start | bytes 5406720
  1340.5 756.6 %reduce-scatter.48.cloned.1.call-start = ((), (), s32[]{:S(2)}) async-start(), calls=%async_computation.25 | async-start | bytes 5406720
  1361.2 928.7 %reduce-scatter.46.cloned.1.call-start = ((), (), s32[]{:S(2)}) async-start(), calls=%async_computation.24 | async-start | bytes 5406720
  1381.9 1100.6 %reduce-scatter.44.cloned.1.call-start = ((), (), s32[]{:S(2)}) async-start(), calls=%async_computation.23 | async-start | bytes 5406720
  1401.9 1384.0 %reduce-scatter.42.cloned.1.call-start = ((), (), s32[]{:S(2)}) async-start(), calls=%async_computation.22 | async-start | bytes 19464192
  1445.9 1621.8 %reduce-scatter.40.cloned.1.call-start = ((), (), s32[]{:S(2)}) async-start(), calls=%async_computation.21 | async-start | bytes 19464192
  1490.4 1860.1 %reduce-scatter.38.cloned.1.call-start = ((), (), s32[]{:S(2)}) async-start(), calls=%async_computation.20 | async-start | bytes 19464192
  1535.1 2096.9 %reduce-scatter.36.cloned.1.call-start = ((), (), s32[]{:S(2)}) async-start(), calls=%async_computation.19 | async-start | bytes 19464192
  1579.9 2147.0 %all-reduce.8.cloned.1.call-start = ((), (), s32[]{:S(2)}) async-start(), calls=%async_computation.17 | async-start | bytes 6586368 | tf_op jit(solution)/shard_map/psum | solution.py:13
  (65 other events, 972.6 us)
Sparse Core Ops, SparseCore 0:
  11.0 72.7 all-gather.4
  87.4 94.0 all-gather.6
  184.6 526.1 all-gather.8
  714.2 181.6 all-gather.10
  1134.5 160.9 reduce-scatter.31
  1300.1 179.1 reduce-scatter.29
  1484.4 246.4 reduce-scatter.33
  1733.5 171.3 reduce-scatter.49
  1907.4 189.6 reduce-scatter.47
  2099.4 190.3 reduce-scatter.45
  2292.4 190.0 reduce-scatter.43
  2489.1 296.7 reduce-scatter.41
  2791.7 275.9 reduce-scatter.39
  3074.3 276.1 reduce-scatter.37
  3356.1 275.7 reduce-scatter.35
  3651.5 75.3 all-reduce.7
where the time goes:
time: 3760 us; the launch traced here: 3750 us
  waiting for transfers between devices  2500 us (66%)
  blocking collectives  637 us (17%)
  matrix products  308 us (8%)
  local copies, waits for them, and re-layouts  191 us (5%)
  starting transfers between devices  65.7 us (2%)
    unnamed x24, waiting for transfers between devices  1880 us
    psum x8, blocking collectives, together(): running = lax.psum(jnp.concatenate([a.ravel() for a in arrays]), axis)  637 us
    all_gather x1, waiting for transfers between devices, shards(): lax.all_gather(head_weight, 'img', axis=1, tiled=True)  296 us
    unnamed x163, local copies, waits for them, and re-layouts  160 us
    reduce_scatter x1, waiting for transfers between devices, shards(): lax.psum_scatter(grad_dilated.astype(jnp.bfloat16), 'img', scatter_dimens...  148 us
    dot_general x81, matrix products, conv_weight(): jnp.einsum(pattern, window, upstream, preferred_element_type=jnp.float32)  134 us
    dot_general x27, matrix products, conv_input(): jnp.einsum(pattern, window, weight[..., tap_index * out_width:(tap_index...  81.4 us
  transfers between devices with their start and end apart: 28, of which 22 were waited for; matrix products, arithmetic and copies ran while one was open for 11% of the time, Pallas kernels for 0%

commit v1 on v0

v1 whole, which is shorter than its diff:
```python
import functools

import jax
import jax.numpy as jnp
from jax import lax
from jax.experimental import pallas as pl
from jax.experimental.pallas import tpu as pltpu
from jax.sharding import Mesh, PartitionSpec as P

EPS = 1e-05
PITCH = 80
F32 = jnp.float32
BF16 = jnp.bfloat16

FINE = ("ylo", "core", "x", "z", "yhi")
ROWS = ("ylo", "core")
IMG = ("x", "z", "yhi")
RING = ("ylo", "yhi")
GROUP = ("ylo", "core", "yhi")
POOL = ("x", "z", "core")


def swap(value, axis, flip):
    count = lax.axis_size(axis)
    return lax.ppermute(value, axis, [(i, i ^ flip) for i in range(count)])


def over_core(value):
    return swap(value, "core", 1)


def over_y(value, flip):
    return swap(value, RING, {1: 2, 2: 1, 3: 3}[flip])


def total(value, everywhere):
    value = value + over_core(value)
    if everywhere:
        for flip in (1, 3):
            value = value + over_y(value, flip)
    for axis in ("x", "z"):
        for flip in (1, 3):
            value = value + swap(value, axis, flip)
    return value


def in_order(mine, other, bit):
    first = bit == 0
    return jnp.where(first, mine, other), jnp.where(first, other, mine)


def gather_rows(value, ylo, core):
    pair = jnp.concatenate(in_order(value, over_core(value), core))
    return jnp.concatenate(in_order(pair, over_y(pair, 1), ylo))


def at_flip(pieces, flip):
    return jnp.where(
        flip < 2,
        jnp.where(flip == 0, pieces[0], pieces[1]),
        jnp.where(flip == 2, pieces[2], pieces[3]),
    )


def to_heads(value, y, core):
    half = value.shape[0] // 2
    near, far = over_y(value, 1), over_y(value, 3)
    across = jnp.concatenate([over_y(far[:half], 1), over_y(near[half:], 3)])
    pieces = (value, near, across, far)
    keep = [at_flip(pieces, y ^ (2 * core + low)) for low in (0, 1)]
    give = [at_flip(pieces, y ^ (2 * (1 - core) + low)) for low in (0, 1)]
    got = over_core(jnp.concatenate(give))
    got = (got[: value.shape[0]], got[value.shape[0] :])
    strips = []
    for low in (0, 1):
        strips += in_order(keep[low], got[low], core)
    return jnp.concatenate(strips)


def from_heads(value, y, core):
    rows = value.shape[0] // 4
    strip = [value[i * rows : (i + 1) * rows] for i in range(4)]
    own = [jnp.where(core == 0, strip[2 * low], strip[2 * low + 1]) for low in (0, 1)]
    other = [jnp.where(core == 0, strip[2 * low + 1], strip[2 * low]) for low in (0, 1)]
    got = over_core(jnp.concatenate(other).astype(BF16))
    got = [got[:rows], got[rows:]]
    first = [jnp.where(core == 0, own[low].astype(BF16), got[low]) for low in (0, 1)]
    second = [jnp.where(core == 0, got[low], own[low].astype(BF16)) for low in (0, 1)]
    pieces = first + second
    mine, near, across, far = (at_flip(pieces, y ^ flip) for flip in range(4))
    half = rows // 2
    from_near = over_y(across[:half], 1)
    from_far = over_y(across[half:], 3)
    near = jnp.concatenate(
        [near[:half], (near[half:].astype(F32) + from_far.astype(F32)).astype(BF16)]
    )
    far = jnp.concatenate(
        [(far[:half].astype(F32) + from_near.astype(F32)).astype(BF16), far[half:]]
    )
    return mine.astype(F32) + over_y(near, 1).astype(F32) + over_y(far, 3).astype(F32)


def shifted(value, dilation, rows_above, rows_below):
    padded = jnp.pad(
        value,
        ((rows_above * PITCH + dilation, rows_below * PITCH + dilation), (0, 0)),
    )
    length = value.shape[0] + (rows_above + rows_below) * PITCH
    return jnp.stack(
        [padded[k * dilation : k * dilation + length] for k in range(3)]
    )


def conv_body(step, rows, x_ref, w_ref, out_ref):
    tap = pl.program_id(0)
    start = pl.multiple_of((tap // 3) * step, 16)
    part = jnp.dot(
        x_ref[tap % 3, pl.ds(start, rows), :], w_ref[...], preferred_element_type=F32
    )

    @pl.when(tap == 0)
    def _():
        out_ref[...] = part

    @pl.when(tap > 0)
    def _():
        out_ref[...] += part


def conv(stack, weight, step, rows):
    _, length, deep = stack.shape
    wide = 512
    return pl.pallas_call(
        functools.partial(conv_body, step, rows),
        grid=(9,),
        in_specs=[
            pl.BlockSpec((3, length, deep), lambda t: (0, 0, 0)),
            pl.BlockSpec((deep, wide), lambda t: (0, t)),
        ],
        out_specs=pl.BlockSpec((rows, wide), lambda t: (0, 0)),
        out_shape=jax.ShapeDtypeStruct((rows, wide), F32),
        compiler_params=pltpu.CompilerParams(vmem_limit_bytes=48 << 20),
        cost_estimate=pl.CostEstimate(
            flops=2 * 9 * rows * deep * wide,
            bytes_accessed=2 * 9 * deep * wide + 6 * length * deep + 4 * rows * wide,
            transcendentals=0,
        ),
    )(stack, weight)


def conv_t_body(step, rows, g_ref, w_ref, out_ref):
    tap = pl.program_id(1)
    start = pl.multiple_of((2 - tap // 3) * step, 16)
    part = lax.dot_general(
        g_ref[2 - tap % 3, pl.ds(start, rows), :],
        w_ref[...],
        (((1,), (1,)), ((), ())),
        preferred_element_type=F32,
    )

    @pl.when(tap == 0)
    def _():
        out_ref[...] = part

    @pl.when(tap > 0)
    def _():
        out_ref[...] += part


def conv_t(stack, weight, step, rows):
    _, length, wide = stack.shape
    deep = weight.shape[0]
    return pl.pallas_call(
        functools.partial(conv_t_body, step, rows),
        grid=(deep // 512, 9),
        in_specs=[
            pl.BlockSpec((3, length, wide), lambda c, t: (0, 0, 0)),
            pl.BlockSpec((512, wide), lambda c, t: (c, t)),
        ],
        out_specs=pl.BlockSpec((rows, 512), lambda c, t: (0, c)),
        out_shape=jax.ShapeDtypeStruct((rows, deep), F32),
        compiler_params=pltpu.CompilerParams(vmem_limit_bytes=48 << 20),
        cost_estimate=pl.CostEstimate(
            flops=2 * 9 * rows * deep * wide,
            bytes_accessed=2 * 9 * deep * wide + 6 * length * wide + 4 * rows * deep,
            transcendentals=0,
        ),
    )(stack, weight)


def conv_w_body(step, rows, x_ref, g_ref, out_ref):
    tap = pl.program_id(0)
    start = pl.multiple_of((2 - tap // 3) * step, 16)
    out_ref[...] = jnp.dot(
        x_ref[...], g_ref[2 - tap % 3, pl.ds(start, rows), :], preferred_element_type=F32
    ).astype(out_ref.dtype)


def conv_w(turned, stack, step):
    deep, rows = turned.shape
    _, length, wide = stack.shape
    return pl.pallas_call(
        functools.partial(conv_w_body, step, rows),
        grid=(9,),
        in_specs=[
            pl.BlockSpec((deep, rows), lambda t: (0, 0)),
            pl.BlockSpec((3, length, wide), lambda t: (0, 0, 0)),
        ],
        out_specs=pl.BlockSpec((deep, wide), lambda t: (0, t)),
        out_shape=jax.ShapeDtypeStruct((deep, 9 * wide), BF16),
        compiler_params=pltpu.CompilerParams(vmem_limit_bytes=48 << 20),
        cost_estimate=pl.CostEstimate(
            flops=2 * 9 * rows * deep * wide,
            bytes_accessed=2 * 9 * deep * wide + 6 * length * wide + 2 * rows * deep,
            transcendentals=0,
        ),
    )(turned, stack)


def sums_of(value, inside):
    return jnp.stack(
        [jnp.sum(value * inside, axis=0), jnp.sum(value * value * inside, axis=0)]
    )


def norm_of(value, sums, gain, bias, count):
    mean = sums[0] / count
    inverse = lax.rsqrt(sums[1] / count - mean * mean + EPS)
    centred = (value - mean) * inverse
    return gain * centred + bias, centred, inverse


def back_sums(upstream, centred):
    return jnp.stack([jnp.sum(upstream * centred, axis=0), jnp.sum(upstream, axis=0)])


def norm_back(upstream, centred, inverse, gain, inside, sums, count):
    return inside * gain * inverse * (upstream - (sums[1] + centred * sums[0]) / count)


def gelu_back(before, upstream):
    unused, pullback = jax.vjp(jax.nn.gelu, before)
    return pullback(upstream)[0]


def strips_of(value):
    _, rows, across, deep = value.shape
    padded = jnp.pad(value[0], ((0, 0), (0, PITCH - across), (0, 0)))
    return padded.reshape(rows * PITCH, deep)


def maps_of(value, across):
    rows = value.shape[0] // PITCH
    return value.reshape(1, rows, PITCH, -1)[:, :, :across]


def shares_summed(value):
    count = lax.axis_size(IMG)
    parts = lax.all_to_all(
        value.reshape(count, value.shape[0] // count, value.shape[1]), IMG, 0, 0
    )
    return jnp.sum(parts.astype(F32), axis=0)


def shards(
    features,
    image_size,
    reduce_weight,
    dilated_weight,
    expand_weight,
    head_weight,
    message_weight,
    gate_weight,
    bottleneck_gain,
    bottleneck_bias,
    expand_gain,
    expand_bias,
    head_gain,
    head_bias,
    depth_cotangent,
    seg_cotangent,
):
    ylo, core, yhi = (lax.axis_index(a) for a in ("ylo", "core", "yhi"))
    plane = lax.axis_index("x") * 4 + lax.axis_index("z")
    y = yhi * 2 + ylo
    strip = ylo * 2 + core
    across = features.shape[2]
    local = core == yhi

    count = jnp.sum(image_size[:, 0].astype(F32) * image_size[:, 1].astype(F32))

    def inside_of(image, first, rows):
        size = lax.dynamic_index_in_dim(image_size, image, 0, keepdims=False)
        at = jnp.arange(rows * PITCH, dtype=jnp.int32)
        valid = (first + at // PITCH < size[0]) & (at % PITCH < size[1])
        return valid.astype(F32)[:, None]

    inside = inside_of(plane * 2 + yhi, strip * 2, 2)
    inside_whole = inside_of(plane * 2 + core, 0, 8)

    group = [
        (i, i ^ 5) for i in range(8) if (i >> 1) & 1 == i & 1
    ]

    def brought(mine, sent):
        return jnp.where(local, mine, lax.ppermute(sent, GROUP, group))

    def of_head(stacked, head):
        return lax.dynamic_index_in_dim(stacked, head, 0, keepdims=False)

    trunk_weights = jnp.concatenate([dilated_weight, expand_weight], axis=1)
    reduce_part = brought(reduce_weight, reduce_weight)
    pool = lax.all_to_all(
        jnp.broadcast_to(reduce_part[None], (16,) + reduce_part.shape), ("x", "z"), 0, 0
    )
    whole_reduce = jnp.stack(in_order(pool, over_core(pool), core), axis=1).reshape(
        -1, reduce_weight.shape[1]
    )
    trunk_part = brought(trunk_weights, trunk_weights)
    whole_trunk = lax.all_gather(trunk_part, POOL, axis=0, tiled=True)
    wide = dilated_weight.shape[1]
    whole_dilated, whole_expand = whole_trunk[:, :wide], whole_trunk[:, wide:]
    task_weights = jnp.concatenate([message_weight, gate_weight], axis=2)
    head_part = brought(of_head(head_weight, y), of_head(head_weight, y ^ 3))
    task_part = brought(of_head(task_weights, y), of_head(task_weights, y ^ 3))
    whole_head = lax.all_gather(head_part, POOL, axis=0, tiled=True)
    whole_task = lax.all_gather(task_part, POOL, axis=0, tiled=True)
    whole_message, whole_gate = whole_task[:, :wide], whole_task[:, wide:]

    base = strips_of(features) * inside.astype(BF16)
    cotangents = to_heads(
        jnp.concatenate([strips_of(depth_cotangent), strips_of(seg_cotangent)], axis=1),
        y,
        core,
    ).astype(F32)
    base_image = gather_rows(base, ylo, core)

    pre_one = jnp.dot(base, whole_reduce, preferred_element_type=F32)
    norm_one, centred_one, inverse_one = norm_of(
        pre_one, total(sums_of(pre_one, inside), True), bottleneck_gain[0], bottleneck_bias[0], count
    )
    act_one = gather_rows((jax.nn.gelu(norm_one) * inside).astype(BF16), ylo, core)

    def strip_stack(image):
        padded = jnp.pad(image, ((2 * PITCH + 2, 2 * PITCH + 2), (0, 0)))
        return jnp.stack(
            [
                lax.dynamic_slice_in_dim(padded, strip * (2 * PITCH) + 2 * k, 6 * PITCH, 0)
                for k in range(3)
            ]
        )

    pre_two = conv(strip_stack(act_one), whole_dilated, 2 * PITCH, 2 * PITCH)
    norm_two, centred_two, inverse_two = norm_of(
        pre_two, total(sums_of(pre_two, inside), True), bottleneck_gain[1], bottleneck_bias[1], count
    )
    act_two = (jax.nn.gelu(norm_two) * inside).astype(BF16)
    act_two_image = gather_rows(act_two, ylo, core)
    pre_three = jnp.dot(act_two, whole_expand, preferred_element_type=F32)
    norm_three, centred_three, inverse_three = norm_of(
        pre_three, total(sums_of(pre_three, inside), True), expand_gain, expand_bias, count
    )
    joined = norm_three + base.astype(F32)
    trunk = to_heads((jax.nn.gelu(joined) * inside).astype(BF16), y, core)

    pre_head = conv(shifted(trunk, 1, 1, 1), whole_head, PITCH, 8 * PITCH)
    gain_here, bias_here = of_head(head_gain, y), of_head(head_bias, y)
    norm_head, centred_head, inverse_head = norm_of(
        pre_head, total(sums_of(pre_head, inside_whole), False), gain_here, bias_here, count
    )
    task = (jax.nn.gelu(norm_head) * inside_whole).astype(BF16)
    message = conv(shifted(task, 1, 1, 1), whole_message, PITCH, 8 * PITCH)
    gate = jax.nn.sigmoid(jnp.dot(task, whole_gate, preferred_element_type=F32))
    gated = (gate * message).astype(BF16)
    streams = from_heads(
        jnp.concatenate(
            [jnp.where(y == 0, task, gated), jnp.where(y == 1, task, gated)], axis=1
        ),
        y,
        core,
    )
    streams = maps_of(streams * inside, across)
    depth_out, seg_out = jnp.split(streams, 2, axis=3)

    cot_depth, cot_seg = jnp.split(cotangents * inside_whole, 2, axis=1)
    receive = jnp.where(y == 0, cot_seg, jnp.where(y == 1, cot_depth, cot_depth + cot_seg))
    direct = jnp.where(y == 0, cot_depth, jnp.where(y == 1, cot_seg, jnp.zeros_like(cot_seg)))
    d_logit = (receive * message * gate * (1.0 - gate)).astype(BF16)
    d_message = (receive * gate).astype(BF16)
    d_message_stack = shifted(d_message, 1, 1, 1)
    d_task = (
        direct
        + lax.dot_general(
            d_logit, whole_gate, (((1,), (1,)), ((), ())), preferred_element_type=F32
        )
        + conv_t(d_message_stack, whole_message, PITCH, 8 * PITCH)
    )
    d_norm_head = gelu_back(norm_head, d_task * inside_whole)
    head_sums_here = back_sums(d_norm_head, centred_head)
    head_sums = total(head_sums_here, False)
    d_pre_head = norm_back(
        d_norm_head, centred_head, inverse_head, gain_here, inside_whole, head_sums, count
    ).astype(BF16)
    d_head_stack = shifted(d_pre_head, 1, 1, 1)

    head_share = lax.psum_scatter(
        conv_w(trunk.T, d_head_stack, PITCH), POOL, scatter_dimension=0, tiled=True
    )
    task_turned = task.T
    task_share = lax.psum_scatter(
        jnp.concatenate(
            [
                conv_w(task_turned, d_message_stack, PITCH),
                jnp.dot(task_turned, d_logit, preferred_element_type=F32).astype(BF16),
            ],
            axis=1,
        ),
        POOL,
        scatter_dimension=0,
        tiled=True,
    )

    d_trunk = from_heads(conv_t(d_head_stack, whole_head, PITCH, 8 * PITCH), y, core)
    d_joined = gelu_back(joined, d_trunk * inside)
    placed_sums = jnp.where(
        jnp.arange(4)[None, :, None] == y, head_sums_here[:, None], jnp.zeros((1, 1, 1), F32)
    ).reshape(2, -1)
    wide_sums = total(
        jnp.concatenate([back_sums(d_joined, centred_three), placed_sums], axis=1), True
    )
    deep = expand_gain.shape[0]
    expand_sums, all_head_sums = wide_sums[:, :deep], wide_sums[:, deep:]
    d_pre_three = norm_back(
        d_joined, centred_three, inverse_three, expand_gain, inside, expand_sums, count
    ).astype(BF16)
    d_act_two = lax.dot_general(
        d_pre_three, whole_expand, (((1,), (1,)), ((), ())), preferred_element_type=F32
    )
    d_norm_two = gelu_back(norm_two, d_act_two * inside)
    second_sums = total(back_sums(d_norm_two, centred_two), True)
    d_pre_two = gather_rows(
        norm_back(
            d_norm_two, centred_two, inverse_two, bottleneck_gain[1], inside, second_sums, count
        ).astype(BF16),
        ylo,
        core,
    )
    d_act_one = conv_t(strip_stack(d_pre_two), whole_dilated, 2 * PITCH, 2 * PITCH)
    d_norm_one = gelu_back(norm_one, d_act_one * inside)
    first_sums = total(back_sums(d_norm_one, centred_one), True)
    d_pre_one = norm_back(
        d_norm_one, centred_one, inverse_one, bottleneck_gain[0], inside, first_sums, count
    ).astype(BF16)
    d_base = d_joined + lax.dot_general(
        d_pre_one, whole_reduce, (((1,), (1,)), ((), ())), preferred_element_type=F32
    )
    input_grad = maps_of(d_base * inside, across)

    d_three_part = lax.all_to_all(
        jnp.stack(jnp.split(d_pre_three, 4, axis=1)), ROWS, 0, 0
    ).reshape(8 * PITCH, -1)
    d_two_part = lax.dynamic_slice_in_dim(d_pre_two, strip * 128, 128, 1)
    d_one_part = lax.dynamic_slice_in_dim(
        gather_rows(d_pre_one, ylo, core), strip * 128, 128, 1
    )
    grad_expand = jnp.dot(act_two_image.T, d_three_part, preferred_element_type=F32)
    grad_dilated = conv_w(act_one.T, shifted(d_two_part, 2, 2, 2), 2 * PITCH)
    grad_reduce = jnp.dot(base_image.T, d_one_part, preferred_element_type=F32)
    trunk_share = shares_summed(
        jnp.concatenate([grad_expand.astype(BF16), grad_dilated], axis=1)
    ).astype(BF16)
    reduce_share = shares_summed(grad_reduce.astype(BF16)).astype(BF16)
    all_reduce = gather_rows(reduce_share, ylo, core).reshape(4, -1, 128)
    all_trunk = gather_rows(trunk_share, ylo, core).reshape(4, 16, -1)
    sum_reduce = jnp.moveaxis(all_reduce, 0, 1).reshape(-1, 512).astype(F32)
    sum_expand = jnp.moveaxis(all_trunk[:, :, :512], 0, 1).reshape(16, -1).astype(F32)
    sum_dilated = (
        jnp.moveaxis(all_trunk[:, :, 512:].reshape(4, 16, 9, 128), 0, 2)
        .reshape(16, -1)
        .astype(F32)
    )

    def all_heads(share):
        pieces = [share]
        for flip in (1, 2, 3):
            pairs = []
            for i in range(8):
                low, c, high = i >> 2, (i >> 1) & 1, i & 1
                to = (high * 2 + low) ^ flip
                if to >> 1 == c:
                    pairs.append((i, ((to & 1) << 2) | (c << 1) | (to >> 1)))
            pieces.append(lax.ppermute(share, GROUP, pairs))
        low = [jnp.stack(in_order(pieces[0], pieces[1], ylo)), jnp.stack(in_order(pieces[2], pieces[3], ylo))]
        stacked = jnp.concatenate(in_order(low[0], low[1], yhi))
        pairs = [(i, i ^ 2) for i in range(8) if (i >> 1) & 1 == i & 1]
        return jnp.where(local, stacked, lax.ppermute(stacked, GROUP, pairs)).astype(F32)

    sum_head = all_heads(head_share)
    sum_task = all_heads(task_share)
    sum_message, sum_gate = sum_task[:, :, :wide], sum_task[:, :, wide:]

    return (
        depth_out,
        seg_out,
        input_grad,
        sum_reduce,
        sum_dilated,
        sum_expand,
        sum_head,
        sum_message,
        sum_gate,
        jnp.stack([first_sums[0], second_sums[0]]),
        jnp.stack([first_sums[1], second_sums[1]]),
        expand_sums[0],
        expand_sums[1],
        all_head_sums[0].reshape(4, -1),
        all_head_sums[1].reshape(4, -1),
    )


def solution(mesh):
    fine = Mesh(mesh.devices.reshape(2, 2, 4, 4, 2), FINE)
    maps = P(IMG, ROWS, None, None)
    placed = (
        maps,
        P(),
        P(IMG, None),
        P(IMG, None),
        P(IMG, None),
        P(None, IMG, None),
        P(None, IMG, None),
        P(None, IMG, None),
        P(),
        P(),
        P(),
        P(),
        P(),
        P(),
        maps,
        maps,
    )
    return jax.shard_map(
        shards,
        mesh=fine,
        in_specs=placed,
        out_specs=(
            maps,
            maps,
            maps,
            P(IMG, None),
            P(IMG, None),
            P(IMG, None),
            P(None, IMG, None),
            P(None, IMG, None),
            P(None, IMG, None),
            P(),
            P(),
            P(),
            P(),
            P(),
            P(),
        ),
        check_vma=False,
    )
```

time: 3760 us -> 864 us (0.23)
  waiting for transfers between devices: 2500 us -> 236 us
  blocking collectives: 637 us -> 21.5 us
  matrix products: 308 us -> 23.5 us
  Pallas kernels: 0 us -> 113 us
  starting transfers between devices: 65.7 us -> 176 us
  other arithmetic: 36.3 us -> 126 us
  local copies, waits for them, and re-layouts: 191 us -> 138 us
    unnamed x24 -> x5, waiting for transfers between devices: 1880 us -> 0.08 us
    psum x8 -> x0, blocking collectives: 637 us -> none  [together(): running = lax.psum(jnp.concatenate([a.ravel() for a in arrays]), axis)]
    all_gather x4 -> x3, waiting for transfers between devices: 373 us -> 0.04 us  [the longest x1 0.02 us: shards(): whole_trunk = lax.all_gather(trunk_part, POOL, axis=0, tiled=True)]
    dot_general x147 -> x9, matrix products: 308 us -> 23.5 us  [the longest x1 3.79 us: shards(): lax.dot_general(d_pre_three, whole_expand, (((1,), (1,)), ((), ())), pref...]
    ppermute x12 -> x99, waiting for transfers between devices: 19 us -> 217 us  [the longest x87 178 us: swap(): return lax.ppermute(value, axis, [(i, i ^ flip) for i in range(count)])]
    reduce_scatter x3 -> x2, waiting for transfers between devices: 148 us -> 0.04 us  [the longest x1 0.02 us: shards(): lax.psum_scatter(jnp.concatenate([conv_w(task_turned, d_message_stack, PI...]
    unnamed x163 -> x251, local copies, waits for them, and re-layouts: 160 us -> 34.7 us
    pallas_call x0 -> x9, Pallas kernels: none -> 113 us  [the longest x3 50 us: conv_t(): pl.pallas_call(functools.partial(conv_t_body, step, rows), grid=(deep //...]
  transfers between devices with their start and end apart: 28 -> 107, of which waited for: 22 -> 72; matrix products, arithmetic and copies ran while one was open for 11% -> 29% of each run, Pallas kernels for 0% -> 11%
where the time goes in v1:
time: 864 us; the launch traced here: 851 us
  waiting for transfers between devices  236 us (27%)
  starting transfers between devices  176 us (20%)
  local copies, waits for them, and re-layouts  138 us (16%)
  other arithmetic  126 us (15%)
  Pallas kernels  113 us (13%)
  matrix products  23.5 us (3%)
  blocking collectives  21.5 us (2%)
  between operations  16.7 us (2%)
    ppermute x87, waiting for transfers between devices, swap(): return lax.ppermute(value, axis, [(i, i ^ flip) for i in range(count)])  178 us
    ppermute x87, starting transfers between devices, swap(): return lax.ppermute(value, axis, [(i, i ^ flip) for i in range(count)])  137 us
    pallas_call x3, Pallas kernels, conv_t(): pl.pallas_call(functools.partial(conv_t_body, step, rows), grid=(deep //...  50 us
    unnamed x251, local copies, waits for them, and re-layouts  34.7 us
    pallas_call x3, Pallas kernels, conv(): pl.pallas_call(functools.partial(conv_body, step, rows), grid=(9,), in_sp...  34.6 us
    pallas_call x3, Pallas kernels, conv_w(): pl.pallas_call(functools.partial(conv_w_body, step, rows), grid=(9,), in_...  28.3 us
    ppermute x4, waiting for transfers between devices, brought(): return jnp.where(local, mine, lax.ppermute(sent, GROUP, group))  22.4 us
    all_to_all x1, blocking collectives, shards(): lax.all_to_all(jnp.broadcast_to(reduce_part[None], (16,) + reduce_part.sh...  21.5 us
  transfers between devices with their start and end apart: 107, of which 72 were waited for; matrix products, arithmetic and copies ran while one was open for 29% of the time, Pallas kernels for 11%

profile of v1, /device:TPU:1, one launch (start us, length us, event | category | flops | bytes accessed | tf_op | source)
XLA Modules:
  0.0 850.7 jit_solution(17258783828135952958)
XLA Ops:
  10.3 6.8 collective-permute-done.11
  20.3 10.5 %collective-permute-done.31 = bf16[64,4608]{1,0:T(8,128)(2,1)S(1)} collective-permute-done((bf16[64,4608]{1,0:T(8,128)(2,1)S(1)}, bf16[64,4608]{1,0:T(8,128)(2,1)S(1)}, u32[]{:S(2)}, u32[]{:S(2)}) %collective-permute-start.31) | collective-permute-done | bytes 589856 | tf_op jit(solution)/shard_map/ppermute | solution.py:306
  39.6 21.5 %all_to_all.20 = bf16[16,64,512]{2,1,0:T(8,128)(2,1)S(1)} all-to-all(bf16[16,64,512]{2,1,0:T(8,128)(2,1)S(1)} %broadcast_in_dim.25), channel_id=1, replica_groups=mesh['ylo'=2,'core'=2,'x'=4,'z'=4,'yhi'=2] {'x','z'}, dimensions={0} | all-to-all | bytes 2097152 | tf_op jit(solution)/shard_map/all_to_all | solution.py:313
  61.1 13.2 %collective-permute-start.1 = (bf16[16,64,512]{2,1,0:T(8,128)(2,1)S(1)}, bf16[16,64,512]{2,1,0:T(8,128)(2,1)S(1)}, u32[]{:S(2)}, u32[]{:S(2)}) collective-permute-start(bf16[16,64,512]{2,1,0:T(8,128)(2,1)S(1)} %all_to_all.20), channel_id=1, source_target_pairs={{0,32},{32,0},{1,33},{33,1},{2,34},{34,2},{3,35},{35,3},{4,36},{36... | collective-permute-start | bytes 3145736 | tf_op jit(solution)/shard_map/ppermute | solution.py:25
  101.9 5.9 collective-permute-start.9
  109.2 9.0 %collective-permute-done.10 = bf16[320,512]{1,0:T(8,128)(2,1)S(1)} collective-permute-done((bf16[320,512]{1,0:T(8,128)(2,1)S(1)}, bf16[320,512]{1,0:T(8,128)(2,1)S(1)}, u32[]{:S(2)}, u32[]{:S(2)}) %collective-permute-start.10) | collective-permute-done | bytes 327712 | tf_op jit(solution)/shard_map/ppermute | solution.py:25
  125.4 6.8 shard_map.271
  167.9 5.5 collective-permute-start.19
  204.6 8.5 collective-permute-done.26
  219.9 7.8 collective-permute-done.29
  235.9 9.4 %collective-permute-start.30 = (bf16[320,2048]{1,0:T(8,128)(2,1)}, bf16[320,2048]{1,0:T(8,128)(2,1)}, u32[]{:S(2)}, u32[]{:S(2)}) collective-permute-start(bf16[320,2048]{1,0:T(8,128)(2,1)} %copy.151), channel_id=1, source_target_pairs={{0,32},{32,0},{1,33},{33,1},{2,34},{34,2},{3,35},{35,3},{4,36},{36... | collective-permute-start | bytes 3932168 | tf_op jit(solution)/shard_map/ppermute | solution.py:25
  250.8 7.5 collective-permute-done.44
  294.0 5.3 pad_maximum_fusion
  299.4 14.7 %copy.156.x_ref = bf16[3,800,2048]{2,1,0:T(8,128)(2,1)} copy(bf16[3,800,2048]{1,2,0:T(8,128)(2,1)} %pad_maximum_fusion) | data formatting | bytes 19660800 | tf_op jit(solution)/shard_map/stack | solution.py:109
  314.1 19.4 %shard_map.272 = f32[640,512]{1,0:T(8,128)S(1)} custom-call(bf16[3,800,2048]{2,1,0:T(8,128)(2,1)} %copy.156.x_ref, bf16[2048,4608]{1,0:T(8,128)(2,1)} %all-gather.6.cloned.1.call-done.w_ref), custom_call_target="tpu_custom_call" | custom-call | flops 12079595520 | bytes 30015488 | tf_op jit(solution)/shard_map/pallas_call | solution.py:133
  356.2 8.4 shard_map.273
  374.8 7.1 shard_map.279
  383.3 5.4 pad_maximum_fusion.1
  390.4 8.7 %shard_map.274 = f32[640,512]{1,0:T(8,128)S(1)} custom-call(bf16[3,800,512]{2,1,0:T(8,128)(2,1)S(1)} %copy-done.3, bf16[512,4608]{1,0:T(8,128)(2,1)} %slice.372.w_ref), custom_call_target="tpu_custom_call" | custom-call | flops 3019898880 | bytes 8486912 | tf_op jit(solution)/shard_map/pallas_call | solution.py:173
  421.6 17.9 %shard_map.278 = bf16[2048,4608]{1,0:T(8,128)(2,1)} custom-call(bf16[2048,640]{1,0:T(8,128)(2,1)S(1)} %fusion.127.x_ref, bf16[3,800,512]{2,1,0:T(8,128)(2,1)S(1)} %pad_maximum_fusion.5.g_ref), custom_call_target="tpu_custom_call" | custom-call | flops 12079595520 | bytes 23953408 | tf_op jit(solution)/shard_map/pallas_call | solution.py:202
  442.7 34.2 %shard_map.275 = f32[640,2048]{1,0:T(8,128)} custom-call(bf16[3,800,512]{2,1,0:T(8,128)(2,1)S(1)} %copy-done.5, bf16[2048,4608]{1,0:T(8,128)(2,1)} %all-gather.6.cloned.1.call-done.w_ref), custom_call_target="tpu_custom_call" | custom-call | flops 12079595520 | bytes 26574848 | tf_op jit(solution)/shard_map/pallas_call | solution.py:173
  520.9 10.3 %collective-permute-done.56 = bf16[80,2048]{0,1:T(8,128)(2,1)S(1)} collective-permute-done((bf16[80,2048]{0,1:T(8,128)(2,1)S(1)}, bf16[80,2048]{0,1:T(8,128)(2,1)S(1)}, u32[]{:S(2)}, u32[]{:S(2)}) %collective-permute-start.56) | collective-permute-done | bytes 327712 | tf_op jit(solution)/shard_map/ppermute | solution.py:25
  542.3 9.3 %collective-permute-done.57 = bf16[160,2048]{1,0:T(8,128)(2,1)} collective-permute-done((bf16[160,2048]{1,0:T(8,128)(2,1)}, bf16[160,2048]{1,0:T(8,128)(2,1)}, u32[]{:S(2)}, u32[]{:S(2)}) %collective-permute-start.57) | collective-permute-done | bytes 655392 | tf_op jit(solution)/shard_map/ppermute | solution.py:25
  559.3 6.7 multiply_reduce_fusion
  590.3 5.9 collective-permute-start.87
  641.0 16.6 %collective-permute-done.88 = bf16[320,512]{1,0:T(8,128)(2,1)S(1)} collective-permute-done((bf16[320,512]{1,0:T(8,128)(2,1)S(1)}, bf16[320,512]{1,0:T(8,128)(2,1)S(1)}, u32[]{:S(2)}, u32[]{:S(2)}) %collective-permute-start.88) | collective-permute-done | bytes 327712 | tf_op jit(solution)/shard_map/ppermute | solution.py:25
  669.5 7.1 shard_map.276
  702.2 8.4 all-to-all-start.2
  722.5 11.6 %collective-permute-done.84 = bf16[320,512]{1,0:T(8,128)(2,1)} collective-permute-done((bf16[320,512]{1,0:T(8,128)(2,1)}, bf16[320,512]{1,0:T(8,128)(2,1)}, u32[]{:S(2)}, u32[]{:S(2)}) %collective-permute-start.84) | collective-permute-done | bytes 327712 | tf_op jit(solution)/shard_map/ppermute | solution.py:25
  746.5 7.2 all-to-all-done.1
  775.0 7.3 all-to-all-done.3
  809.9 9.9 %collective-permute-done.92 = bf16[64,4608]{1,0:T(8,128)(2,1)S(1)} collective-permute-done((bf16[64,4608]{1,0:T(8,128)(2,1)S(1)}, bf16[64,4608]{1,0:T(8,128)(2,1)S(1)}, u32[]{:S(2)}, u32[]{:S(2)}) %collective-permute-start.92) | collective-permute-done | bytes 589856 | tf_op jit(solution)/shard_map/ppermute | solution.py:492
  (706 shorter events, 500.3 us)
Async XLA Ops:
  7.2 113.3 %all-gather.4.cloned.1.call-start = ((), (), s32[]{:S(2)}) async-start(), calls=%async_computation.6 | async-start | bytes 7028736 | tf_op jit(solution)/shard_map/all_gather | solution.py:320
  17.8 296.3 %all-gather.6.cloned.1.call-start = ((), (), s32[]{:S(2)}) async-start(), calls=%async_computation.7 | async-start | bytes 19464192 | tf_op jit(solution)/shard_map/all_gather | solution.py:326
  19.0 11.8 %collective-permute-start.31 = (bf16[64,4608]{1,0:T(8,128)(2,1)S(1)}, bf16[64,4608]{1,0:T(8,128)(2,1)S(1)}, u32[]{:S(2)}, u32[]{:S(2)}) collective-permute-start(bf16[64,4608]{1,0:T(8,128)(2,1)S(1)} %dynamic-slice_bitcast_fusion), channel_id=1, source_target_pairs={{0,65},{33,96},{64,1},{97,32},{2,67},{35,98},{66,3},{99,34},{4,69}... | collective-permute-start | bytes 1769480 | tf_op jit(solution)/shard_map/ppermute | solution.py:306
  32.9 315.1 %all-gather.8.cloned.1.call-start = ((), (), s32[]{:S(2)}) async-start(), calls=%async_computation.8 | async-start | bytes 5406720 | tf_op jit(solution)/shard_map/all_gather | solution.py:327
  61.1 17.9 %collective-permute-start.1 = (bf16[16,64,512]{2,1,0:T(8,128)(2,1)S(1)}, bf16[16,64,512]{2,1,0:T(8,128)(2,1)S(1)}, u32[]{:S(2)}, u32[]{:S(2)}) collective-permute-start(bf16[16,64,512]{2,1,0:T(8,128)(2,1)S(1)} %all_to_all.20), channel_id=1, source_target_pairs={{0,32},{32,0},{1,33},{33,1},{2,34},{34,2},{3,35},{35,3},{4,36},{36... | collective-permute-start | bytes 3145736 | tf_op jit(solution)/shard_map/ppermute | solution.py:25
  175.3 18.7 %collective-permute-start.37 = (bf16[16,5120]{1,0:T(8,128)(2,1)S(1)}, bf16[16,5120]{1,0:T(8,128)(2,1)S(1)}, u32[]{:S(2)}, u32[]{:S(2)}) collective-permute-start(bf16[16,5120]{1,0:T(8,128)(2,1)S(1)} %dynamic-slice_bitcast_fusion.1), channel_id=1, source_target_pairs={{0,65},{33,96},{64,1},{97,32},{2,67},{35,98},{66,3},{99,34},{4,69}... | collective-permute-start | bytes 491528 | tf_op jit(solution)/shard_map/ppermute | solution.py:306
  195.7 597.6 %reduce-scatter.5.cloned.1.call-start = ((), (), s32[]{:S(2)}) async-start(), calls=%async_computation.10 | async-start | bytes 5406720 | tf_op jit(solution)/shard_map/reduce_scatter | solution.py:410
  203.3 12.5 %collective-permute-start.27 = (bf16[160,2048]{1,0:T(8,128)(2,1)}, bf16[160,2048]{1,0:T(8,128)(2,1)}, u32[]{:S(2)}, u32[]{:S(2)}) collective-permute-start(bf16[160,2048]{1,0:T(8,128)(2,1)} %copy.141), channel_id=1, source_target_pairs={{0,65},{1,64},{64,1},{65,0},{2,67},{3,66},{66,3},{67,2},{4,69},{5,... | collective-permute-start | bytes 1966088 | tf_op jit(solution)/shard_map/ppermute | solution.py:25
  214.6 13.0 %collective-permute-start.29 = (bf16[80,2048]{0,1:T(8,128)(2,1)}, bf16[80,2048]{0,1:T(8,128)(2,1)}, u32[]{:S(2)}, u32[]{:S(2)}) collective-permute-start(bf16[80,2048]{0,1:T(8,128)(2,1)} %slice.366), channel_id=1, source_target_pairs={{0,65},{1,64},{64,1},{65,0},{2,67},{3,66},{66,3},{67,2},{4,69},{5,... | collective-permute-start | bytes 983048 | tf_op jit(solution)/shard_map/ppermute | solution.py:25
  235.9 38.5 %collective-permute-start.30 = (bf16[320,2048]{1,0:T(8,128)(2,1)}, bf16[320,2048]{1,0:T(8,128)(2,1)}, u32[]{:S(2)}, u32[]{:S(2)}) collective-permute-start(bf16[320,2048]{1,0:T(8,128)(2,1)} %copy.151), channel_id=1, source_target_pairs={{0,32},{32,0},{1,33},{33,1},{2,34},{34,2},{3,35},{35,3},{4,36},{36... | collective-permute-start | bytes 3932168 | tf_op jit(solution)/shard_map/ppermute | solution.py:25
  272.2 68.6 %collective-permute-start.47 = (bf16[320,1024]{1,0:T(8,128)(2,1)}, bf16[320,1024]{1,0:T(8,128)(2,1)}, u32[]{:S(2)}, u32[]{:S(2)}) collective-permute-start(bf16[320,1024]{1,0:T(8,128)(2,1)} %pad_maximum_fusion.24), channel_id=1, source_target_pairs={{0,32},{32,0},{1,33},{33,1},{2,34},{34,2},{3,35},{35,3},{4,36},{36... | collective-permute-start | bytes 1966088 | tf_op jit(solution)/shard_map/ppermute | solution.py:25
  388.7 412.3 %reduce-scatter.3.cloned.1.call-start = ((), (), s32[]{:S(2)}) async-start(), calls=%async_computation.9 | async-start | bytes 19464192 | tf_op jit(solution)/shard_map/reduce_scatter | solution.py:406
  518.0 13.2 %collective-permute-start.56 = (bf16[80,2048]{0,1:T(8,128)(2,1)S(1)}, bf16[80,2048]{0,1:T(8,128)(2,1)S(1)}, u32[]{:S(2)}, u32[]{:S(2)}) collective-permute-start(bf16[80,2048]{0,1:T(8,128)(2,1)S(1)} %get-tuple-element.116), channel_id=1, source_target_pairs={{0,64},{1,65},{64,0},{65,1},{2,66},{3,67},{66,2},{67,3},{4,68},{5,... | collective-permute-start | bytes 983048 | tf_op jit(solution)/shard_map/ppermute | solution.py:25
  518.3 19.1 %collective-permute-start.54 = (bf16[80,2048]{0,1:T(8,128)(2,1)}, bf16[80,2048]{0,1:T(8,128)(2,1)}, u32[]{:S(2)}, u32[]{:S(2)}) collective-permute-start(bf16[80,2048]{0,1:T(8,128)(2,1)} %get-tuple-element.115), channel_id=1, source_target_pairs={{0,65},{1,64},{64,1},{65,0},{2,67},{3,66},{66,3},{67,2},{4,69},{5,... | collective-permute-start | bytes 983048 | tf_op jit(solution)/shard_map/ppermute | solution.py:25
  535.0 16.6 %collective-permute-start.57 = (bf16[160,2048]{1,0:T(8,128)(2,1)}, bf16[160,2048]{1,0:T(8,128)(2,1)}, u32[]{:S(2)}, u32[]{:S(2)}) collective-permute-start(bf16[160,2048]{1,0:T(8,128)(2,1)} %copy.166), channel_id=1, source_target_pairs={{0,65},{1,64},{64,1},{65,0},{2,67},{3,66},{66,3},{67,2},{4,69},{5,... | collective-permute-start | bytes 1966088 | tf_op jit(solution)/shard_map/ppermute | solution.py:25
  541.9 15.1 %collective-permute-start.55 = (bf16[160,2048]{1,0:T(8,128)(2,1)S(1)}, bf16[160,2048]{1,0:T(8,128)(2,1)}, u32[]{:S(2)}, u32[]{:S(2)}) collective-permute-start(bf16[160,2048]{1,0:T(8,128)(2,1)S(1)} %copy.164), channel_id=1, source_target_pairs={{0,64},{1,65},{64,0},{65,1},{2,66},{3,67},{66,2},{67,3},{4,68},{5,... | collective-permute-start | bytes 1966088 | tf_op jit(solution)/shard_map/ppermute | solution.py:25
  590.3 19.2 %collective-permute-start.87 = (bf16[160,512]{1,0:T(8,128)(2,1)S(1)}, bf16[160,512]{1,0:T(8,128)(2,1)}, u32[]{:S(2)}, u32[]{:S(2)}) collective-permute-start(bf16[160,512]{1,0:T(8,128)(2,1)S(1)} %copy-done.70), channel_id=1, source_target_pairs={{0,32},{32,0},{1,33},{33,1},{2,34},{34,2},{3,35},{35,3},{4,36},{36... | collective-permute-start | bytes 491528 | tf_op jit(solution)/shard_map/ppermute | solution.py:25
  597.4 13.9 %collective-permute-start.81 = (bf16[160,2048]{1,0:T(8,128)(2,1)}, bf16[160,2048]{1,0:T(8,128)(2,1)}, u32[]{:S(2)}, u32[]{:S(2)}) collective-permute-start(bf16[160,2048]{1,0:T(8,128)(2,1)} %copy.170), channel_id=1, source_target_pairs={{0,32},{32,0},{1,33},{33,1},{2,34},{34,2},{3,35},{35,3},{4,36},{36... | collective-permute-start | bytes 1966088 | tf_op jit(solution)/shard_map/ppermute | solution.py:25
  621.5 37.0 %collective-permute-start.82 = (bf16[320,2048]{1,0:T(8,128)(2,1)}, bf16[320,2048]{1,0:T(8,128)(2,1)}, u32[]{:S(2)}, u32[]{:S(2)}) collective-permute-start(bf16[320,2048]{1,0:T(8,128)(2,1)} %copy.173), channel_id=1, source_target_pairs={{0,64},{1,65},{64,0},{65,1},{2,66},{3,67},{66,2},{67,3},{4,68},{5,... | collective-permute-start | bytes 3932168 | tf_op jit(solution)/shard_map/ppermute | solution.py:25
  622.3 35.2 %collective-permute-start.88 = (bf16[320,512]{1,0:T(8,128)(2,1)S(1)}, bf16[320,512]{1,0:T(8,128)(2,1)S(1)}, u32[]{:S(2)}, u32[]{:S(2)}) collective-permute-start(bf16[320,512]{1,0:T(8,128)(2,1)S(1)} %pad_maximum_fusion.33), channel_id=1, source_target_pairs={{0,64},{1,65},{64,0},{65,1},{2,66},{3,67},{66,2},{67,3},{4,68},{5,... | collective-permute-start | bytes 983048 | tf_op jit(solution)/shard_map/ppermute | solution.py:25
  633.2 29.0 %collective-permute-start.38 = (bf16[320,1024]{1,0:T(8,128)(2,1)}, bf16[320,1024]{1,0:T(8,128)(2,1)}, u32[]{:S(2)}, u32[]{:S(2)}) collective-permute-start(bf16[320,1024]{1,0:T(8,128)(2,1)} %pad_maximum_fusion.23), channel_id=1, source_target_pairs={{0,32},{32,0},{1,33},{33,1},{2,34},{34,2},{3,35},{35,3},{4,36},{36... | collective-permute-start | bytes 1966088 | tf_op jit(solution)/shard_map/ppermute | solution.py:25
  638.4 22.0 %collective-permute-start.72 = (bf16[160,512]{1,0:T(8,128)(2,1)S(1)}, bf16[160,512]{1,0:T(8,128)(2,1)S(1)}, u32[]{:S(2)}, u32[]{:S(2)}) collective-permute-start(bf16[160,512]{1,0:T(8,128)(2,1)S(1)} %multiply_convert_fusion.8), channel_id=1, source_target_pairs={{0,32},{32,0},{1,33},{33,1},{2,34},{34,2},{3,35},{35,3},{4,36},{36... | collective-permute-start | bytes 491528 | tf_op jit(solution)/shard_map/ppermute | solution.py:25
  688.4 23.1 %collective-permute-start.39 = (bf16[80,1024]{1,0:T(8,128)(2,1)S(1)}, bf16[80,1024]{1,0:T(8,128)(2,1)}, u32[]{:S(2)}, u32[]{:S(2)}) collective-permute-start(bf16[80,1024]{1,0:T(8,128)(2,1)S(1)} %get-tuple-element.160), channel_id=1, source_target_pairs={{0,65},{1,64},{64,1},{65,0},{2,67},{3,66},{66,3},{67,2},{4,69},{5,... | collective-permute-start | bytes 491528 | tf_op jit(solution)/shard_map/ppermute | solution.py:25
  694.2 65.0 %collective-permute-start.42 = (bf16[160,1024]{1,0:T(8,128)(2,1)}, bf16[160,1024]{1,0:T(8,128)(2,1)}, u32[]{:S(2)}, u32[]{:S(2)}) collective-permute-start(bf16[160,1024]{1,0:T(8,128)(2,1)} %pad_maximum_fusion.29), channel_id=1, source_target_pairs={{0,65},{1,64},{64,1},{65,0},{2,67},{3,66},{66,3},{67,2},{4,69},{5,... | collective-permute-start | bytes 983048 | tf_op jit(solution)/shard_map/ppermute | solution.py:25
  702.2 17.7 %all-to-all-start.2 = ((bf16[4,160,512]{2,1,0:T(8,128)(2,1)}), bf16[4,160,512]{2,1,0:T(8,128)(2,1)S(1)}, u32[]{:S(2)}, u32[]{:S(2)}) async-start(bf16[4,160,512]{2,1,0:T(8,128)(2,1)} %copy.177), calls=%async_computation.2 | async-start | bytes 1310720 | tf_op jit(solution)/shard_map/all_to_all | solution.py:459
  713.3 45.9 %collective-permute-start.40 = (bf16[160,1024]{1,0:T(8,128)(2,1)}, bf16[160,1024]{1,0:T(8,128)(2,1)}, u32[]{:S(2)}, u32[]{:S(2)}) collective-permute-start(bf16[160,1024]{1,0:T(8,128)(2,1)} %pad_maximum_fusion.28), channel_id=1, source_target_pairs={{0,64},{1,65},{64,0},{65,1},{2,66},{3,67},{66,2},{67,3},{4,68},{5,... | collective-permute-start | bytes 983048 | tf_op jit(solution)/shard_map/ppermute | solution.py:25
  715.8 18.3 %collective-permute-start.84 = (bf16[320,512]{1,0:T(8,128)(2,1)}, bf16[320,512]{1,0:T(8,128)(2,1)}, u32[]{:S(2)}, u32[]{:S(2)}) collective-permute-start(bf16[320,512]{1,0:T(8,128)(2,1)} %pad_maximum_fusion.32), channel_id=1, source_target_pairs={{0,64},{1,65},{64,0},{65,1},{2,66},{3,67},{66,2},{67,3},{4,68},{5,... | collective-permute-start | bytes 983048 | tf_op jit(solution)/shard_map/ppermute | solution.py:25
  737.0 16.6 %all-to-all-start.1 = ((bf16[32,64,128]{2,1,0:T(8,128)(2,1)}), bf16[32,64,128]{2,1,0:T(8,128)(2,1)S(1)}, u32[]{:S(2)}, u32[]{:S(2)}) async-start(bf16[32,64,128]{2,1,0:T(8,128)(2,1)} %bitcast.189), calls=%async_computation.1 | async-start | bytes 1048576 | tf_op jit(solution)/shard_map/all_to_all | solution.py:259
  754.4 27.9 %all-to-all-start.3 = ((bf16[32,16,1664]{2,1,0:T(8,128)(2,1)}), bf16[32,16,1664]{2,1,0:T(8,128)(2,1)}, u32[]{:S(2)}, u32[]{:S(2)}) async-start(bf16[32,16,1664]{2,1,0:T(8,128)(2,1)} %bitcast.89), calls=%async_computation.3 | async-start | bytes 3407872 | tf_op jit(solution)/shard_map/all_to_all | solution.py:259
  803.6 16.2 %collective-permute-start.92 = (bf16[64,4608]{1,0:T(8,128)(2,1)S(1)}, bf16[64,4608]{1,0:T(8,128)(2,1)S(1)}, u32[]{:S(2)}, u32[]{:S(2)}) collective-permute-start(bf16[64,4608]{1,0:T(8,128)(2,1)S(1)} %copy-done.74), channel_id=1, source_target_pairs={{1,0},{32,33},{65,64},{96,97},{3,2},{34,35},{67,66},{98,99},{5,4},... | collective-permute-start | bytes 1769480 | tf_op jit(solution)/shard_map/ppermute | solution.py:492
  808.3 14.1 %collective-permute-start.93 = (bf16[64,4608]{1,0:T(8,128)(2,1)S(1)}, bf16[64,4608]{1,0:T(8,128)(2,1)S(1)}, u32[]{:S(2)}, u32[]{:S(2)}) collective-permute-start(bf16[64,4608]{1,0:T(8,128)(2,1)S(1)} %copy-done.74), channel_id=1, source_target_pairs={{1,64},{32,97},{65,0},{96,33},{3,66},{34,99},{67,2},{98,35},{5,68}... | collective-permute-start | bytes 1769480 | tf_op jit(solution)/shard_map/ppermute | solution.py:492
  824.3 14.8 %collective-permute-start.94 = (bf16[4,64,4608]{2,1,0:T(8,128)(2,1)}, bf16[4,64,4608]{2,1,0:T(8,128)(2,1)}, u32[]{:S(2)}, u32[]{:S(2)}) collective-permute-start(bf16[4,64,4608]{2,1,0:T(8,128)(2,1)} %pad_maximum_fusion.6), channel_id=1, source_target_pairs={{0,32},{33,1},{64,96},{97,65},{2,34},{35,3},{66,98},{99,67},{4,36}... | collective-permute-start | bytes 7077896 | tf_op jit(solution)/shard_map/ppermute | solution.py:496
  (193 other events, 2189.4 us)
Sparse Core Ops, SparseCore 0:
  17.9 61.7 all-gather.3
  81.9 74.6 all-gather.5
  195.8 52.4 all-gather.7
  388.8 84.4 reduce-scatter.4
  477.6 123.8 reduce-scatter.2

commit v2 on v1

v2 whole, which is shorter than its diff:
```python
import functools

import jax
import jax.numpy as jnp
from jax import lax
from jax.experimental import pallas as pl
from jax.experimental.pallas import tpu as pltpu
from jax.sharding import Mesh, PartitionSpec as P

EPS = 1e-05
PITCH = 80
ROOT = 0.7978845608028654
CUBE = 0.044715
F32 = jnp.float32
BF16 = jnp.bfloat16

FINE = ("ylo", "core", "x", "z", "yhi")
ROWS = ("ylo", "core")
IMG = ("x", "z", "yhi")
RING = ("ylo", "yhi")
GROUP = ("ylo", "core", "yhi")
POOL = ("x", "z", "core")


def swap(value, axis, flip):
    count = lax.axis_size(axis)
    return lax.ppermute(value, axis, [(i, i ^ flip) for i in range(count)])


def over_core(value):
    return swap(value, "core", 1)


def over_y(value, flip):
    return swap(value, RING, {1: 2, 2: 1, 3: 3}[flip])


def fold(value, *partners):
    for axis, flip in partners:
        value = value + (over_y(value, flip) if axis == "y" else swap(value, axis, flip))
    return value


CORE, LINE, PLANE, RIDGE = ("core", 1), (("x", 1), ("x", 3)), (("z", 1), ("z", 3)), (("y", 1), ("y", 3))


def hold(*arrays):
    return lax.optimization_barrier(arrays)


def in_order(mine, other, bit):
    first = bit == 0
    return jnp.where(first, mine, other), jnp.where(first, other, mine)


def beside_rows(value):
    return (
        value,
        over_y(value, 1),
        over_core(value),
        lax.ppermute(value, GROUP, [(i, i ^ 6) for i in range(8)]),
    )


def from_rows(parts):
    own, low, other, both = parts
    return (
        own,
        over_y(low, 1),
        over_core(other),
        lax.ppermute(both, GROUP, [(i, i ^ 6) for i in range(8)]),
    )


def beside_y(value):
    return over_y(value, 1), over_y(value, 3)


def across_y(near, far):
    half = near.shape[0] // 2
    return over_y(far[:half], 1), over_y(near[half:], 3)


def sent_home(kept_here, got, same):
    return jnp.where(same, kept_here, got), jnp.where(same, got, kept_here)


def half_way(other):
    half = other.shape[1] // 2
    return over_y(other[0, :half], 1), over_y(other[0, half:], 3)


def last_way(own, other, from_near, from_far):
    half = own.shape[1] // 2
    near = jnp.concatenate(
        [own[1, :half], (own[1, half:].astype(F32) + from_far.astype(F32)).astype(BF16)]
    )
    far = jnp.concatenate(
        [(other[1, :half].astype(F32) + from_near.astype(F32)).astype(BF16), other[1, half:]]
    )
    return own[0], over_y(near, 1), over_y(far, 3)


def gelu_parts(value):
    squared = value * value
    bend = jnp.tanh(ROOT * value * (1.0 + CUBE * squared))
    return 0.5 * (1.0 + bend), bend, squared


def gelu(value):
    return value * gelu_parts(value)[0]


def gelu_slope(value):
    level, bend, squared = gelu_parts(value)
    return level + 0.5 * value * (1.0 - bend * bend) * ROOT * (1.0 + 3.0 * CUBE * squared)


def moments(sums_ref, count):
    mean = sums_ref[0:1, :] / count
    return mean, lax.rsqrt(sums_ref[1:2, :] / count - mean * mean + EPS)


def store_sums(sums_ref, first, second):
    sums_ref[0:1, :] = jnp.sum(first, axis=0, keepdims=True)
    sums_ref[1:2, :] = jnp.sum(second, axis=0, keepdims=True)


def add_sums(sums_ref, first, second, columns=slice(None)):
    sums_ref[0:1, columns] += jnp.sum(first, axis=0, keepdims=True)
    sums_ref[1:2, columns] += jnp.sum(second, axis=0, keepdims=True)


def store_moved(stack_ref, start, value, dilation, columns=slice(None)):
    rows = pl.ds(start, PITCH)
    stack_ref[0, rows, columns] = pltpu.roll(value, dilation, 0).astype(BF16)
    stack_ref[1, rows, columns] = value.astype(BF16)
    stack_ref[2, rows, columns] = pltpu.roll(value, PITCH - dilation, 0).astype(BF16)


def clear_ends(stack_ref, rows):
    length = stack_ref.shape[1]
    empty = jnp.zeros((3, rows, stack_ref.shape[2]), BF16)
    stack_ref[:, 0:rows, :] = empty
    stack_ref[:, length - rows : length, :] = empty


def move_map(stack_ref, map_ref, dilation):
    clear_ends(stack_ref, dilation * PITCH)

    @pl.loop(0, 8)
    def _(r):
        at = pl.multiple_of(r * PITCH, 16)
        store_moved(
            stack_ref,
            pl.multiple_of(at + dilation * PITCH, 16),
            map_ref[pl.ds(at, PITCH), :].astype(F32),
            dilation,
        )


def times_turned(first, second):
    return lax.dot_general(first, second, (((1,), (1,)), ((), ())), preferred_element_type=F32)


def whole(shape):
    return pl.BlockSpec(shape, lambda *at: (0,) * len(shape), pipeline_mode=pl.Buffered(1))


def kept(shape):
    return pl.BlockSpec(shape, lambda *at: (0,) * len(shape))


SCALARS = pl.BlockSpec(memory_space=pltpu.SMEM)


def call(kernel, grid, in_specs, out_specs, outs, scratch, flops, *operands):
    moved = sum(a.size * a.dtype.itemsize for a in operands)
    return pl.pallas_call(
        kernel,
        grid=grid,
        in_specs=in_specs,
        out_specs=out_specs,
        out_shape=[jax.ShapeDtypeStruct(*o) for o in outs],
        scratch_shapes=scratch,
        compiler_params=pltpu.CompilerParams(vmem_limit_bytes=56 << 20),
        cost_estimate=pl.CostEstimate(flops=flops, bytes_accessed=moved, transcendentals=0),
    )(*operands)


def clear_image(image_ref):
    strip = 2 * PITCH
    empty = jnp.zeros((strip, image_ref.shape[1]), BF16)
    image_ref[0:strip, :] = empty
    image_ref[5 * strip : 6 * strip, :] = empty


def window_moved(stack_ref, image_ref, start):
    @pl.loop(0, 6)
    def _(r):
        at = pl.multiple_of(r * PITCH, 16)
        value = image_ref[pl.ds(pl.multiple_of(start + at, 16), PITCH), :]
        store_moved(stack_ref, at, value.astype(F32), 2)


def dilated_kernel(
    count_ref, at_ref, p0, p1, p2, p3, sums_ref, gain_ref, bias_ref, inside_ref, mine_ref, w_ref,
    out_ref, out_sums, image_out, image_ref, stack_ref, total_ref,
):
    tap = pl.program_id(0)
    strip = 2 * PITCH

    @pl.when(tap == 0)
    def _():
        clear_image(image_ref)
        mean, inverse = moments(sums_ref, count_ref[0])
        for k, piece in enumerate((p0, p1, p2, p3)):
            start = pl.multiple_of(at_ref[k], 16)
            normed = gain_ref[...] * ((piece[...].astype(F32) - mean) * inverse) + bias_ref[...]
            act = gelu(normed) * inside_ref[pl.ds(start, strip), :]
            image_ref[pl.ds(pl.multiple_of(start + strip, 16), strip), :] = act.astype(BF16)
        window_moved(stack_ref, image_ref, at_ref[0])
        image_out[...] = image_ref[strip : 5 * strip, :]
        total_ref[...] = jnp.zeros_like(total_ref)

    start = pl.multiple_of((tap // 3) * strip, 16)
    total_ref[...] += jnp.dot(
        stack_ref[tap % 3, pl.ds(start, strip), :], w_ref[...], preferred_element_type=F32
    )

    @pl.when(tap == 8)
    def _():
        out = total_ref[...].astype(BF16)
        out_ref[...] = out
        out = out.astype(F32)
        value = out * mine_ref[...]
        store_sums(out_sums, value, value * out)


def dilated_forward(count, at, pieces, sums, gain, bias, inside, mine, weights, first_block):
    strip, deep = pieces[0].shape
    operands = (*pieces, sums, gain, bias, inside, mine)
    return call(
        dilated_kernel,
        (9,),
        [SCALARS, SCALARS]
        + [whole(a.shape) for a in operands]
        + [pl.BlockSpec((deep, 512), lambda t: (0, first_block + t))],
        [kept((strip, 512)), kept((2, 512)), kept((4 * strip, deep))],
        [((strip, 512), BF16), ((2, 512), F32), ((4 * strip, deep), BF16)],
        [
            pltpu.VMEM((6 * strip, deep), BF16),
            pltpu.VMEM((3, 3 * strip, deep), BF16),
            pltpu.VMEM((strip, 512), F32),
        ],
        18 * strip * deep * 512,
        count,
        at,
        *operands,
        weights,
    )


def expand_kernel(count_ref, value_ref, sums_ref, gain_ref, bias_ref, inside_ref, w_ref, act_ref, out_ref, out_sums):
    mean, inverse = moments(sums_ref, count_ref[0])
    normed = gain_ref[...] * ((value_ref[...].astype(F32) - mean) * inverse) + bias_ref[...]
    act = (gelu(normed) * inside_ref[...]).astype(BF16)
    act_ref[...] = act
    for c in range(4):
        columns = slice(c * 512, (c + 1) * 512)
        part = jnp.dot(act, w_ref[:, columns], preferred_element_type=F32).astype(BF16)
        out_ref[:, columns] = part
        part = part.astype(F32)
        out_sums[0:1, columns] = jnp.sum(part, axis=0, keepdims=True)
        out_sums[1:2, columns] = jnp.sum(part * part, axis=0, keepdims=True)


def expand_forward(count, value, sums, gain, bias, inside, weights):
    rows, deep = value.shape
    return call(
        expand_kernel,
        (1,),
        [SCALARS]
        + [whole(a.shape) for a in (value, sums, gain, bias, inside)]
        + [whole((deep, 2048))],
        [kept((rows, deep)), kept((rows, 2048)), kept((2, 2048))],
        [((rows, deep), BF16), ((rows, 2048), BF16), ((2, 2048), F32)],
        [],
        2 * rows * deep * 2048,
        count,
        value,
        sums,
        gain,
        bias,
        inside,
        weights,
    )


def head_kernel(
    count_ref, at_ref, keep_ref, got_ref, base_keep, base_got, sums_ref, gain_ref, bias_ref, inside_ref, w_ref,
    out_ref, out_sums, trunk_ref, slope_ref, steep_ref, stack_ref,
):
    tap = pl.program_id(0)
    strip = 2 * PITCH

    @pl.when(tap == 0)
    def _():
        clear_ends(stack_ref, PITCH)
        mean, inverse = moments(sums_ref, count_ref[0])
        for k, (values, bases) in enumerate(((keep_ref, base_keep), (got_ref, base_got))):

            @pl.loop(0, 4)
            def _(r):
                source = pl.ds(pl.multiple_of(r * PITCH, 16), PITCH)
                first = at_ref[2 * k + r // 2] + (r % 2) * PITCH
                first = pl.multiple_of(first, 16)
                rows = pl.ds(first, PITCH)
                inside = inside_ref[rows, :]
                for c in range(4):
                    columns = slice(c * 512, (c + 1) * 512)
                    centred = (values[source, columns].astype(F32) - mean[:, columns]) * inverse[:, columns]
                    joined = (
                        gain_ref[:, columns] * centred
                        + bias_ref[:, columns]
                        + bases[source, columns].astype(F32)
                    )
                    level, bend, squared = gelu_parts(joined)
                    trunk = joined * level * inside
                    slope = (
                        level + 0.5 * joined * (1.0 - bend * bend) * ROOT * (1.0 + 3.0 * CUBE * squared)
                    ) * inside
                    trunk_ref[rows, columns] = trunk.astype(BF16)
                    slope_ref[rows, columns] = slope.astype(BF16)
                    steep_ref[rows, columns] = (slope * centred).astype(BF16)
                    store_moved(stack_ref, pl.multiple_of(first + PITCH, 16), trunk, 1, columns)

        out_ref[...] = jnp.zeros_like(out_ref)

    start = pl.multiple_of((tap // 3) * PITCH, 16)
    out_ref[...] += jnp.dot(
        stack_ref[tap % 3, pl.ds(start, 4 * strip), :], w_ref[...], preferred_element_type=F32
    )

    @pl.when(tap == 8)
    def _():
        value = out_ref[...] * inside_ref[...]
        store_sums(out_sums, value, value * out_ref[...])


def head_forward(count, at, keep, got, base_keep, base_got, sums, gain, bias, inside, weights):
    rows = inside.shape[0]
    deep = keep.shape[1]
    return call(
        head_kernel,
        (9,),
        [SCALARS, SCALARS]
        + [whole(keep.shape)] * 4
        + [whole(a.shape) for a in (sums, gain, bias, inside)]
        + [pl.BlockSpec((deep, 512), lambda t: (0, t))],
        [whole((rows, 512)), kept((2, 512))] + [whole((rows, deep))] * 3,
        [((rows, 512), F32), ((2, 512), F32)] + [((rows, deep), BF16)] * 3,
        [pltpu.VMEM((3, rows + 2 * PITCH, deep), BF16)],
        18 * rows * deep * 512,
        count,
        at,
        keep,
        got,
        base_keep,
        base_got,
        sums,
        gain,
        bias,
        inside,
        weights,
    )


def message_kernel(
    count_ref, at_ref, y_ref, value_ref, sums_ref, gain_ref, bias_ref, inside_ref, w_ref, cot_keep, cot_got,
    task_ref, streams_keep, streams_give, d_message_ref, d_logit_ref, d_norm_ref, out_sums,
    stack_ref, total_ref, gate_ref,
):
    rows_all, deep = value_ref.shape
    mean, inverse = moments(sums_ref, count_ref[0])
    gain, bias = gain_ref[...], bias_ref[...]
    number = y_ref[0]
    clear_ends(stack_ref, PITCH)

    def centred_at(rows):
        return (value_ref[rows, :] - mean) * inverse

    @pl.loop(0, 8)
    def _(r):
        at = pl.multiple_of(r * PITCH, 16)
        rows = pl.ds(at, PITCH)
        task = gelu(gain * centred_at(rows) + bias) * inside_ref[rows, :]
        task_ref[rows, :] = task.astype(BF16)
        store_moved(stack_ref, pl.multiple_of(at + PITCH, 16), task, 1)

    gate_ref[...] = jnp.dot(
        task_ref[...], w_ref[:, 9 * 512 : 10 * 512], preferred_element_type=F32
    )
    total_ref[...] = jnp.zeros_like(total_ref)

    @pl.loop(0, 9)
    def _(tap):
        start = pl.multiple_of((tap // 3) * PITCH, 16)
        total_ref[...] += jnp.dot(
            stack_ref[tap % 3, pl.ds(start, rows_all), :],
            w_ref[:, pl.ds(pl.multiple_of(tap * 512, 512), 512)],
            preferred_element_type=F32,
        )

    for k, cots in enumerate((cot_keep, cot_got)):

        @pl.loop(0, 4)
        def _(r):
            source = pl.ds(pl.multiple_of(r * PITCH, 16), PITCH)
            at = pl.multiple_of(at_ref[2 * k + r // 2] + (r % 2) * PITCH, 16)
            rows = pl.ds(at, PITCH)
            inside = inside_ref[rows, :]
            message = total_ref[rows, :]
            gate = 1.0 / (1.0 + jnp.exp(-gate_ref[rows, :]))
            cot_depth = cots[source, :deep].astype(F32) * inside
            cot_seg = cots[source, deep:].astype(F32) * inside
            receive = jnp.where(
                number == 0, cot_seg, jnp.where(number == 1, cot_depth, cot_depth + cot_seg)
            )
            direct = jnp.where(
                number == 0, cot_depth, jnp.where(number == 1, cot_seg, jnp.zeros_like(cot_seg))
            )
            task = task_ref[rows, :]
            gated = (gate * message).astype(BF16)
            slot = pl.ds(pl.multiple_of((r % 2) * PITCH, 16), PITCH)
            streams_ref = (streams_keep, streams_give)[k]
            streams_ref[r // 2, slot, :deep] = jnp.where(number == 0, task, gated)
            streams_ref[r // 2, slot, deep:] = jnp.where(number == 1, task, gated)
            d_logit_ref[rows, :] = (receive * message * gate * (1.0 - gate)).astype(BF16)
            d_message = receive * gate
            d_message_ref[rows, :] = d_message.astype(BF16)
            store_moved(stack_ref, pl.multiple_of(at + PITCH, 16), d_message, 1)
            total_ref[rows, :] = direct

    total_ref[...] += times_turned(d_logit_ref[...], w_ref[:, 9 * 512 : 10 * 512])

    @pl.loop(0, 9)
    def _(tap):
        start = pl.multiple_of((2 - tap // 3) * PITCH, 16)
        total_ref[...] += times_turned(
            stack_ref[2 - tap % 3, pl.ds(start, rows_all), :],
            w_ref[:, pl.ds(pl.multiple_of(tap * 512, 512), 512)],
        )

    out_sums[...] = jnp.zeros_like(out_sums)

    @pl.loop(0, 8)
    def _(r):
        rows = pl.ds(pl.multiple_of(r * PITCH, 16), PITCH)
        centred = centred_at(rows)
        upstream = gelu_slope(gain * centred + bias) * total_ref[rows, :] * inside_ref[rows, :]
        d_norm_ref[rows, :] = upstream
        add_sums(out_sums, upstream * centred, upstream)


def message_stage(count, at, y, value, sums, gain, bias, inside, weights, cot_keep, cot_got):
    rows, deep = value.shape
    return call(
        message_kernel,
        (1,),
        [SCALARS] * 3
        + [whole(a.shape) for a in (value, sums, gain, bias, inside, weights)]
        + [whole((rows // 2, 2 * deep))] * 2,
        [
            kept((rows, deep)),
            kept((2, rows // 4, 2 * deep)),
            kept((2, rows // 4, 2 * deep)),
            kept((rows, deep)),
            kept((rows, deep)),
            kept((rows, deep)),
            kept((2, deep)),
        ],
        [
            ((rows, deep), BF16),
            ((2, rows // 4, 2 * deep), BF16),
            ((2, rows // 4, 2 * deep), BF16),
            ((rows, deep), BF16),
            ((rows, deep), BF16),
            ((rows, deep), F32),
            ((2, deep), F32),
        ],
        [
            pltpu.VMEM((3, rows + 2 * PITCH, deep), BF16),
            pltpu.VMEM((rows, deep), F32),
            pltpu.VMEM((rows, deep), F32),
        ],
        40 * rows * deep * 512,
        count,
        at,
        y,
        value,
        sums,
        gain,
        bias,
        inside,
        weights,
        cot_keep,
        cot_got,
    )


def weight_kernel(dilation, chunk, x_ref, g_ref, *rest):
    *more, out_ref, turned_ref, stack_ref = rest
    tap = pl.program_id(0)
    rows = x_ref.shape[0]

    @pl.when(tap == 0)
    def _():
        for c in range(0, x_ref.shape[1], chunk):
            turned_ref[c : c + chunk, :] = x_ref[:, c : c + chunk].T
        move_map(stack_ref, g_ref, dilation)

    def product(g):
        return jnp.dot(turned_ref[...], g, preferred_element_type=F32).astype(BF16)

    @pl.when(tap < 9)
    def _():
        start = pl.multiple_of((2 - tap // 3) * dilation * PITCH, 16)
        out_ref[...] = product(stack_ref[2 - tap % 3, pl.ds(start, rows), :])

    if more:

        @pl.when(tap == 9)
        def _():
            out_ref[...] = product(more[0][...])


def conv_weight(image, upstream, dilation, centre=()):
    rows, deep = image.shape
    wide = upstream.shape[1]
    blocks = 9 + len(centre)
    (out,) = call(
        functools.partial(weight_kernel, dilation, 512),
        (blocks,),
        [whole((rows, deep)), whole((rows, wide))] + [whole((rows, wide)) for a in centre],
        [pl.BlockSpec((deep, wide), lambda t: (0, t))],
        [((deep, blocks * wide), BF16)],
        [
            pltpu.VMEM((deep, rows), BF16),
            pltpu.VMEM((3, rows + 2 * dilation * PITCH, wide), BF16),
        ],
        2 * blocks * rows * deep * wide,
        image,
        upstream,
        *centre,
    )
    return out


def trunk_kernel(
    at_ref, g_ref, slope_ref, steep_ref, w_ref, keep_ref, give_ref, sums_ref, stack_ref, turned_ref, total_ref, line_ref
):
    tap = pl.program_id(0)
    rows = g_ref.shape[0]

    @pl.when(tap == 0)
    def _():
        move_map(stack_ref, g_ref, 1)
        for k in range(9):
            start = (2 - k // 3) * PITCH
            turned_ref[k] = stack_ref[2 - k % 3, start : start + rows, :].T

    part = jnp.dot(w_ref[...], turned_ref[tap], preferred_element_type=F32)

    @pl.when(tap == 0)
    def _():
        total_ref[...] = part

    @pl.when(tap > 0)
    def _():
        total_ref[...] += part

    @pl.when(tap == 8)
    def _():
        for c in range(0, total_ref.shape[0], 512):
            columns = slice(c, c + 512)
            value = total_ref[columns, :].T
            line_ref[...] = value
            sums_ref[0:1, columns] = jnp.sum(
                value * steep_ref[:, columns].astype(F32), axis=0, keepdims=True
            )
            sums_ref[1:2, columns] = jnp.sum(
                value * slope_ref[:, columns].astype(F32), axis=0, keepdims=True
            )
            for k in range(4):
                start = pl.multiple_of(at_ref[k], 16)
                out_ref = (keep_ref, give_ref)[k // 2]
                out_ref[k % 2, :, columns] = line_ref[pl.ds(start, rows // 4), :].astype(BF16)


def trunk_back(at, upstream, slope, steep, weights):
    rows, wide = upstream.shape
    deep = weights.shape[0]
    return call(
        trunk_kernel,
        (9,),
        [SCALARS, whole((rows, wide)), whole((rows, deep)), whole((rows, deep))]
        + [pl.BlockSpec((deep, wide), lambda t: (0, t))],
        [whole((2, rows // 4, deep))] * 2 + [kept((2, deep))],
        [((2, rows // 4, deep), BF16)] * 2 + [((2, deep), F32)],
        [
            pltpu.VMEM((3, rows + 2 * PITCH, wide), BF16),
            pltpu.VMEM((9, wide, rows), BF16),
            pltpu.VMEM((deep, rows), F32),
            pltpu.VMEM((rows, 512), F32),
        ],
        18 * rows * deep * wide,
        at,
        upstream,
        slope,
        steep,
        weights,
    )
def joined_kernel(
    count_ref, at_ref, own_ref, near_ref, far_ref, pre_ref, base_ref, sums_ref, gain_ref, bias_ref, inside_ref, back_ref,
    w_ref, low_ref, low_sums, low_gain, low_bias,
    d_joined_ref, c0, c1, c2, c3, d_norm_ref, out_sums, d_pre_ref,
):
    count = count_ref[0]
    mean, inverse = moments(sums_ref, count)
    inside = inside_ref[...]
    for c in range(4):
        columns = slice(c * 512, (c + 1) * 512)
        centred = (pre_ref[:, columns].astype(F32) - mean[:, columns]) * inverse[:, columns]
        gain = gain_ref[:, columns]
        joined = gain * centred + bias_ref[:, columns] + base_ref[:, columns].astype(F32)
        d_trunk = (
            own_ref[:, columns].astype(F32)
            + near_ref[:, columns].astype(F32)
            + far_ref[:, columns].astype(F32)
        )
        d_joined = gelu_slope(joined) * d_trunk * inside
        d_joined_ref[:, columns] = d_joined
        shift = (back_ref[1:2, columns] + centred * back_ref[0:1, columns]) / count
        d_pre_ref[:, columns] = (
            inside * gain * inverse[:, columns] * (d_joined - shift)
        ).astype(BF16)
    for k, part_ref in enumerate((c0, c1, c2, c3)):
        first = pl.multiple_of(at_ref[k] // (2 * PITCH) * 512, 512)
        part_ref[...] = d_pre_ref[:, pl.ds(first, 512)]
    d_act = times_turned(d_pre_ref[...], w_ref[...])
    mean, inverse = moments(low_sums, count)
    centred = (low_ref[...].astype(F32) - mean) * inverse
    upstream = gelu_slope(low_gain[...] * centred + low_bias[...]) * d_act * inside
    upstream = upstream.astype(BF16)
    d_norm_ref[...] = upstream
    upstream = upstream.astype(F32)
    store_sums(out_sums, upstream * centred, upstream)


def joined_back(count, at, pieces, pre, base, sums, gain, bias, inside, back, weights, low, low_sums, low_gain, low_bias):
    rows, deep = pre.shape
    narrow = low.shape[1]
    operands = (*pieces, pre, base, sums, gain, bias, inside, back)
    lower = (low, low_sums, low_gain, low_bias)
    out_d_joined, *columns, out_d_norm, out_sums = call(
        joined_kernel,
        (1,),
        [SCALARS, SCALARS]
        + [whole(a.shape) for a in pieces]
        + [whole(pre.shape)] * 2
        + [whole(a.shape) for a in operands[5:]]
        + [whole((narrow, deep))]
        + [whole(a.shape) for a in lower],
        [kept((rows, deep))] + [kept((rows, 512))] * 4 + [kept((rows, narrow)), kept((2, narrow))],
        [((rows, deep), F32)]
        + [((rows, 512), BF16)] * 4
        + [((rows, narrow), BF16), ((2, narrow), F32)],
        [pltpu.VMEM((rows, deep), BF16)],
        2 * rows * deep * narrow,
        count,
        at,
        *operands,
        weights,
        *lower,
    )
    return out_d_joined, columns, out_d_norm, out_sums


def dilated_back_kernel(
    count_ref, at_ref, u0, u1, u2, u3, p0, p1, p2, p3, sums_ref, back_ref, gain_ref, inside_ref,
    w_ref, low_ref, low_sums, low_gain, low_bias, mine_ref,
    d_norm_ref, out_sums, part_ref,
    image_ref, stack_ref, turned_ref, total_ref,
):
    tap = pl.program_id(0)
    strip = 2 * PITCH
    count = count_ref[0]

    @pl.when(tap == 0)
    def _():
        clear_image(image_ref)
        mean, inverse = moments(sums_ref, count)
        for k, (up, value) in enumerate(((u0, p0), (u1, p1), (u2, p2), (u3, p3))):
            start = pl.multiple_of(at_ref[k], 16)
            centred = (value[...].astype(F32) - mean) * inverse
            shift = (back_ref[1:2, :] + centred * back_ref[0:1, :]) / count
            scale = inside_ref[pl.ds(start, strip), :] * (gain_ref[...] * inverse)
            lowered = (scale * (up[...].astype(F32) - shift)).astype(BF16)
            image_ref[pl.ds(pl.multiple_of(start + strip, 16), strip), :] = lowered
        window_moved(stack_ref, image_ref, at_ref[0])
        mine = pl.multiple_of(at_ref[0] // strip * 128, 128)
        part_ref[...] = image_ref[strip : 5 * strip, pl.ds(mine, 128)]
        for k in range(9):
            start = (2 - k // 3) * strip
            turned_ref[k] = stack_ref[2 - k % 3, start : start + strip, :].T
        total_ref[...] = jnp.zeros_like(total_ref)

    total_ref[...] += jnp.dot(w_ref[...], turned_ref[tap], preferred_element_type=F32)

    @pl.when(tap == 8)
    def _():
        mean, inverse = moments(low_sums, count)
        centred = (low_ref[...].astype(F32) - mean) * inverse
        slope = gelu_slope(low_gain[...] * centred + low_bias[...])
        upstream = (slope * total_ref[...].T * mine_ref[...]).astype(BF16)
        d_norm_ref[...] = upstream
        upstream = upstream.astype(F32)
        store_sums(out_sums, upstream * centred, upstream)


def dilated_back(
    count, at, ups, values, sums, back, gain, inside, weights, first_block, low, low_sums, low_gain, low_bias, mine
):
    strip, wide = ups[0].shape
    operands = (*ups, *values, sums, back, gain, inside)
    lower = (low, low_sums, low_gain, low_bias, mine)
    return call(
        dilated_back_kernel,
        (9,),
        [SCALARS, SCALARS]
        + [whole(a.shape) for a in operands]
        + [pl.BlockSpec((512, wide), lambda t: (0, first_block + t))]
        + [whole(a.shape) for a in lower],
        [kept((strip, 512)), kept((2, 512)), kept((4 * strip, 128))],
        [((strip, 512), BF16), ((2, 512), F32), ((4 * strip, 128), BF16)],
        [
            pltpu.VMEM((6 * strip, wide), BF16),
            pltpu.VMEM((3, 3 * strip, wide), BF16),
            pltpu.VMEM((9, wide, strip), BF16),
            pltpu.VMEM((512, strip), F32),
        ],
        18 * strip * wide * 512,
        count,
        at,
        *operands,
        weights,
        *lower,
    )


def heads_kernel(at_ref, local_ref, *refs):
    *pieces, got_ref = refs[:5]
    outs = refs[5:]

    def put(k, value):
        first = 0
        for out_ref in outs:
            last = first + out_ref.shape[2]
            out_ref[at_ref[k]] = value[:, first:last].astype(F32)
            first = last

    @pl.when(local_ref[0] == 1)
    def _():
        for k, piece in enumerate(pieces):
            put(k, piece)

    @pl.when(local_ref[0] == 0)
    def _():
        for k in range(4):
            put(k, got_ref.at[k])


def heads_placed(at, local, pieces, got, widths):
    rows, deep = pieces[0].shape
    return call(
        heads_kernel,
        (1,),
        [SCALARS, SCALARS] + [whole((rows, deep))] * 4 + [whole((4, rows, deep))],
        [whole((4, rows, wide)) for wide in widths],
        [((4, rows, wide), F32) for wide in widths],
        [],
        0,
        at,
        local,
        *pieces,
        got,
    )


def sums_of(value):
    return jnp.stack([jnp.sum(value, axis=0), jnp.sum(value * value, axis=0)])


def centred_by(value, sums, count):
    mean = sums[0] / count
    inverse = lax.rsqrt(sums[1] / count - mean * mean + EPS)
    return (value.astype(F32) - mean) * inverse, inverse


def norm_back(upstream, value, sums, gain, inside, back, count):
    centred, inverse = centred_by(value, sums, count)
    return (
        inside * gain * inverse * (upstream.astype(F32) - (back[1] + centred * back[0]) / count)
    ).astype(BF16)


def turned_dot(first, second):
    return lax.dot_general(first, second, (((0,), (0,)), ((), ())), preferred_element_type=F32)


def strips_of(value):
    _, rows, across, deep = value.shape
    padded = jnp.pad(value[0], ((0, 0), (0, PITCH - across), (0, 0)))
    return padded.reshape(rows * PITCH, deep)


def maps_of(value, across):
    rows = value.shape[0] // PITCH
    return value.reshape(1, rows, PITCH, -1)[:, :, :across]


def shares_summed(value, axes, dtype=BF16):
    count = lax.axis_size(axes)
    parts = lax.all_to_all(
        value.reshape(count, value.shape[0] // count, value.shape[1]), axes, 0, 0
    )
    return jnp.sum(parts.astype(F32), axis=0).astype(dtype)


def shards(
    features,
    image_size,
    reduce_weight,
    dilated_weight,
    expand_weight,
    head_weight,
    message_weight,
    gate_weight,
    bottleneck_gain,
    bottleneck_bias,
    expand_gain,
    expand_bias,
    head_gain,
    head_bias,
    depth_cotangent,
    seg_cotangent,
):
    ylo, core, yhi = (lax.axis_index(a) for a in ("ylo", "core", "yhi"))
    plane = lax.axis_index("x") * 4 + lax.axis_index("z")
    y = yhi * 2 + ylo
    strip = ylo * 2 + core
    across = features.shape[2]
    local = core == yhi

    count = jnp.sum(image_size[:, 0].astype(F32) * image_size[:, 1].astype(F32))
    count_here = count.reshape(1)

    def inside_of(sizes, image, first, rows):
        size = lax.dynamic_index_in_dim(sizes, image, 0, keepdims=False)
        at = jnp.arange(rows * PITCH, dtype=jnp.int32)
        valid = (first + at // PITCH < size[0]) & (at % PITCH < size[1])
        return valid.astype(F32)[:, None]

    length = 2 * PITCH
    row_at = (jnp.stack([strip, strip ^ 2, strip ^ 1, strip ^ 3]) * length).astype(jnp.int32)
    head_at = (
        jnp.stack(
            [
                ylo * 2 + core,
                (1 - ylo) * 2 + core,
                ylo * 2 + 1 - core,
                (1 - ylo) * 2 + 1 - core,
            ]
        )
        * length
    ).astype(jnp.int32)

    group = [(i, i ^ 5) for i in range(8) if (i >> 1) & 1 == i & 1]

    def brought(mine, sent):
        return jnp.where(local, mine, lax.ppermute(sent, GROUP, group))

    def of_head(stacked, head):
        return lax.dynamic_index_in_dim(stacked, head, 0, keepdims=False)

    planes = 16
    deep = features.shape[3]
    same = yhi == core
    reduce_part = brought(reduce_weight, reduce_weight)
    copies, y_first, sizes_first, feature_maps, dilated_first, expand_first = hold(
        jnp.broadcast_to(reduce_part[None], (planes,) + reduce_part.shape),
        y,
        image_size,
        features,
        dilated_weight,
        expand_weight,
    )
    reduce_half = lax.all_to_all(copies, ("x", "z"), 0, 0)
    whole_reduce = jnp.stack(
        in_order(reduce_half, over_core(reduce_half), core), axis=1
    ).reshape(-1, reduce_weight.shape[1])
    inside = inside_of(sizes_first, plane * 2 + yhi, strip * 2, 2)
    inside_own = inside_of(sizes_first, plane * 2 + yhi, 0, 8)
    inside_whole = inside_of(sizes_first, plane * 2 + core, 0, 8)
    base = strips_of(feature_maps) * inside.astype(BF16)
    near, far = beside_y(base)
    trunk_weights = jnp.concatenate([expand_first, dilated_first], axis=1)
    trunk_part = brought(trunk_weights, trunk_weights)
    whole_trunk = lax.all_gather(trunk_part, POOL, axis=0, tiled=True)
    first_tap = expand_weight.shape[1] // 512
    task_weights = jnp.concatenate([message_weight, gate_weight], axis=2)
    head_part = brought(of_head(head_weight, y_first), of_head(head_weight, y_first ^ 3))
    task_part = brought(of_head(task_weights, y_first), of_head(task_weights, y_first ^ 3))
    whole_reduce, near, far, head_part, task_part, inside, inside_own, inside_whole = hold(
        whole_reduce, near, far, head_part, task_part, inside, inside_own, inside_whole
    )
    whole_head = lax.all_gather(head_part, POOL, axis=0, tiled=True)
    whole_task = lax.all_gather(task_part, POOL, axis=0, tiled=True)

    pre_one = jnp.dot(base, whole_reduce, preferred_element_type=F32).astype(BF16)
    wide_one = pre_one.astype(F32)
    sums_one = sums_of(wide_one)
    across_low, across_high = across_y(near, far)
    sums_one = fold(sums_one, CORE, *LINE)
    sums_one, ones = hold(sums_one, beside_rows(pre_one))
    sums_one = fold(sums_one, *PLANE, *RIDGE)
    pre_two, sums_two, act_one_image = dilated_forward(
        count_here,
        row_at,
        ones,
        sums_one,
        bottleneck_gain[:1],
        bottleneck_bias[:1],
        inside_own,
        inside,
        whole_trunk,
        first_tap,
    )
    pre_two, sums_two, near, far, across_low, across_high = hold(
        pre_two, sums_two, near, far, across_low, across_high
    )
    base_own = jnp.concatenate([base, near])
    base_other = jnp.concatenate([across_low, across_high, far])
    base_keep = jnp.where(same, base_own, base_other)
    base_got = over_core(jnp.where(same, base_other, base_own))
    base_image = jnp.concatenate([base_own, over_core(base_own)])
    sums_two = fold(sums_two, CORE, *LINE, *PLANE)
    sums_two, base_keep, base_got, base_image = hold(sums_two, base_keep, base_got, base_image)
    sums_two = fold(sums_two, *RIDGE)
    act_two, pre_three, sums_three = expand_forward(
        count_here, pre_two, sums_two, bottleneck_gain[1:], bottleneck_bias[1:], inside, whole_trunk
    )
    near, far = beside_y(pre_three)
    sums_three = fold(sums_three, CORE, *LINE)
    sums_three, near, far = hold(sums_three, near, far)
    across_low, across_high = across_y(near, far)
    sums_three = fold(sums_three, *PLANE)
    sums_three, near, far, across_low, across_high = hold(
        sums_three, near, far, across_low, across_high
    )
    pre_own = jnp.concatenate([pre_three, near])
    pre_other = jnp.concatenate([across_low, across_high, far])
    pre_keep = jnp.where(same, pre_own, pre_other)
    pre_got = over_core(jnp.where(same, pre_other, pre_own))
    sums_three = fold(sums_three, *RIDGE)
    sums_three, depth_cots, seg_cots = hold(sums_three, depth_cotangent, seg_cotangent)

    gain_here, bias_here = of_head(head_gain, y)[None], of_head(head_bias, y)[None]
    wide_gain, wide_bias = expand_gain[None], expand_bias[None]
    pre_head, sums_head, trunk, slope, steep = head_forward(
        count_here,
        head_at,
        pre_keep,
        pre_got,
        base_keep,
        base_got,
        sums_three,
        wide_gain,
        wide_bias,
        inside_whole,
        whole_head,
    )
    cots = jnp.concatenate([strips_of(depth_cots), strips_of(seg_cots)], axis=1)
    near, far = beside_y(cots)
    sums_head, near, far = hold(sums_head, near, far)
    across_low, across_high = across_y(near, far)
    sums_head = fold(sums_head, CORE, *LINE)
    sums_head, near, far, across_low, across_high = hold(
        sums_head, near, far, across_low, across_high
    )
    cots_own = jnp.concatenate([cots, near])
    cots_other = jnp.concatenate([across_low, across_high, far])
    cots_keep = jnp.where(same, cots_own, cots_other)
    cots_got = over_core(jnp.where(same, cots_other, cots_own))
    sums_head = fold(sums_head, *PLANE)
    task, streams_keep, streams_give, d_message, d_logit, d_norm_head, back_here = message_stage(
        count_here,
        head_at,
        y.astype(jnp.int32).reshape(1),
        pre_head,
        sums_head,
        gain_here,
        bias_here,
        inside_whole,
        whole_task,
        cots_keep,
        cots_got,
    )
    task_grad, back_here = hold(conv_weight(task, d_message, 1, (d_logit,)), back_here)
    task_share = lax.psum_scatter(task_grad, POOL, scatter_dimension=0, tiled=True)
    back_head = fold(back_here, CORE, *LINE)
    back_head, twos = hold(back_head, beside_rows(pre_two))
    back_head = fold(back_head, *PLANE)
    back_head, streams_keep, streams_got = hold(
        back_head, streams_keep, over_core(streams_give)
    )
    d_pre_head = norm_back(
        d_norm_head, pre_head, sums_head, gain_here, inside_whole, back_head, count
    )
    streams_own, streams_other = sent_home(streams_keep, streams_got, same)
    d_pre_head, streams_own, streams_other = hold(d_pre_head, streams_own, streams_other)
    from_near, from_far = half_way(streams_other)
    head_grad = conv_weight(trunk, d_pre_head, 1)
    head_grad, d_pre_head, from_near, from_far = hold(head_grad, d_pre_head, from_near, from_far)
    streams = last_way(streams_own, streams_other, from_near, from_far)
    trunk_keep, trunk_give, back_three = trunk_back(head_at, d_pre_head, slope, steep, whole_head)
    trunk_keep, trunk_give, back_three, streams, head_grad, task_share = hold(
        trunk_keep, trunk_give, back_three, streams, head_grad, task_share
    )
    head_share = lax.psum_scatter(head_grad, POOL, scatter_dimension=0, tiled=True)
    placed = jnp.where(
        jnp.arange(4)[None, :, None] == y, back_here[:, None], jnp.zeros((1, 1, 1), F32)
    ).reshape(2, -1)
    back_wide = fold(jnp.concatenate([back_three, placed], axis=1), CORE)
    back_wide, trunk_keep, trunk_got = hold(back_wide, trunk_keep, over_core(trunk_give))
    trunk_own, trunk_other = sent_home(trunk_keep, trunk_got, same)
    from_near, from_far = half_way(trunk_other)
    back_wide = fold(back_wide, *LINE)
    back_wide, from_near, from_far = hold(back_wide, from_near, from_far)
    pieces = last_way(trunk_own, trunk_other, from_near, from_far)
    back_wide = fold(back_wide, *PLANE)
    back_wide, pieces = hold(back_wide, pieces)
    back_wide = fold(back_wide, *RIDGE)
    back_three, back_heads = back_wide[:, :deep], back_wide[:, deep:]
    d_joined, d_three_parts, d_norm_two, back_two = joined_back(
        count_here,
        row_at,
        pieces,
        pre_three,
        base,
        sums_three,
        wide_gain,
        wide_bias,
        inside,
        back_three,
        whole_trunk,
        pre_two,
        sums_two,
        bottleneck_gain[1:],
        bottleneck_bias[1:],
    )
    back_two = fold(back_two, CORE, *LINE)
    back_two, d_norm_twos = hold(back_two, beside_rows(d_norm_two))
    back_two = fold(back_two, *PLANE, *RIDGE)

    d_three_part = jnp.concatenate(from_rows(d_three_parts))
    normed_rows, unused = centred_by(jnp.concatenate(twos), sums_two, count)
    act_two_rows = jax.nn.gelu(
        bottleneck_gain[1] * normed_rows + bottleneck_bias[1]
    ).astype(BF16)
    grad_expand = turned_dot(act_two_rows, d_three_part).astype(BF16)
    back_two, grad_expand = hold(back_two, grad_expand)
    d_norm_one, back_one, d_two_part = dilated_back(
        count_here,
        row_at,
        d_norm_twos,
        twos,
        sums_two,
        back_two,
        bottleneck_gain[1:],
        inside_own,
        whole_trunk,
        first_tap,
        pre_one,
        sums_one,
        bottleneck_gain[:1],
        bottleneck_bias[:1],
        inside,
    )
    def to_chips(share):
        pieces = [share]
        for flip in (1, 2, 3):
            pairs = []
            for i in range(8):
                low, c, high = i >> 2, (i >> 1) & 1, i & 1
                to = (high * 2 + low) ^ flip
                if to >> 1 == c:
                    pairs.append((i, ((to & 1) << 2) | (c << 1) | (to >> 1)))
            pieces.append(lax.ppermute(share, GROUP, pairs))
        return tuple(pieces)

    heads_at = jnp.stack([y, y ^ 1, y ^ 2, y ^ 3]).astype(jnp.int32)
    local_here = local.astype(jnp.int32).reshape(1)

    def to_cores(pieces, *widths):
        pairs = [(i, i ^ 2) for i in range(8) if (i >> 1) & 1 == i & 1]
        got = lax.ppermute(jnp.stack(pieces), GROUP, pairs)
        return heads_placed(heads_at, local_here, pieces, got, widths)

    back_one = fold(back_one, CORE, *RIDGE)
    grad_dilated = conv_weight(act_one_image, d_two_part, 2)
    trunk_grad = jnp.concatenate([grad_expand, grad_dilated], axis=1)
    back_one = fold(back_one, *LINE, *PLANE)
    back_one, trunk_grad, head_share = hold(back_one, trunk_grad, head_share)
    d_pre_one = norm_back(
        d_norm_one, pre_one, sums_one, bottleneck_gain[0], inside, back_one, count
    )
    d_one_parts = [
        lax.dynamic_slice_in_dim(d_pre_one, (strip ^ flip) * 128, 128, 1) for flip in (0, 2, 1, 3)
    ]
    d_one_part = jnp.concatenate(from_rows(d_one_parts))
    trunk_share = shares_summed(trunk_grad, IMG)
    grad_reduce = turned_dot(base_image, d_one_part).astype(BF16)
    reduce_share = shares_summed(grad_reduce, IMG)
    head_pieces = to_chips(head_share)

    def all_strips(value):
        pair = in_order(value, over_core(value), core)
        pair = jnp.stack(pair)
        return jnp.concatenate(in_order(pair, over_y(pair, 1), ylo))

    all_trunk = all_strips(trunk_share)
    sum_expand = jnp.moveaxis(all_trunk[:, :, :512], 0, 1).reshape(16, -1).astype(F32)
    sum_dilated = (
        jnp.moveaxis(all_trunk[:, :, 512:].reshape(4, 16, 9, 128), 0, 2)
        .reshape(16, -1)
        .astype(F32)
    )
    sum_reduce = jnp.moveaxis(all_strips(reduce_share), 0, 1).reshape(-1, 512).astype(F32)

    wide = message_weight.shape[2]
    (sum_head,) = to_cores(head_pieces, wide)
    task_share, d_pre_one = hold(task_share, d_pre_one)
    sum_message, sum_gate = to_cores(to_chips(task_share), wide, gate_weight.shape[2])

    d_base = d_joined + times_turned(d_pre_one, whole_reduce)
    input_grad = maps_of(d_base * inside, across)

    streams = maps_of(sum(a.astype(F32) for a in streams) * inside, across)
    depth_out, seg_out = jnp.split(streams, 2, axis=3)

    return (
        depth_out,
        seg_out,
        input_grad,
        sum_reduce,
        sum_dilated,
        sum_expand,
        sum_head,
        sum_message,
        sum_gate,
        jnp.stack([back_one[0], back_two[0]]),
        jnp.stack([back_one[1], back_two[1]]),
        back_three[0],
        back_three[1],
        back_heads[0].reshape(4, -1),
        back_heads[1].reshape(4, -1),
    )


def solution(mesh):
    fine = Mesh(mesh.devices.reshape(2, 2, 4, 4, 2), FINE)
    maps = P(IMG, ROWS, None, None)
    placed = (
        maps,
        P(),
        P(IMG, None),
        P(IMG, None),
        P(IMG, None),
        P(None, IMG, None),
        P(None, IMG, None),
        P(None, IMG, None),
        P(),
        P(),
        P(),
        P(),
        P(),
        P(),
        maps,
        maps,
    )
    return jax.shard_map(
        shards,
        mesh=fine,
        in_specs=placed,
        out_specs=(
            maps,
            maps,
            maps,
            P(IMG, None),
            P(IMG, None),
            P(IMG, None),
            P(None, IMG, None),
            P(None, IMG, None),
            P(None, IMG, None),
            P(),
            P(),
            P(),
            P(),
            P(),
            P(),
        ),
        check_vma=False,
    )
```

time: 864 us -> 589 us (0.68)
  local copies, waits for them, and re-layouts: 138 us -> 27 us
  waiting for transfers between devices: 236 us -> 156 us
  other arithmetic: 126 us -> 48.1 us
  Pallas kernels: 113 us -> 156 us
  blocking collectives: 21.5 us -> 0 us
  matrix products: 23.5 us -> 5.62 us
    ppermute x87 -> x93, waiting for transfers between devices: 178 us -> 119 us  [swap(): return lax.ppermute(value, axis, [(i, i ^ flip) for i in range(count)])]
    pallas_call x9 -> x12, Pallas kernels: 113 us -> 156 us  [call(): pl.pallas_call(kernel, grid=grid, in_specs=in_specs, out_specs=out_specs,...]
    unnamed x251 -> x133, local copies, waits for them, and re-layouts: 34.7 us -> 8.28 us
    another operation x12 -> x2, local copies, waits for them, and re-layouts: 25.2 us -> 1.21 us  [the longest x1 0.61 us: shards(): back_heads[0].reshape(4, -1)]
    slice x23 -> x12, local copies, waits for them, and re-layouts: 26.7 us -> 4.4 us  [the longest x6 2.54 us: across_y(): return (over_y(far[:half], 1), over_y(near[half:], 3))]
    all_to_all x1 -> x0, blocking collectives: 21.5 us -> none  [shards(): lax.all_to_all(jnp.broadcast_to(reduce_part[None], (16,) + reduce_part.sh...]
    ppermute x87 -> x93, starting transfers between devices: 137 us -> 116 us  [swap(): return lax.ppermute(value, axis, [(i, i ^ flip) for i in range(count)])]
    concatenate x26 -> x8, other arithmetic: 24.2 us -> 4.66 us  [the longest x1 2.74 us: shards(): trunk_grad = jnp.concatenate([grad_expand, grad_dilated], axis=1)]
  transfers between devices with their start and end apart: 107 -> 118, of which waited for: 72 -> 65; matrix products, arithmetic and copies ran while one was open for 29% -> 13% of each run, Pallas kernels for 11% -> 21%
where the time goes in v2:
time: 589 us; the launch traced here: 578 us
  starting transfers between devices  169 us (29%)
  waiting for transfers between devices  156 us (26%)
  Pallas kernels  156 us (26%)
  other arithmetic  48.1 us (8%)
  local copies, waits for them, and re-layouts  27 us (5%)
  between operations  15.8 us (3%)
    pallas_call x12, Pallas kernels, call(): pl.pallas_call(kernel, grid=grid, in_specs=in_specs, out_specs=out_specs,...  156 us
    ppermute x93, waiting for transfers between devices, swap(): return lax.ppermute(value, axis, [(i, i ^ flip) for i in range(count)])  119 us
    ppermute x93, starting transfers between devices, swap(): return lax.ppermute(value, axis, [(i, i ^ flip) for i in range(count)])  116 us
    all_to_all x2, starting transfers between devices, shares_summed(): lax.all_to_all(value.reshape(count, value.shape[0] // count, value.shape[...  16.4 us
    ppermute x6, starting transfers between devices, to_chips(): pieces.append(lax.ppermute(share, GROUP, pairs))  14.4 us
    all_to_all x2, waiting for transfers between devices, shares_summed(): lax.all_to_all(value.reshape(count, value.shape[0] // count, value.shape[...  13.1 us
    ppermute x4, waiting for transfers between devices, brought(): return jnp.where(local, mine, lax.ppermute(sent, GROUP, group))  11.9 us
  transfers between devices with their start and end apart: 118, of which 65 were waited for; matrix products, arithmetic and copies ran while one was open for 13% of the time, Pallas kernels for 21%

profile of v2, /device:TPU:1, one launch (start us, length us, event | category | flops | bytes accessed | tf_op | source)
XLA Modules:
  0.0 578.2 jit_solution(4696556690984181750)
XLA Ops:
  8.7 5.4 collective-permute-done
  16.7 6.5 %collective-permute-done.16 = bf16[16,6656]{1,0:T(8,128)(2,1)S(1)} collective-permute-done((bf16[16,6656]{1,0:T(8,128)(2,1)S(1)}, bf16[16,6656]{1,0:T(8,128)(2,1)S(1)}, u32[]{:S(2)}, u32[]{:S(2)}) %collective-permute-start.16) | collective-permute-done | bytes 213024 | tf_op jit(solution)/shard_map/ppermute | solution.py:892
  26.8 8.2 %all-to-all-start = ((bf16[16,64,512]{2,1,0:T(8,128)(2,1)}), bf16[16,64,512]{2,1,0:T(8,128)(2,1)S(1)}, u32[]{:S(2)}, u32[]{:S(2)}) async-start(bf16[16,64,512]{2,1,0:T(8,128)(2,1)} %broadcast_in_dim.36), calls=%async_computation | async-start | bytes 2097152 | tf_op jit(solution)/shard_map/all_to_all | solution.py:909
  47.3 8.3 %collective-permute-start.1 = (bf16[16,64,512]{2,1,0:T(8,128)(2,1)S(1)}, bf16[16,64,512]{2,1,0:T(8,128)(2,1)S(1)}, u32[]{:S(2)}, u32[]{:S(2)}) collective-permute-start(bf16[16,64,512]{2,1,0:T(8,128)(2,1)S(1)} %all-to-all-done), channel_id=1, source_target_pairs={{0,32},{32,0},{1,33},{33,1},{2,34},{34,2},{3,35},{35,3},{4,36},{36... | collective-permute-start | bytes 3145736 | tf_op jit(solution)/shard_map/ppermute | solution.py:27
  71.6 3.4 collective-permute-done.9.p1
  94.1 9.8 %shard_map.271 = (bf16[160,512]{1,0:T(8,128)(2,1)}, f32[2,512]{1,0:T(2,128)}, bf16[640,512]{1,0:T(8,128)(2,1)}) custom-call(f32[1]{0:T(128)} %bitcast.4.count_ref, s32[4]{0:T(128)} %add_multiply_fusion.3.at_ref, bf16[160,512]{1,0:T(8,128)(2,1)} %get-tuple-element.147.p0.low_ref, bf16[160,512]{1,0:T(8,128)(2,1)} %collective-permute-done.9.p1, ...), custom_call_target="tpu_custom_call" | custom-call | flops 754974720 | bytes 7482516 | tf_op jit(solution)/shard_map/pallas_call | solution.py:179
  108.9 3.9 collective-permute-start.25
  113.2 4.0 collective-permute-done.19
  135.7 4.1 collective-permute-done.27
  140.3 3.9 shard_map.272
  144.4 5.8 %collective-permute-start.28 = (f32[2,2048]{1,0:T(2,128)}, f32[2,2048]{1,0:T(2,128)S(1)}, u32[]{:S(2)}, u32[]{:S(2)}) collective-permute-start(f32[2,2048]{1,0:T(2,128)} %get-tuple-element.168), channel_id=1, source_target_pairs={{0,32},{32,0},{1,33},{33,1},{2,34},{34,2},{3,35},{35,3},{4,36},{36... | collective-permute-start | bytes 49160 | tf_op jit(solution)/shard_map/ppermute | solution.py:27
  173.4 3.9 collective-permute-start.37
  185.1 29.6 %shard_map.273 = (f32[640,512]{1,0:T(8,128)}, f32[2,512]{1,0:T(2,128)}, bf16[640,2048]{1,0:T(8,128)(2,1)}, bf16[640,2048]{1,0:T(8,128)(2,1)}, bf16[640,2048]{1,0:T(8,128)(2,1)}) custom-call(f32[1]{0:T(128)} %bitcast.4.count_ref, s32[4]{0:T(128)} %add_multiply_fusion.2.at_ref, bf16[320,2048]{1,0:T(8,128)(2,1)} %get-tuple-element.282.keep_ref, ...), custom_call_target="tpu_custom_call" | custom-call | flops 12079595520 | bytes 24152596 | tf_op jit(solution)/shard_map/pallas_call | solution.py:179
  241.9 20.6 %shard_map.274 = (bf16[640,512]{1,0:T(8,128)(2,1)}, bf16[2,160,1024]{2,1,0:T(8,128)(2,1)}, bf16[2,160,1024]{2,1,0:T(8,128)(2,1)}, bf16[640,512]{1,0:T(8,128)(2,1...) custom-call(f32[1]{0:T(128)} %bitcast.4.count_ref, s32[4]{0:T(128)} %add_multiply_fusion.2.at_ref, ...), custom_call_target="tpu_custom_call" | custom-call | flops 6710886400 | bytes 7875096 | tf_op jit(solution)/shard_map/pallas_call | solution.py:179
  262.5 9.8 %shard_map.275 = bf16[512,5120]{1,0:T(8,128)(2,1)} custom-call(bf16[640,512]{1,0:T(8,128)(2,1)} %get-tuple-element.197.x_ref, bf16[640,512]{1,0:T(8,128)(2,1)} %get-tuple-element.198.g_ref, bf16[640,512]{1,0:T(8,128)(2,1)} %get-tuple-element.199.rest_0_), custom_call_target="tpu_custom_call" | custom-call | flops 3355443200 | bytes 1966080 | tf_op jit(solution)/shard_map/pallas_call | solution.py:179
  298.5 20.9 %shard_map.276 = bf16[2048,4608]{1,0:T(8,128)(2,1)} custom-call(bf16[640,2048]{1,0:T(8,128)(2,1)} %get-tuple-element.182.x_ref, bf16[640,512]{1,0:T(8,128)(2,1)} %multiply_convert_fusion.g_ref), custom_call_target="tpu_custom_call" | custom-call | flops 12079595520 | bytes 3276800 | tf_op jit(solution)/shard_map/pallas_call | solution.py:179
  325.6 29.8 %shard_map.277 = (bf16[2,160,2048]{2,1,0:T(8,128)(2,1)}, bf16[2,160,2048]{2,1,0:T(8,128)(2,1)}, f32[2,2048]{1,0:T(2,128)}) custom-call(s32[4]{0:T(128)} %add_multiply_fusion.2.at_ref, bf16[640,512]{1,0:T(8,128)(2,1)} %multiply_convert_fusion.g_ref, bf16[640,2048]{1,0:T(8,128)(2,1)} %get-tuple-element.211.slope_ref, ...), custom_call_target="tpu_custom_call" | custom-call | flops 12079595520 | bytes 24772624 | tf_op jit(solution)/shard_map/pallas_call | solution.py:179
  356.4 6.1 %collective-permute-start.64 = (bf16[2,160,2048]{2,1,0:T(8,128)(2,1)}, bf16[2,160,2048]{2,1,0:T(8,128)(2,1)S(1)}, u32[]{:S(2)}, u32[]{:S(2)}) collective-permute-start(bf16[2,160,2048]{2,1,0:T(8,128)(2,1)} %get-tuple-element.226), channel_id=1, source_target_pairs={{0,32},{32,0},{1,33},{33,1},{2,34},{34,2},{3,35},{35,3},{4,36},{36... | collective-permute-start | bytes 3932168 | tf_op jit(solution)/shard_map/ppermute | solution.py:27
  372.4 3.5 collective-permute-done.68
  384.8 7.6 %collective-permute-done.72.far_ref = bf16[160,2048]{1,0:T(8,128)(2,1)S(1)} collective-permute-done((bf16[160,2048]{1,0:T(8,128)(2,1)S(1)}, bf16[160,2048]{1,0:T(8,128)(2,1)S(1)}, u32[]{:S(2)}, u32[]{:S(2)}) %collective-permute-start.72) | collective-permute-done | bytes 655392 | tf_op jit(solution)/shard_map/ppermute | solution.py:27
  400.2 7.2 %shard_map.278 = (f32[160,2048]{1,0:T(8,128)}, bf16[160,512]{1,0:T(8,128)(2,1)}, bf16[160,512]{1,0:T(8,128)(2,1)}, bf16[160,512]{1,0:T(8,128)(2,1)}, bf16[160,51...) custom-call(f32[1]{0:T(128)} %bitcast.4.count_ref, s32[4]{0:T(128)} %add_multiply_fusion.3.at_ref, ...), custom_call_target="tpu_custom_call" | custom-call | flops 335544320 | bytes 10314388 | tf_op jit(solution)/shard_map/pallas_call | solution.py:179
  433.2 4.2 collective-permute-done.83
  442.1 10.8 %shard_map.279 = (bf16[160,512]{1,0:T(8,128)(2,1)}, f32[2,512]{1,0:T(2,128)}, bf16[640,128]{1,0:T(8,128)(2,1)}) custom-call(f32[1]{0:T(128)} %bitcast.4.count_ref, s32[4]{0:T(128)} %add_multiply_fusion.3.at_ref, bf16[160,512]{1,0:T(8,128)(2,1)} %get-tuple-element.241.u0, bf16[160,512]{1,0:T(8,128)(2,1)} %copy-done.37, bf16[160,512]{1,0:T(8,128)(2,1)} %copy-done.36, ...), custom_call_target="tpu_custom_call" | custom-call | flops 754974720 | bytes 8311956 | tf_op jit(solution)/shard_map/pallas_call | solution.py:179
  469.1 6.5 %shard_map.280 = bf16[512,1152]{1,0:T(8,128)(2,1)} custom-call(bf16[640,512]{1,0:T(8,128)(2,1)} %get-tuple-element.258.x_ref, bf16[640,128]{1,0:T(8,128)(2,1)} %get-tuple-element.259.g_ref), custom_call_target="tpu_custom_call" | custom-call | flops 754974720 | bytes 819200 | tf_op jit(solution)/shard_map/pallas_call | solution.py:179
  478.6 3.6 collective-permute-done.94
  482.3 3.9 collective-permute-start.104
  499.0 12.4 %all-to-all-start.1 = ((bf16[32,64,128]{2,1,0:T(8,128)(2,1)}), bf16[32,64,128]{2,1,0:T(8,128)(2,1)S(1)}, u32[]{:S(2)}, u32[]{:S(2)}) async-start(bf16[32,64,128]{2,1,0:T(8,128)(2,1)} %bitcast.151), calls=%async_computation.3 | async-start | bytes 1048576 | tf_op jit(solution)/shard_map/all_to_all | solution.py:835
  513.3 11.8 %all-to-all-done.1 = bf16[32,64,128]{2,1,0:T(8,128)(2,1)S(1)} async-done(((bf16[32,64,128]{2,1,0:T(8,128)(2,1)}), bf16[32,64,128]{2,1,0:T(8,128)(2,1)S(1)}, u32[]{:S(2)}, u32[]{:S(2)}) %all-to-all-start.1) | async-done | bytes 524320 | tf_op jit(solution)/shard_map/all_to_all | solution.py:835
  525.9 4.0 all-to-all-start.2
  544.8 4.3 collective-permute-done.108.refs_3_
  549.1 3.8 collective-permute-done.107.refs_2_
  566.3 4.9 shard_map.281
  (512 shorter events, 289.9 us)
Async XLA Ops:
  7.2 86.9 %all-gather.4.cloned.1.call-start = ((), (), s32[]{:S(2)}) async-start(), calls=%async_computation.5 | async-start | bytes 7028736 | tf_op jit(solution)/shard_map/all_gather | solution.py:920
  26.6 31.5 %collective-permute-start.3 = (bf16[160,2048]{1,0:T(8,128)(2,1)S(1)}, bf16[160,2048]{1,0:T(8,128)(2,1)}, u32[]{:S(2)}, u32[]{:S(2)}) collective-permute-start(bf16[160,2048]{1,0:T(8,128)(2,1)S(1)} %bitcast_multiply_fusion.base_ref), channel_id=1, source_target_pairs={{0,65},{1,64},{64,1},{65,0},{2,67},{3,66},{66,3},{67,2},{4,69},{5,... | collective-permute-start | bytes 1966088 | tf_op jit(solution)/shard_map/ppermute | solution.py:27
  26.7 31.5 %collective-permute-start.2 = (bf16[160,2048]{1,0:T(8,128)(2,1)S(1)}, bf16[160,2048]{1,0:T(8,128)(2,1)S(1)}, u32[]{:S(2)}, u32[]{:S(2)}) collective-permute-start(bf16[160,2048]{1,0:T(8,128)(2,1)S(1)} %bitcast_multiply_fusion.base_ref), channel_id=1, source_target_pairs={{0,64},{1,65},{64,0},{65,1},{2,66},{3,67},{66,2},{67,3},{4,68},{5,... | collective-permute-start | bytes 1966088 | tf_op jit(solution)/shard_map/ppermute | solution.py:27
  26.8 20.5 %all-to-all-start = ((bf16[16,64,512]{2,1,0:T(8,128)(2,1)}), bf16[16,64,512]{2,1,0:T(8,128)(2,1)S(1)}, u32[]{:S(2)}, u32[]{:S(2)}) async-start(bf16[16,64,512]{2,1,0:T(8,128)(2,1)} %broadcast_in_dim.36), calls=%async_computation | async-start | bytes 2097152 | tf_op jit(solution)/shard_map/all_to_all | solution.py:909
  35.0 150.1 %all-gather.6.cloned.1.call-start = ((), (), s32[]{:S(2)}) async-start(), calls=%async_computation.6 | async-start | bytes 19464192 | tf_op jit(solution)/shard_map/all_gather | solution.py:928
  58.2 182.8 %all-gather.8.cloned.1.call-start = ((), (), s32[]{:S(2)}) async-start(), calls=%async_computation.7 | async-start | bytes 5406720 | tf_op jit(solution)/shard_map/all_gather | solution.py:929
  62.0 294.2 %reduce-scatter.3.cloned.1.call-start = ((), (), s32[]{:S(2)}) async-start(), calls=%async_computation.8 | async-start | bytes 5406720 | tf_op jit(solution)/shard_map/reduce_scatter | solution.py:1021
  78.7 25.2 %collective-permute-start.17 = (bf16[80,2048]{1,0:T(8,128)(2,1)}, bf16[80,2048]{1,0:T(8,128)(2,1)}, u32[]{:S(2)}, u32[]{:S(2)}) collective-permute-start(bf16[80,2048]{1,0:T(8,128)(2,1)} %slice.182), channel_id=1, source_target_pairs={{0,64},{1,65},{64,0},{65,1},{2,66},{3,67},{66,2},{67,3},{4,68},{5,... | collective-permute-start | bytes 983048 | tf_op jit(solution)/shard_map/ppermute | solution.py:27
  79.8 24.1 %collective-permute-start.18 = (bf16[80,2048]{1,0:T(8,128)(2,1)}, bf16[80,2048]{1,0:T(8,128)(2,1)}, u32[]{:S(2)}, u32[]{:S(2)}) collective-permute-start(bf16[80,2048]{1,0:T(8,128)(2,1)} %slice.183), channel_id=1, source_target_pairs={{0,65},{1,64},{64,1},{65,0},{2,67},{3,66},{66,3},{67,2},{4,69},{5,... | collective-permute-start | bytes 983048 | tf_op jit(solution)/shard_map/ppermute | solution.py:27
  108.9 22.0 %collective-permute-start.25 = (bf16[320,2048]{1,0:T(8,128)(2,1)S(1)}, bf16[320,2048]{1,0:T(8,128)(2,1)S(1)}, u32[]{:S(2)}, u32[]{:S(2)}) collective-permute-start(bf16[320,2048]{1,0:T(8,128)(2,1)S(1)} %get-tuple-element.294), channel_id=1, source_target_pairs={{0,32},{32,0},{1,33},{33,1},{2,34},{34,2},{3,35},{35,3},{4,36},{36... | collective-permute-start | bytes 3932168 | tf_op jit(solution)/shard_map/ppermute | solution.py:27
  112.7 19.9 %collective-permute-start.24 = (bf16[320,2048]{1,0:T(8,128)(2,1)S(1)}, bf16[320,2048]{1,0:T(8,128)(2,1)S(1)}, u32[]{:S(2)}, u32[]{:S(2)}) collective-permute-start(bf16[320,2048]{1,0:T(8,128)(2,1)S(1)} %get-tuple-element.283), channel_id=1, source_target_pairs={{0,32},{32,0},{1,33},{33,1},{2,34},{34,2},{3,35},{35,3},{4,36},{36... | collective-permute-start | bytes 3932168 | tf_op jit(solution)/shard_map/ppermute | solution.py:27
  144.3 15.7 %collective-permute-start.32 = (bf16[160,2048]{1,0:T(8,128)(2,1)}, bf16[160,2048]{1,0:T(8,128)(2,1)S(1)}, u32[]{:S(2)}, u32[]{:S(2)}) collective-permute-start(bf16[160,2048]{1,0:T(8,128)(2,1)} %get-tuple-element.167.pre_ref), channel_id=1, source_target_pairs={{0,65},{1,64},{64,1},{65,0},{2,67},{3,66},{66,3},{67,2},{4,69},{5,... | collective-permute-start | bytes 1966088 | tf_op jit(solution)/shard_map/ppermute | solution.py:27
  144.3 15.7 %collective-permute-start.31 = (bf16[160,2048]{1,0:T(8,128)(2,1)}, bf16[160,2048]{1,0:T(8,128)(2,1)S(1)}, u32[]{:S(2)}, u32[]{:S(2)}) collective-permute-start(bf16[160,2048]{1,0:T(8,128)(2,1)} %get-tuple-element.167.pre_ref), channel_id=1, source_target_pairs={{0,64},{1,65},{64,0},{65,1},{2,66},{3,67},{66,2},{67,3},{4,68},{5,... | collective-permute-start | bytes 1966088 | tf_op jit(solution)/shard_map/ppermute | solution.py:27
  184.9 29.8 %collective-permute-start.41 = (bf16[160,1024]{1,0:T(8,128)(2,1)S(1)}, bf16[160,1024]{1,0:T(8,128)(2,1)S(1)}, u32[]{:S(2)}, u32[]{:S(2)}) collective-permute-start(bf16[160,1024]{1,0:T(8,128)(2,1)S(1)} %pad_maximum_fusion.9), channel_id=1, source_target_pairs={{0,65},{1,64},{64,1},{65,0},{2,67},{3,66},{66,3},{67,2},{4,69},{5,... | collective-permute-start | bytes 983048 | tf_op jit(solution)/shard_map/ppermute | solution.py:27
  185.0 29.7 %collective-permute-start.40 = (bf16[160,1024]{1,0:T(8,128)(2,1)S(1)}, bf16[160,1024]{1,0:T(8,128)(2,1)S(1)}, u32[]{:S(2)}, u32[]{:S(2)}) collective-permute-start(bf16[160,1024]{1,0:T(8,128)(2,1)S(1)} %pad_maximum_fusion.9), channel_id=1, source_target_pairs={{0,64},{1,65},{64,0},{65,1},{2,66},{3,67},{66,2},{67,3},{4,68},{5,... | collective-permute-start | bytes 983048 | tf_op jit(solution)/shard_map/ppermute | solution.py:27
  214.8 15.0 %collective-permute-start.45 = (bf16[80,1024]{1,0:T(8,128)(2,1)S(1)}, bf16[80,1024]{1,0:T(8,128)(2,1)S(1)}, u32[]{:S(2)}, u32[]{:S(2)}) collective-permute-start(bf16[80,1024]{1,0:T(8,128)(2,1)S(1)} %slice.188), channel_id=1, source_target_pairs={{0,64},{1,65},{64,0},{65,1},{2,66},{3,67},{66,2},{67,3},{4,68},{5,... | collective-permute-start | bytes 491528 | tf_op jit(solution)/shard_map/ppermute | solution.py:27
  272.4 209.9 %reduce-scatter.5.cloned.1.call-start = ((), (), s32[]{:S(2)}) async-start(), calls=%async_computation.9 | async-start | bytes 19464192 | tf_op jit(solution)/shard_map/reduce_scatter | solution.py:1041
  273.4 19.0 %collective-permute-start.58 = (bf16[2,160,1024]{2,1,0:T(8,128)(2,1)S(1)}, bf16[2,160,1024]{2,1,0:T(8,128)(2,1)}, u32[]{:S(2)}, u32[]{:S(2)}) collective-permute-start(bf16[2,160,1024]{2,1,0:T(8,128)(2,1)S(1)} %copy-done.58), channel_id=1, source_target_pairs={{0,32},{32,0},{1,33},{33,1},{2,34},{34,2},{3,35},{35,3},{4,36},{36... | collective-permute-start | bytes 1966088 | tf_op jit(solution)/shard_map/ppermute | solution.py:27
  297.4 22.0 %collective-permute-start.60 = (bf16[80,1024]{1,0:T(8,128)(2,1)}, bf16[80,1024]{1,0:T(8,128)(2,1)}, u32[]{:S(2)}, u32[]{:S(2)}) collective-permute-start(bf16[80,1024]{1,0:T(8,128)(2,1)} %get-tuple-element.298), channel_id=1, source_target_pairs={{0,65},{1,64},{64,1},{65,0},{2,67},{3,66},{66,3},{67,2},{4,69},{5,... | collective-permute-start | bytes 491528 | tf_op jit(solution)/shard_map/ppermute | solution.py:27
  297.6 21.8 %collective-permute-start.59 = (bf16[80,1024]{1,0:T(8,128)(2,1)}, bf16[80,1024]{1,0:T(8,128)(2,1)}, u32[]{:S(2)}, u32[]{:S(2)}) collective-permute-start(bf16[80,1024]{1,0:T(8,128)(2,1)} %get-tuple-element.299), channel_id=1, source_target_pairs={{0,64},{1,65},{64,0},{65,1},{2,66},{3,67},{66,2},{67,3},{4,68},{5,... | collective-permute-start | bytes 491528 | tf_op jit(solution)/shard_map/ppermute | solution.py:27
  320.5 35.0 %collective-permute-start.61 = (bf16[160,1024]{1,0:T(8,128)(2,1)S(1)}, bf16[160,1024]{1,0:T(8,128)(2,1)S(1)}, u32[]{:S(2)}, u32[]{:S(2)}) collective-permute-start(bf16[160,1024]{1,0:T(8,128)(2,1)S(1)} %pad_maximum_fusion.10), channel_id=1, source_target_pairs={{0,64},{1,65},{64,0},{65,1},{2,66},{3,67},{66,2},{67,3},{4,68},{5,... | collective-permute-start | bytes 983048 | tf_op jit(solution)/shard_map/ppermute | solution.py:27
  322.9 33.2 %collective-permute-start.62 = (bf16[160,1024]{1,0:T(8,128)(2,1)S(1)}, bf16[160,1024]{1,0:T(8,128)(2,1)}, u32[]{:S(2)}, u32[]{:S(2)}) collective-permute-start(bf16[160,1024]{1,0:T(8,128)(2,1)S(1)} %pad_maximum_fusion.11), channel_id=1, source_target_pairs={{0,65},{1,64},{64,1},{65,0},{2,67},{3,66},{66,3},{67,2},{4,69},{5,... | collective-permute-start | bytes 983048 | tf_op jit(solution)/shard_map/ppermute | solution.py:27
  376.1 16.3 %collective-permute-start.72 = (bf16[160,2048]{1,0:T(8,128)(2,1)S(1)}, bf16[160,2048]{1,0:T(8,128)(2,1)S(1)}, u32[]{:S(2)}, u32[]{:S(2)}) collective-permute-start(bf16[160,2048]{1,0:T(8,128)(2,1)S(1)} %pad_maximum_fusion.7), channel_id=1, source_target_pairs={{0,65},{1,64},{64,1},{65,0},{2,67},{3,66},{66,3},{67,2},{4,69},{5,... | collective-permute-start | bytes 1966088 | tf_op jit(solution)/shard_map/ppermute | solution.py:27
  482.3 57.1 %collective-permute-start.104 = (bf16[64,4608]{1,0:T(8,128)(2,1)}, bf16[64,4608]{1,0:T(8,128)(2,1)}, u32[]{:S(2)}, u32[]{:S(2)}) collective-permute-start(bf16[64,4608]{1,0:T(8,128)(2,1)} %reduce-scatter.5.cloned.1.call-done.refs_0_), channel_id=1, source_target_pairs={{1,64},{32,97},{65,0},{96,33},{3,66},{34,99},{67,2},{98,35},{5,68}... | collective-permute-start | bytes 1769480 | tf_op jit(solution)/shard_map/ppermute | solution.py:1110
  486.1 54.0 %collective-permute-start.103 = (bf16[64,4608]{1,0:T(8,128)(2,1)}, bf16[64,4608]{1,0:T(8,128)(2,1)}, u32[]{:S(2)}, u32[]{:S(2)}) collective-permute-start(bf16[64,4608]{1,0:T(8,128)(2,1)} %reduce-scatter.5.cloned.1.call-done.refs_0_), channel_id=1, source_target_pairs={{1,0},{32,33},{65,64},{96,97},{3,2},{34,35},{67,66},{98,99},{5,4},... | collective-permute-start | bytes 1769480 | tf_op jit(solution)/shard_map/ppermute | solution.py:1110
  495.8 44.4 %collective-permute-start.102 = (bf16[64,4608]{1,0:T(8,128)(2,1)}, bf16[64,4608]{1,0:T(8,128)(2,1)}, u32[]{:S(2)}, u32[]{:S(2)}) collective-permute-start(bf16[64,4608]{1,0:T(8,128)(2,1)} %reduce-scatter.5.cloned.1.call-done.refs_0_), channel_id=1, source_target_pairs={{0,64},{33,97},{64,0},{97,33},{2,66},{35,99},{66,2},{99,35},{4,68}... | collective-permute-start | bytes 1769480 | tf_op jit(solution)/shard_map/ppermute | solution.py:1110
  499.0 26.1 %all-to-all-start.1 = ((bf16[32,64,128]{2,1,0:T(8,128)(2,1)}), bf16[32,64,128]{2,1,0:T(8,128)(2,1)S(1)}, u32[]{:S(2)}, u32[]{:S(2)}) async-start(bf16[32,64,128]{2,1,0:T(8,128)(2,1)} %bitcast.151), calls=%async_computation.3 | async-start | bytes 1048576 | tf_op jit(solution)/shard_map/all_to_all | solution.py:835
  525.9 29.7 %all-to-all-start.2 = ((bf16[32,16,1664]{2,1,0:T(8,128)(2,1)}), bf16[32,16,1664]{2,1,0:T(8,128)(2,1)S(1)}, u32[]{:S(2)}, u32[]{:S(2)}) async-start(bf16[32,16,1664]{2,1,0:T(8,128)(2,1)} %bitcast.65), calls=%async_computation.4 | async-start | bytes 3407872 | tf_op jit(solution)/shard_map/all_to_all | solution.py:835
  533.2 15.9 %collective-permute-start.108 = (bf16[16,5120]{1,0:T(8,128)(2,1)S(1)}, bf16[16,5120]{1,0:T(8,128)(2,1)S(1)}, u32[]{:S(2)}, u32[]{:S(2)}) collective-permute-start(bf16[16,5120]{1,0:T(8,128)(2,1)S(1)} %copy-done.19), channel_id=1, source_target_pairs={{1,64},{32,97},{65,0},{96,33},{3,66},{34,99},{67,2},{98,35},{5,68}... | collective-permute-start | bytes 491528 | tf_op jit(solution)/shard_map/ppermute | solution.py:1110
  536.5 16.4 %collective-permute-start.107 = (bf16[16,5120]{1,0:T(8,128)(2,1)S(1)}, bf16[16,5120]{1,0:T(8,128)(2,1)S(1)}, u32[]{:S(2)}, u32[]{:S(2)}) collective-permute-start(bf16[16,5120]{1,0:T(8,128)(2,1)S(1)} %copy-done.19), channel_id=1, source_target_pairs={{1,0},{32,33},{65,64},{96,97},{3,2},{34,35},{67,66},{98,99},{5,4},... | collective-permute-start | bytes 491528 | tf_op jit(solution)/shard_map/ppermute | solution.py:1110
  540.1 19.1 %collective-permute-start.99 = (bf16[2,64,128]{2,1,0:T(8,128)(2,1)S(1)}, bf16[2,64,128]{2,1,0:T(8,128)(2,1)S(1)}, u32[]{:S(2)}, u32[]{:S(2)}) collective-permute-start(bf16[2,64,128]{2,1,0:T(8,128)(2,1)S(1)} %pad_maximum_fusion.15), channel_id=1, source_target_pairs={{0,64},{1,65},{64,0},{65,1},{2,66},{3,67},{66,2},{67,3},{4,68},{5,... | collective-permute-start | bytes 98312 | tf_op jit(solution)/shard_map/ppermute | solution.py:27
  543.5 22.8 %collective-permute-start.105 = (bf16[4,64,4608]{2,1,0:T(8,128)(2,1)}, bf16[4,64,4608]{2,1,0:T(8,128)(2,1)}, u32[]{:S(2)}, u32[]{:S(2)}) collective-permute-start(bf16[4,64,4608]{2,1,0:T(8,128)(2,1)} %pad_maximum_fusion.1), channel_id=1, source_target_pairs={{0,32},{33,1},{64,96},{97,65},{2,34},{35,3},{66,98},{99,67},{4,36}... | collective-permute-start | bytes 7077896 | tf_op jit(solution)/shard_map/ppermute | solution.py:1118
  (146 other events, 1577.8 us)
Sparse Core Ops, SparseCore 0:
  24.0 60.9 all-gather.3
  87.3 76.5 all-gather.5
  166.7 46.8 all-gather.7
  272.5 81.5 reduce-scatter.2
  358.4 121.6 reduce-scatter.4

commit v3 on v2

--- a/solution.py
+++ b/solution.py
@@ -53,23 +53,20 @@
     return jnp.where(first, mine, other), jnp.where(first, other, mine)
 
 
-def beside_rows(value):
-    return (
-        value,
-        over_y(value, 1),
-        over_core(value),
-        lax.ppermute(value, GROUP, [(i, i ^ 6) for i in range(8)]),
-    )
-
-
-def from_rows(parts):
-    own, low, other, both = parts
-    return (
-        own,
-        over_y(low, 1),
-        over_core(other),
-        lax.ppermute(both, GROUP, [(i, i ^ 6) for i in range(8)]),
-    )
+def around_y(value):
+    return value, over_y(value, 1), over_y(value, 2), over_y(value, 3)
+
+
+def for_me(parts):
+    own, near, across, far = parts
+    return own, over_y(near, 1), over_y(across, 2), over_y(far, 3)
+
+
+HOME = [(i, ((i & 1) << 2) | (((i >> 2) & 1) << 1) | ((i >> 1) & 1)) for i in range(8)]
+
+
+def sent_home(value):
+    return lax.ppermute(value, GROUP, HOME)
 
 
 def beside_y(value):
@@ -81,24 +78,20 @@
     return over_y(far[:half], 1), over_y(near[half:], 3)
 
 
-def sent_home(kept_here, got, same):
-    return jnp.where(same, kept_here, got), jnp.where(same, got, kept_here)
-
-
-def half_way(other):
-    half = other.shape[1] // 2
-    return over_y(other[0, :half], 1), over_y(other[0, half:], 3)
-
-
-def last_way(own, other, from_near, from_far):
-    half = own.shape[1] // 2
+def half_way(across):
+    half = across.shape[0] // 2
+    return over_y(across[:half], 1), over_y(across[half:], 3)
+
+
+def last_way(own, near, far, from_near, from_far):
+    half = own.shape[0] // 2
     near = jnp.concatenate(
-        [own[1, :half], (own[1, half:].astype(F32) + from_far.astype(F32)).astype(BF16)]
+        [near[:half], (near[half:].astype(F32) + from_far.astype(F32)).astype(BF16)]
     )
     far = jnp.concatenate(
-        [(other[1, :half].astype(F32) + from_near.astype(F32)).astype(BF16), other[1, half:]]
-    )
-    return own[0], over_y(near, 1), over_y(far, 3)
+        [(far[:half].astype(F32) + from_near.astype(F32)).astype(BF16), far[half:]]
+    )
+    return own, over_y(near, 1), over_y(far, 3)
 
 
 def gelu_parts(value):
@@ -195,8 +188,8 @@
     image_ref[5 * strip : 6 * strip, :] = empty
 
 
-def window_moved(stack_ref, image_ref, start):
-    @pl.loop(0, 6)
+def window_moved(stack_ref, image_ref, start, rows):
+    @pl.loop(0, rows)
     def _(r):
         at = pl.multiple_of(r * PITCH, 16)
         value = image_ref[pl.ds(pl.multiple_of(start + at, 16), PITCH), :]
@@ -204,8 +197,8 @@
 
 
 def dilated_kernel(
-    count_ref, at_ref, p0, p1, p2, p3, sums_ref, gain_ref, bias_ref, inside_ref, mine_ref, w_ref,
-    out_ref, out_sums, image_out, image_ref, stack_ref, total_ref,
+    count_ref, at_ref, value_ref, sums_ref, gain_ref, bias_ref, inside_ref, w_ref,
+    out_ref, out_sums, image_out, value_out, image_ref, stack_ref, total_ref,
 ):
     tap = pl.program_id(0)
     strip = 2 * PITCH
@@ -214,18 +207,20 @@
     def _():
         clear_image(image_ref)
         mean, inverse = moments(sums_ref, count_ref[0])
-        for k, piece in enumerate((p0, p1, p2, p3)):
+        for k in range(4):
             start = pl.multiple_of(at_ref[k], 16)
-            normed = gain_ref[...] * ((piece[...].astype(F32) - mean) * inverse) + bias_ref[...]
-            act = gelu(normed) * inside_ref[pl.ds(start, strip), :]
-            image_ref[pl.ds(pl.multiple_of(start + strip, 16), strip), :] = act.astype(BF16)
-        window_moved(stack_ref, image_ref, at_ref[0])
-        image_out[...] = image_ref[strip : 5 * strip, :]
+            value = value_ref[k * strip : (k + 1) * strip, :]
+            value_out[pl.ds(start, strip), :] = value
+            normed = gain_ref[...] * ((value.astype(F32) - mean) * inverse) + bias_ref[...]
+            act = (gelu(normed) * inside_ref[pl.ds(start, strip), :]).astype(BF16)
+            image_ref[pl.ds(pl.multiple_of(start + strip, 16), strip), :] = act
+            image_out[pl.ds(start, strip), :] = act
+        window_moved(stack_ref, image_ref, 0, 12)
         total_ref[...] = jnp.zeros_like(total_ref)
 
     start = pl.multiple_of((tap // 3) * strip, 16)
     total_ref[...] += jnp.dot(
-        stack_ref[tap % 3, pl.ds(start, strip), :], w_ref[...], preferred_element_type=F32
+        stack_ref[tap % 3, pl.ds(start, 4 * strip), :], w_ref[...], preferred_element_type=F32
     )
 
     @pl.when(tap == 8)
@@ -233,27 +228,28 @@
         out = total_ref[...].astype(BF16)
         out_ref[...] = out
         out = out.astype(F32)
-        value = out * mine_ref[...]
+        value = out * inside_ref[...]
         store_sums(out_sums, value, value * out)
 
 
-def dilated_forward(count, at, pieces, sums, gain, bias, inside, mine, weights, first_block):
-    strip, deep = pieces[0].shape
-    operands = (*pieces, sums, gain, bias, inside, mine)
+def dilated_forward(count, at, value, sums, gain, bias, inside, weights, first_block):
+    rows, deep = value.shape
+    strip = 2 * PITCH
+    operands = (value, sums, gain, bias, inside)
     return call(
         dilated_kernel,
         (9,),
         [SCALARS, SCALARS]
         + [whole(a.shape) for a in operands]
         + [pl.BlockSpec((deep, 512), lambda t: (0, first_block + t))],
-        [kept((strip, 512)), kept((2, 512)), kept((4 * strip, deep))],
-        [((strip, 512), BF16), ((2, 512), F32), ((4 * strip, deep), BF16)],
+        [kept((rows, 512)), kept((2, 512)), kept((rows, deep)), kept((rows, deep))],
+        [((rows, 512), BF16), ((2, 512), F32), ((rows, deep), BF16), ((rows, deep), BF16)],
         [
-            pltpu.VMEM((6 * strip, deep), BF16),
-            pltpu.VMEM((3, 3 * strip, deep), BF16),
-            pltpu.VMEM((strip, 512), F32),
+            pltpu.VMEM((rows + 2 * strip, deep), BF16),
+            pltpu.VMEM((3, rows + 2 * strip, deep), BF16),
+            pltpu.VMEM((rows, 512), F32),
         ],
-        18 * strip * deep * 512,
+        18 * rows * deep * 512,
         count,
         at,
         *operands,
@@ -298,17 +294,17 @@
 
 
 def head_kernel(
-    count_ref, at_ref, keep_ref, got_ref, base_keep, base_got, sums_ref, gain_ref, bias_ref, inside_ref, w_ref,
-    out_ref, out_sums, trunk_ref, slope_ref, steep_ref, stack_ref,
+    count_ref, at_ref, value_ref, base_keep, base_got, sums_ref, gain_ref, bias_ref, inside_ref, w_ref,
+    out_ref, out_sums, trunk_ref, slope_ref, steep_ref, base_out, stack_ref,
 ):
     tap = pl.program_id(0)
-    strip = 2 * PITCH
+    rows_all = out_ref.shape[0]
 
     @pl.when(tap == 0)
     def _():
         clear_ends(stack_ref, PITCH)
         mean, inverse = moments(sums_ref, count_ref[0])
-        for k, (values, bases) in enumerate(((keep_ref, base_keep), (got_ref, base_got))):
+        for k, bases in enumerate((base_keep, base_got)):
 
             @pl.loop(0, 4)
             def _(r):
@@ -319,12 +315,10 @@
                 inside = inside_ref[rows, :]
                 for c in range(4):
                     columns = slice(c * 512, (c + 1) * 512)
-                    centred = (values[source, columns].astype(F32) - mean[:, columns]) * inverse[:, columns]
-                    joined = (
-                        gain_ref[:, columns] * centred
-                        + bias_ref[:, columns]
-                        + bases[source, columns].astype(F32)
-                    )
+                    centred = (value_ref[rows, columns].astype(F32) - mean[:, columns]) * inverse[:, columns]
+                    base = bases[source, columns]
+                    base_out[rows, columns] = base
+                    joined = gain_ref[:, columns] * centred + bias_ref[:, columns] + base.astype(F32)
                     level, bend, squared = gelu_parts(joined)
                     trunk = joined * level * inside
                     slope = (
@@ -339,7 +333,7 @@
 
     start = pl.multiple_of((tap // 3) * PITCH, 16)
     out_ref[...] += jnp.dot(
-        stack_ref[tap % 3, pl.ds(start, 4 * strip), :], w_ref[...], preferred_element_type=F32
+        stack_ref[tap % 3, pl.ds(start, rows_all), :], w_ref[...], preferred_element_type=F32
     )
 
     @pl.when(tap == 8)
@@ -348,38 +342,30 @@
         store_sums(out_sums, value, value * out_ref[...])
 
 
-def head_forward(count, at, keep, got, base_keep, base_got, sums, gain, bias, inside, weights):
-    rows = inside.shape[0]
-    deep = keep.shape[1]
+def head_forward(count, at, value, base_keep, base_got, sums, gain, bias, inside, weights):
+    rows, deep = value.shape
+    operands = (value, base_keep, base_got, sums, gain, bias, inside)
     return call(
         head_kernel,
         (9,),
         [SCALARS, SCALARS]
-        + [whole(keep.shape)] * 4
-        + [whole(a.shape) for a in (sums, gain, bias, inside)]
+        + [whole(a.shape) for a in operands]
         + [pl.BlockSpec((deep, 512), lambda t: (0, t))],
-        [whole((rows, 512)), kept((2, 512))] + [whole((rows, deep))] * 3,
-        [((rows, 512), F32), ((2, 512), F32)] + [((rows, deep), BF16)] * 3,
+        [whole((rows, 512)), kept((2, 512))] + [whole((rows, deep))] * 4,
+        [((rows, 512), F32), ((2, 512), F32)] + [((rows, deep), BF16)] * 4,
         [pltpu.VMEM((3, rows + 2 * PITCH, deep), BF16)],
         18 * rows * deep * 512,
         count,
         at,
-        keep,
-        got,
-        base_keep,
-        base_got,
-        sums,
-        gain,
-        bias,
-        inside,
+        *operands,
         weights,
     )
 
 
 def message_kernel(
-    count_ref, at_ref, y_ref, value_ref, sums_ref, gain_ref, bias_ref, inside_ref, w_ref, cot_keep, cot_got,
-    task_ref, streams_keep, streams_give, d_message_ref, d_logit_ref, d_norm_ref, out_sums,
-    stack_ref, total_ref, gate_ref,
+    count_ref, at_ref, ring_ref, y_ref, value_ref, sums_ref, gain_ref, bias_ref, inside_ref, w_ref, cot_keep, cot_got,
+    task_ref, s0, s1, s2, s3, d_message_ref, d_logit_ref, d_norm_ref, out_sums,
+    stack_ref, total_ref, gate_ref, streams_ref,
 ):
     rows_all, deep = value_ref.shape
     mean, inverse = moments(sums_ref, count_ref[0])
@@ -432,15 +418,17 @@
             )
             task = task_ref[rows, :]
             gated = (gate * message).astype(BF16)
-            slot = pl.ds(pl.multiple_of((r % 2) * PITCH, 16), PITCH)
-            streams_ref = (streams_keep, streams_give)[k]
-            streams_ref[r // 2, slot, :deep] = jnp.where(number == 0, task, gated)
-            streams_ref[r // 2, slot, deep:] = jnp.where(number == 1, task, gated)
+            streams_ref[rows, :deep] = jnp.where(number == 0, task, gated)
+            streams_ref[rows, deep:] = jnp.where(number == 1, task, gated)
             d_logit_ref[rows, :] = (receive * message * gate * (1.0 - gate)).astype(BF16)
             d_message = receive * gate
             d_message_ref[rows, :] = d_message.astype(BF16)
             store_moved(stack_ref, pl.multiple_of(at + PITCH, 16), d_message, 1)
             total_ref[rows, :] = direct
+
+    for k, stream_ref in enumerate((s0, s1, s2, s3)):
+        first = pl.multiple_of(ring_ref[k], 16)
+        stream_ref[...] = streams_ref[pl.ds(first, 2 * PITCH), :]
 
     total_ref[...] += times_turned(d_logit_ref[...], w_ref[:, 9 * 512 : 10 * 512])
 
@@ -463,18 +451,17 @@
         add_sums(out_sums, upstream * centred, upstream)
 
 
-def message_stage(count, at, y, value, sums, gain, bias, inside, weights, cot_keep, cot_got):
+def message_stage(count, at, ring, y, value, sums, gain, bias, inside, weights, cot_keep, cot_got):
     rows, deep = value.shape
     return call(
         message_kernel,
         (1,),
-        [SCALARS] * 3
+        [SCALARS] * 4
         + [whole(a.shape) for a in (value, sums, gain, bias, inside, weights)]
         + [whole((rows // 2, 2 * deep))] * 2,
         [
             kept((rows, deep)),
-            kept((2, rows // 4, 2 * deep)),
-            kept((2, rows // 4, 2 * deep)),
+            *[kept((rows // 4, 2 * deep))] * 4,
             kept((rows, deep)),
             kept((rows, deep)),
             kept((rows, deep)),
@@ -482,8 +469,7 @@
         ],
         [
             ((rows, deep), BF16),
-            ((2, rows // 4, 2 * deep), BF16),
-            ((2, rows // 4, 2 * deep), BF16),
+            *[((rows // 4, 2 * deep), BF16)] * 4,
             ((rows, deep), BF16),
             ((rows, deep), BF16),
             ((rows, deep), F32),
@@ -493,10 +479,12 @@
             pltpu.VMEM((3, rows + 2 * PITCH, deep), BF16),
             pltpu.VMEM((rows, deep), F32),
             pltpu.VMEM((rows, deep), F32),
+            pltpu.VMEM((rows, 2 * deep), BF16),
         ],
         40 * rows * deep * 512,
         count,
         at,
+        ring,
         y,
         value,
         sums,
@@ -558,7 +546,7 @@
 
 
 def trunk_kernel(
-    at_ref, g_ref, slope_ref, steep_ref, w_ref, keep_ref, give_ref, sums_ref, stack_ref, turned_ref, total_ref, line_ref
+    at_ref, g_ref, slope_ref, steep_ref, w_ref, o0, o1, o2, o3, sums_ref, stack_ref, turned_ref, total_ref, line_ref
 ):
     tap = pl.program_id(0)
     rows = g_ref.shape[0]
@@ -594,8 +582,8 @@
             )
             for k in range(4):
                 start = pl.multiple_of(at_ref[k], 16)
-                out_ref = (keep_ref, give_ref)[k // 2]
-                out_ref[k % 2, :, columns] = line_ref[pl.ds(start, rows // 4), :].astype(BF16)
+                out_ref = (o0, o1, o2, o3)[k]
+                out_ref[:, columns] = line_ref[pl.ds(start, rows // 4), :].astype(BF16)
 
 
 def trunk_back(at, upstream, slope, steep, weights):
@@ -606,8 +594,8 @@
         (9,),
         [SCALARS, whole((rows, wide)), whole((rows, deep)), whole((rows, deep))]
         + [pl.BlockSpec((deep, wide), lambda t: (0, t))],
-        [whole((2, rows // 4, deep))] * 2 + [kept((2, deep))],
-        [((2, rows // 4, deep), BF16)] * 2 + [((2, deep), F32)],
+        [whole((rows // 4, deep))] * 4 + [kept((2, deep))],
+        [((rows // 4, deep), BF16)] * 4 + [((2, deep), F32)],
         [
             pltpu.VMEM((3, rows + 2 * PITCH, wide), BF16),
             pltpu.VMEM((9, wide, rows), BF16),
@@ -640,7 +628,7 @@
             + far_ref[:, columns].astype(F32)
         )
         d_joined = gelu_slope(joined) * d_trunk * inside
-        d_joined_ref[:, columns] = d_joined
+        d_joined_ref[:, columns] = d_joined.astype(BF16)
         shift = (back_ref[1:2, columns] + centred * back_ref[0:1, columns]) / count
         d_pre_ref[:, columns] = (
             inside * gain * inverse[:, columns] * (d_joined - shift)
@@ -673,7 +661,7 @@
         + [whole((narrow, deep))]
         + [whole(a.shape) for a in lower],
         [kept((rows, deep))] + [kept((rows, 512))] * 4 + [kept((rows, narrow)), kept((2, narrow))],
-        [((rows, deep), F32)]
+        [((rows, deep), BF16)]
         + [((rows, 512), BF16)] * 4
         + [((rows, narrow), BF16), ((2, narrow), F32)],
         [pltpu.VMEM((rows, deep), BF16)],
@@ -688,32 +676,33 @@
 
 
 def dilated_back_kernel(
-    count_ref, at_ref, u0, u1, u2, u3, p0, p1, p2, p3, sums_ref, back_ref, gain_ref, inside_ref,
-    w_ref, low_ref, low_sums, low_gain, low_bias, mine_ref,
+    count_ref, at_ref, u0, u1, u2, u3, value_ref, sums_ref, back_ref, gain_ref, inside_ref,
+    w_ref, low_ref, low_sums, low_gain, low_bias,
     d_norm_ref, out_sums, part_ref,
     image_ref, stack_ref, turned_ref, total_ref,
 ):
     tap = pl.program_id(0)
     strip = 2 * PITCH
+    rows = value_ref.shape[0]
     count = count_ref[0]
 
     @pl.when(tap == 0)
     def _():
         clear_image(image_ref)
         mean, inverse = moments(sums_ref, count)
-        for k, (up, value) in enumerate(((u0, p0), (u1, p1), (u2, p2), (u3, p3))):
+        for k, up in enumerate((u0, u1, u2, u3)):
             start = pl.multiple_of(at_ref[k], 16)
-            centred = (value[...].astype(F32) - mean) * inverse
+            centred = (value_ref[pl.ds(start, strip), :].astype(F32) - mean) * inverse
             shift = (back_ref[1:2, :] + centred * back_ref[0:1, :]) / count
             scale = inside_ref[pl.ds(start, strip), :] * (gain_ref[...] * inverse)
             lowered = (scale * (up[...].astype(F32) - shift)).astype(BF16)
             image_ref[pl.ds(pl.multiple_of(start + strip, 16), strip), :] = lowered
-        window_moved(stack_ref, image_ref, at_ref[0])
+        window_moved(stack_ref, image_ref, 0, 12)
         mine = pl.multiple_of(at_ref[0] // strip * 128, 128)
         part_ref[...] = image_ref[strip : 5 * strip, pl.ds(mine, 128)]
         for k in range(9):
             start = (2 - k // 3) * strip
-            turned_ref[k] = stack_ref[2 - k % 3, start : start + strip, :].T
+            turned_ref[k] = stack_ref[2 - k % 3, start : start + rows, :].T
         total_ref[...] = jnp.zeros_like(total_ref)
 
     total_ref[...] += jnp.dot(w_ref[...], turned_ref[tap], preferred_element_type=F32)
@@ -723,18 +712,19 @@
         mean, inverse = moments(low_sums, count)
         centred = (low_ref[...].astype(F32) - mean) * inverse
         slope = gelu_slope(low_gain[...] * centred + low_bias[...])
-        upstream = (slope * total_ref[...].T * mine_ref[...]).astype(BF16)
+        upstream = (slope * total_ref[...].T * inside_ref[...]).astype(BF16)
         d_norm_ref[...] = upstream
         upstream = upstream.astype(F32)
         store_sums(out_sums, upstream * centred, upstream)
 
 
 def dilated_back(
-    count, at, ups, values, sums, back, gain, inside, weights, first_block, low, low_sums, low_gain, low_bias, mine
+    count, at, ups, value, sums, back, gain, inside, weights, first_block, low, low_sums, low_gain, low_bias
 ):
-    strip, wide = ups[0].shape
-    operands = (*ups, *values, sums, back, gain, inside)
-    lower = (low, low_sums, low_gain, low_bias, mine)
+    rows, wide = value.shape
+    strip = 2 * PITCH
+    operands = (*ups, value, sums, back, gain, inside)
+    lower = (low, low_sums, low_gain, low_bias)
     return call(
         dilated_back_kernel,
         (9,),
@@ -742,15 +732,15 @@
         + [whole(a.shape) for a in operands]
         + [pl.BlockSpec((512, wide), lambda t: (0, first_block + t))]
         + [whole(a.shape) for a in lower],
-        [kept((strip, 512)), kept((2, 512)), kept((4 * strip, 128))],
-        [((strip, 512), BF16), ((2, 512), F32), ((4 * strip, 128), BF16)],
+        [kept((rows, 512)), kept((2, 512)), kept((rows, 128))],
+        [((rows, 512), BF16), ((2, 512), F32), ((rows, 128), BF16)],
         [
-            pltpu.VMEM((6 * strip, wide), BF16),
-            pltpu.VMEM((3, 3 * strip, wide), BF16),
-            pltpu.VMEM((9, wide, strip), BF16),
-            pltpu.VMEM((512, strip), F32),
+            pltpu.VMEM((rows + 2 * strip, wide), BF16),
+            pltpu.VMEM((3, rows + 2 * strip, wide), BF16),
+            pltpu.VMEM((9, wide, rows), BF16),
+            pltpu.VMEM((512, rows), F32),
         ],
-        18 * strip * wide * 512,
+        18 * rows * wide * 512,
         count,
         at,
         *operands,
@@ -830,12 +820,15 @@
     return value.reshape(1, rows, PITCH, -1)[:, :, :across]
 
 
-def shares_summed(value, axes, dtype=BF16):
+def shares_sent(value, axes):
     count = lax.axis_size(axes)
-    parts = lax.all_to_all(
+    return lax.all_to_all(
         value.reshape(count, value.shape[0] // count, value.shape[1]), axes, 0, 0
     )
-    return jnp.sum(parts.astype(F32), axis=0).astype(dtype)
+
+
+def parts_summed(parts):
+    return jnp.sum(parts.astype(F32), axis=0).astype(BF16)
 
 
 def shards(
@@ -860,7 +853,7 @@
     plane = lax.axis_index("x") * 4 + lax.axis_index("z")
     y = yhi * 2 + ylo
     strip = ylo * 2 + core
-    across = features.shape[2]
+    width = features.shape[2]
     local = core == yhi
 
     count = jnp.sum(image_size[:, 0].astype(F32) * image_size[:, 1].astype(F32))
@@ -873,7 +866,6 @@
         return valid.astype(F32)[:, None]
 
     length = 2 * PITCH
-    row_at = (jnp.stack([strip, strip ^ 2, strip ^ 1, strip ^ 3]) * length).astype(jnp.int32)
     head_at = (
         jnp.stack(
             [
@@ -885,6 +877,7 @@
         )
         * length
     ).astype(jnp.int32)
+    ring_at = (jnp.stack([y, y ^ 1, y ^ 2, y ^ 3]) * length).astype(jnp.int32)
 
     group = [(i, i ^ 5) for i in range(8) if (i >> 1) & 1 == i & 1]
 
@@ -895,94 +888,94 @@
         return lax.dynamic_index_in_dim(stacked, head, 0, keepdims=False)
 
     planes = 16
+
     deep = features.shape[3]
     same = yhi == core
-    reduce_part = brought(reduce_weight, reduce_weight)
-    copies, y_first, sizes_first, feature_maps, dilated_first, expand_first = hold(
-        jnp.broadcast_to(reduce_part[None], (planes,) + reduce_part.shape),
-        y,
-        image_size,
-        features,
-        dilated_weight,
-        expand_weight,
+    inside = inside_of(image_size, plane * 2 + yhi, strip * 2, 2)
+    base = strips_of(features) * inside.astype(BF16)
+    near, far = beside_y(base)
+    channels = expand_weight.shape[0]
+    wide_trunk = expand_weight.shape[1] + dilated_weight.shape[1]
+    first_weights = jnp.concatenate(
+        [expand_weight, dilated_weight, reduce_weight.reshape(channels, -1)], axis=1
+    )
+    first_part = brought(first_weights, first_weights)
+    reduce_part = first_part[:, wide_trunk:].reshape(reduce_weight.shape)
+    copies, sizes_first = hold(
+        jnp.broadcast_to(reduce_part[None], (planes,) + reduce_part.shape), image_size
     )
     reduce_half = lax.all_to_all(copies, ("x", "z"), 0, 0)
     whole_reduce = jnp.stack(
         in_order(reduce_half, over_core(reduce_half), core), axis=1
     ).reshape(-1, reduce_weight.shape[1])
-    inside = inside_of(sizes_first, plane * 2 + yhi, strip * 2, 2)
-    inside_own = inside_of(sizes_first, plane * 2 + yhi, 0, 8)
+    whole_trunk = lax.all_gather(first_part[:, :wide_trunk], POOL, axis=0, tiled=True)
+    first_tap = expand_weight.shape[1] // 512
     inside_whole = inside_of(sizes_first, plane * 2 + core, 0, 8)
-    base = strips_of(feature_maps) * inside.astype(BF16)
-    near, far = beside_y(base)
-    trunk_weights = jnp.concatenate([expand_first, dilated_first], axis=1)
-    trunk_part = brought(trunk_weights, trunk_weights)
-    whole_trunk = lax.all_gather(trunk_part, POOL, axis=0, tiled=True)
-    first_tap = expand_weight.shape[1] // 512
-    task_weights = jnp.concatenate([message_weight, gate_weight], axis=2)
+
+    def spread(own, near, across_low, across_high, far):
+        mine = jnp.concatenate([own, near])
+        other = jnp.concatenate([across_low, across_high, far])
+        return jnp.where(same, mine, other), over_core(jnp.where(same, other, mine))
+
+    near, far, y_first = hold(near, far, y)
     head_part = brought(of_head(head_weight, y_first), of_head(head_weight, y_first ^ 3))
-    task_part = brought(of_head(task_weights, y_first), of_head(task_weights, y_first ^ 3))
-    whole_reduce, near, far, head_part, task_part, inside, inside_own, inside_whole = hold(
-        whole_reduce, near, far, head_part, task_part, inside, inside_own, inside_whole
+    base_keep, base_got = spread(base, near, *across_y(near, far), far)
+    whole_reduce, base_keep, base_got, inside_whole, head_part = hold(
+        whole_reduce, base_keep, base_got, inside_whole, head_part
     )
     whole_head = lax.all_gather(head_part, POOL, axis=0, tiled=True)
-    whole_task = lax.all_gather(task_part, POOL, axis=0, tiled=True)
-
-    pre_one = jnp.dot(base, whole_reduce, preferred_element_type=F32).astype(BF16)
-    wide_one = pre_one.astype(F32)
-    sums_one = sums_of(wide_one)
-    across_low, across_high = across_y(near, far)
-    sums_one = fold(sums_one, CORE, *LINE)
-    sums_one, ones = hold(sums_one, beside_rows(pre_one))
-    sums_one = fold(sums_one, *PLANE, *RIDGE)
-    pre_two, sums_two, act_one_image = dilated_forward(
+
+    pre_one = jnp.concatenate(
+        [
+            jnp.dot(a, whole_reduce, preferred_element_type=F32).astype(BF16)
+            for a in (base_keep, base_got)
+        ]
+    )
+    sums_one = fold(sums_of(pre_one.astype(F32)), CORE, *LINE, *PLANE)
+    pre_two, sums_two, act_one_image, pre_one_image = dilated_forward(
         count_here,
-        row_at,
-        ones,
+        head_at,
+        pre_one,
         sums_one,
         bottleneck_gain[:1],
         bottleneck_bias[:1],
-        inside_own,
-        inside,
+        inside_whole,
         whole_trunk,
         first_tap,
     )
-    pre_two, sums_two, near, far, across_low, across_high = hold(
-        pre_two, sums_two, near, far, across_low, across_high
-    )
-    base_own = jnp.concatenate([base, near])
-    base_other = jnp.concatenate([across_low, across_high, far])
-    base_keep = jnp.where(same, base_own, base_other)
-    base_got = over_core(jnp.where(same, base_other, base_own))
-    base_image = jnp.concatenate([base_own, over_core(base_own)])
-    sums_two = fold(sums_two, CORE, *LINE, *PLANE)
-    sums_two, base_keep, base_got, base_image = hold(sums_two, base_keep, base_got, base_image)
-    sums_two = fold(sums_two, *RIDGE)
+    sums_two = fold(sums_two, CORE, *LINE)
+    sums_two, y_later, depth_cots, seg_cots = hold(sums_two, y, depth_cotangent, seg_cotangent)
+    task_weights = jnp.concatenate([message_weight, gate_weight], axis=2)
+    task_part = brought(of_head(task_weights, y_later), of_head(task_weights, y_later ^ 3))
+    cots = jnp.concatenate([strips_of(depth_cots), strips_of(seg_cots)], axis=1)
+    near, far = beside_y(cots)
+    sums_two = fold(sums_two, *PLANE)
     act_two, pre_three, sums_three = expand_forward(
-        count_here, pre_two, sums_two, bottleneck_gain[1:], bottleneck_bias[1:], inside, whole_trunk
-    )
-    near, far = beside_y(pre_three)
-    sums_three = fold(sums_three, CORE, *LINE)
-    sums_three, near, far = hold(sums_three, near, far)
+        count_here,
+        pre_two,
+        sums_two,
+        bottleneck_gain[1:],
+        bottleneck_bias[1:],
+        inside_whole,
+        whole_trunk,
+    )
+    sums_three, near, far, task_part = hold(fold(sums_three, CORE), near, far, task_part)
+    whole_task = lax.all_gather(task_part, POOL, axis=0, tiled=True)
     across_low, across_high = across_y(near, far)
-    sums_three = fold(sums_three, *PLANE)
+    sums_three = fold(sums_three, *LINE)
     sums_three, near, far, across_low, across_high = hold(
         sums_three, near, far, across_low, across_high
     )
-    pre_own = jnp.concatenate([pre_three, near])
-    pre_other = jnp.concatenate([across_low, across_high, far])
-    pre_keep = jnp.where(same, pre_own, pre_other)
-    pre_got = over_core(jnp.where(same, pre_other, pre_own))
-    sums_three = fold(sums_three, *RIDGE)
-    sums_three, depth_cots, seg_cots = hold(sums_three, depth_cotangent, seg_cotangent)
+    cots_keep, cots_got = spread(cots, near, across_low, across_high, far)
+    sums_three = fold(sums_three, *PLANE)
+    sums_three, cots_keep, cots_got = hold(sums_three, cots_keep, cots_got)
 
     gain_here, bias_here = of_head(head_gain, y)[None], of_head(head_bias, y)[None]
     wide_gain, wide_bias = expand_gain[None], expand_bias[None]
-    pre_head, sums_head, trunk, slope, steep = head_forward(
+    pre_head, sums_head, trunk, slope, steep, base_image = head_forward(
         count_here,
         head_at,
-        pre_keep,
-        pre_got,
+        pre_three,
         base_keep,
         base_got,
         sums_three,
@@ -991,22 +984,11 @@
         inside_whole,
         whole_head,
     )
-    cots = jnp.concatenate([strips_of(depth_cots), strips_of(seg_cots)], axis=1)
-    near, far = beside_y(cots)
-    sums_head, near, far = hold(sums_head, near, far)
-    across_low, across_high = across_y(near, far)
-    sums_head = fold(sums_head, CORE, *LINE)
-    sums_head, near, far, across_low, across_high = hold(
-        sums_head, near, far, across_low, across_high
-    )
-    cots_own = jnp.concatenate([cots, near])
-    cots_other = jnp.concatenate([across_low, across_high, far])
-    cots_keep = jnp.where(same, cots_own, cots_other)
-    cots_got = over_core(jnp.where(same, cots_other, cots_own))
-    sums_head = fold(sums_head, *PLANE)
-    task, streams_keep, streams_give, d_message, d_logit, d_norm_head, back_here = message_stage(
+    sums_head = fold(sums_head, CORE, *LINE, *PLANE)
+    task, *streams, d_message, d_logit, d_norm_head, back_here = message_stage(
         count_here,
         head_at,
+        ring_at,
         y.astype(jnp.int32).reshape(1),
         pre_head,
         sums_head,
@@ -1019,84 +1001,108 @@
     )
     task_grad, back_here = hold(conv_weight(task, d_message, 1, (d_logit,)), back_here)
     task_share = lax.psum_scatter(task_grad, POOL, scatter_dimension=0, tiled=True)
-    back_head = fold(back_here, CORE, *LINE)
-    back_head, twos = hold(back_head, beside_rows(pre_two))
-    back_head = fold(back_head, *PLANE)
-    back_head, streams_keep, streams_got = hold(
-        back_head, streams_keep, over_core(streams_give)
-    )
+    back_head = fold(back_here, CORE, *LINE, *PLANE)
+    back_head, streams = hold(back_head, streams)
     d_pre_head = norm_back(
         d_norm_head, pre_head, sums_head, gain_here, inside_whole, back_head, count
     )
-    streams_own, streams_other = sent_home(streams_keep, streams_got, same)
-    d_pre_head, streams_own, streams_other = hold(d_pre_head, streams_own, streams_other)
-    from_near, from_far = half_way(streams_other)
+    own, near, across, far = streams
+    from_near, from_far = half_way(across)
     head_grad = conv_weight(trunk, d_pre_head, 1)
     head_grad, d_pre_head, from_near, from_far = hold(head_grad, d_pre_head, from_near, from_far)
-    streams = last_way(streams_own, streams_other, from_near, from_far)
-    trunk_keep, trunk_give, back_three = trunk_back(head_at, d_pre_head, slope, steep, whole_head)
-    trunk_keep, trunk_give, back_three, streams, head_grad, task_share = hold(
-        trunk_keep, trunk_give, back_three, streams, head_grad, task_share
+    streams = last_way(own, near, far, from_near, from_far)
+    *d_trunk, back_three = trunk_back(ring_at, d_pre_head, slope, steep, whole_head)
+    d_trunk, back_three, streams, head_grad, task_share = hold(
+        d_trunk, back_three, streams, head_grad, task_share
     )
     head_share = lax.psum_scatter(head_grad, POOL, scatter_dimension=0, tiled=True)
     placed = jnp.where(
         jnp.arange(4)[None, :, None] == y, back_here[:, None], jnp.zeros((1, 1, 1), F32)
     ).reshape(2, -1)
-    back_wide = fold(jnp.concatenate([back_three, placed], axis=1), CORE)
-    back_wide, trunk_keep, trunk_got = hold(back_wide, trunk_keep, over_core(trunk_give))
-    trunk_own, trunk_other = sent_home(trunk_keep, trunk_got, same)
-    from_near, from_far = half_way(trunk_other)
-    back_wide = fold(back_wide, *LINE)
+    back_wide = jnp.concatenate([back_three, placed], axis=1)
+    own, near, across, far = d_trunk
+    from_near, from_far = half_way(across)
+    back_wide = fold(back_wide, CORE, *LINE)
     back_wide, from_near, from_far = hold(back_wide, from_near, from_far)
-    pieces = last_way(trunk_own, trunk_other, from_near, from_far)
+    pieces = last_way(own, near, far, from_near, from_far)
     back_wide = fold(back_wide, *PLANE)
-    back_wide, pieces = hold(back_wide, pieces)
+    def strip_of(value):
+        return lax.dynamic_slice_in_dim(value, y * length, length, 0)
+
+    pre_two_strip, pre_three_strip, base_strip, inside_strip = (
+        strip_of(a) for a in (pre_two, pre_three, base_image, inside_whole)
+    )
+
+    def ring_order(value):
+        return jnp.concatenate(
+            [
+                lax.dynamic_slice_in_dim(value, (y ^ flip) * length, length, 0)
+                for flip in range(4)
+            ]
+        )
+
+    act_two_ring = ring_order(act_two)
+    (
+        back_wide,
+        pieces,
+        pre_two_strip,
+        pre_three_strip,
+        base_strip,
+        inside_strip,
+        act_two_ring,
+    ) = hold(
+        back_wide,
+        pieces,
+        pre_two_strip,
+        pre_three_strip,
+        base_strip,
+        inside_strip,
+        act_two_ring,
+    )
     back_wide = fold(back_wide, *RIDGE)
     back_three, back_heads = back_wide[:, :deep], back_wide[:, deep:]
     d_joined, d_three_parts, d_norm_two, back_two = joined_back(
         count_here,
-        row_at,
+        ring_at,
         pieces,
-        pre_three,
-        base,
+        pre_three_strip,
+        base_strip,
         sums_three,
         wide_gain,
         wide_bias,
-        inside,
+        inside_strip,
         back_three,
         whole_trunk,
-        pre_two,
+        pre_two_strip,
         sums_two,
         bottleneck_gain[1:],
         bottleneck_bias[1:],
     )
     back_two = fold(back_two, CORE, *LINE)
-    back_two, d_norm_twos = hold(back_two, beside_rows(d_norm_two))
+    back_two, d_norm_twos = hold(back_two, around_y(d_norm_two))
     back_two = fold(back_two, *PLANE, *RIDGE)
 
-    d_three_part = jnp.concatenate(from_rows(d_three_parts))
-    normed_rows, unused = centred_by(jnp.concatenate(twos), sums_two, count)
-    act_two_rows = jax.nn.gelu(
-        bottleneck_gain[1] * normed_rows + bottleneck_bias[1]
-    ).astype(BF16)
-    grad_expand = turned_dot(act_two_rows, d_three_part).astype(BF16)
-    back_two, grad_expand = hold(back_two, grad_expand)
+    d_three_part = jnp.concatenate(for_me(d_three_parts))
+    grad_expand = turned_dot(act_two_ring, d_three_part).astype(BF16)
+    back_two, grad_expand, d_joined = hold(back_two, grad_expand, d_joined)
+    homeward = sent_home(
+        jnp.concatenate([d_joined, sum(a.astype(F32) for a in streams).astype(BF16)], axis=1)
+    )
     d_norm_one, back_one, d_two_part = dilated_back(
         count_here,
-        row_at,
+        ring_at,
         d_norm_twos,
-        twos,
+        pre_two,
         sums_two,
         back_two,
         bottleneck_gain[1:],
-        inside_own,
+        inside_whole,
         whole_trunk,
         first_tap,
-        pre_one,
+        pre_one_image,
         sums_one,
         bottleneck_gain[:1],
         bottleneck_bias[:1],
-        inside,
     )
     def to_chips(share):
         pieces = [share]
@@ -1118,46 +1124,44 @@
         got = lax.ppermute(jnp.stack(pieces), GROUP, pairs)
         return heads_placed(heads_at, local_here, pieces, got, widths)
 
-    back_one = fold(back_one, CORE, *RIDGE)
+    back_one = fold(back_one, CORE, *LINE)
     grad_dilated = conv_weight(act_one_image, d_two_part, 2)
     trunk_grad = jnp.concatenate([grad_expand, grad_dilated], axis=1)
-    back_one = fold(back_one, *LINE, *PLANE)
-    back_one, trunk_grad, head_share = hold(back_one, trunk_grad, head_share)
+    back_one, trunk_grad, homeward = hold(back_one, trunk_grad, homeward)
+    back_one = fold(back_one, *PLANE)
     d_pre_one = norm_back(
-        d_norm_one, pre_one, sums_one, bottleneck_gain[0], inside, back_one, count
-    )
-    d_one_parts = [
-        lax.dynamic_slice_in_dim(d_pre_one, (strip ^ flip) * 128, 128, 1) for flip in (0, 2, 1, 3)
-    ]
-    d_one_part = jnp.concatenate(from_rows(d_one_parts))
-    trunk_share = shares_summed(trunk_grad, IMG)
-    grad_reduce = turned_dot(base_image, d_one_part).astype(BF16)
-    reduce_share = shares_summed(grad_reduce, IMG)
-    head_pieces = to_chips(head_share)
-
-    def all_strips(value):
-        pair = in_order(value, over_core(value), core)
-        pair = jnp.stack(pair)
-        return jnp.concatenate(in_order(pair, over_y(pair, 1), ylo))
-
-    all_trunk = all_strips(trunk_share)
-    sum_expand = jnp.moveaxis(all_trunk[:, :, :512], 0, 1).reshape(16, -1).astype(F32)
-    sum_dilated = (
-        jnp.moveaxis(all_trunk[:, :, 512:].reshape(4, 16, 9, 128), 0, 2)
-        .reshape(16, -1)
-        .astype(F32)
-    )
-    sum_reduce = jnp.moveaxis(all_strips(reduce_share), 0, 1).reshape(-1, 512).astype(F32)
-
+        d_norm_one, pre_one_image, sums_one, bottleneck_gain[0], inside_whole, back_one, count
+    )
+    grad_reduce = turned_dot(
+        base_image, lax.dynamic_slice_in_dim(d_pre_one, y * 128, 128, 1)
+    ).astype(BF16)
+    trunk_grad = jnp.concatenate(
+        [trunk_grad, grad_reduce.reshape(trunk_grad.shape[0], -1)], axis=1
+    )
+    trunk_grad, head_share, task_share, d_pre_one = hold(
+        trunk_grad, head_share, task_share, d_pre_one
+    )
+    trunk_parts = shares_sent(trunk_grad, POOL)
     wide = message_weight.shape[2]
-    (sum_head,) = to_cores(head_pieces, wide)
-    task_share, d_pre_one = hold(task_share, d_pre_one)
+    (sum_head,) = to_cores(to_chips(head_share), wide)
     sum_message, sum_gate = to_cores(to_chips(task_share), wide, gate_weight.shape[2])
-
-    d_base = d_joined + times_turned(d_pre_one, whole_reduce)
-    input_grad = maps_of(d_base * inside, across)
-
-    streams = maps_of(sum(a.astype(F32) for a in streams) * inside, across)
+    d_pre_one = sent_home(strip_of(d_pre_one))
+    d_base = homeward[:, :deep].astype(F32) + times_turned(d_pre_one, whole_reduce)
+    input_grad = maps_of(d_base * inside, width)
+    trunk_parts, sum_head, sum_message, sum_gate, input_grad = hold(
+        trunk_parts, sum_head, sum_message, sum_gate, input_grad
+    )
+    all_trunk, all_reduce = to_cores(
+        to_chips(parts_summed(trunk_parts)), trunk_grad.shape[1] - 512, 512
+    )
+    sum_expand = jnp.moveaxis(all_trunk[:, :, :512], 0, 1).reshape(channels, -1)
+    sum_dilated = jnp.moveaxis(
+        all_trunk[:, :, 512:].reshape(4, channels, 9, 128), 0, 2
+    ).reshape(channels, -1)
+    sum_reduce = jnp.moveaxis(all_reduce.reshape(4, -1, 128), 0, 1).reshape(-1, 512)
+
+
+    streams = maps_of(homeward[:, deep:].astype(F32) * inside, width)
     depth_out, seg_out = jnp.split(streams, 2, axis=3)
 
     return (

time: 589 us -> 553 us (0.939)
  waiting for transfers between devices: 156 us -> 126 us
  starting transfers between devices: 169 us -> 153 us
  Pallas kernels: 156 us -> 167 us
  other arithmetic: 48.1 us -> 38.2 us
  local copies, waits for them, and re-layouts: 27 us -> 34.1 us
    ppermute x93 -> x69, waiting for transfers between devices: 119 us -> 88.7 us  [swap(): return lax.ppermute(value, axis, [(i, i ^ flip) for i in range(count)])]
    ppermute x93 -> x69, starting transfers between devices: 116 us -> 95.7 us  [swap(): return lax.ppermute(value, axis, [(i, i ^ flip) for i in range(count)])]
    all_to_all x2 -> x1, waiting for transfers between devices: 13.1 us -> 0.01 us  [shares_sent(): lax.all_to_all(value.reshape(count, value.shape[0] // count, value.shape[...]
    pallas_call x12 -> x13, Pallas kernels: 156 us -> 167 us  [call(): pl.pallas_call(kernel, grid=grid, in_specs=in_specs, out_specs=out_specs,...]
    reduce_scatter x1, waiting for transfers between devices: 0.01 us -> 9.54 us  [shards(): lax.psum_scatter(task_grad, POOL, scatter_dimension=0, tiled=True)]
    dynamic_slice x1 -> x6, local copies, waits for them, and re-layouts: 0.04 us -> 6.3 us  [the longest x5 6.24 us: strip_of(): return lax.dynamic_slice_in_dim(value, y * length, length, 0)]
    ppermute x5 -> x2, starting transfers between devices: 6.78 us -> 13 us  [sent_home(): return lax.ppermute(value, GROUP, HOME)]
    all_to_all x2 -> x1, starting transfers between devices: 16.4 us -> 10.8 us  [shares_sent(): lax.all_to_all(value.reshape(count, value.shape[0] // count, value.shape[...]
  transfers between devices with their start and end apart: 118 -> 93, of which waited for: 65 -> 59; matrix products, arithmetic and copies ran while one was open for 13% -> 12% of each run, Pallas kernels for 21% -> 25%
where the time goes in v3:
time: 553 us; the launch traced here: 543 us
  Pallas kernels  167 us (30%)
  starting transfers between devices  153 us (28%)
  waiting for transfers between devices  126 us (23%)
  other arithmetic  38.2 us (7%)
  local copies, waits for them, and re-layouts  34.1 us (6%)
  between operations  15.6 us (3%)
  matrix products  9.12 us (2%)
    pallas_call x13, Pallas kernels, call(): pl.pallas_call(kernel, grid=grid, in_specs=in_specs, out_specs=out_specs,...  167 us
    ppermute x69, starting transfers between devices, swap(): return lax.ppermute(value, axis, [(i, i ^ flip) for i in range(count)])  95.7 us
    ppermute x69, waiting for transfers between devices, swap(): return lax.ppermute(value, axis, [(i, i ^ flip) for i in range(count)])  88.7 us
    ppermute x9, starting transfers between devices, to_chips(): pieces.append(lax.ppermute(share, GROUP, pairs))  17.7 us
    ppermute x2, starting transfers between devices, sent_home(): return lax.ppermute(value, GROUP, HOME)  13 us
  transfers between devices with their start and end apart: 93, of which 59 were waited for; matrix products, arithmetic and copies ran while one was open for 12% of the time, Pallas kernels for 25%

profile of v3, /device:TPU:1, one launch (start us, length us, event | category | flops | bytes accessed | tf_op | source)
XLA Modules:
  0.0 543.0 jit_solution(14897015779402306796)
XLA Ops:
  11.3 7.5 %collective-permute-done = bf16[16,8704]{1,0:T(8,128)(2,1)S(1)} collective-permute-done((bf16[16,8704]{1,0:T(8,128)(2,1)S(1)}, bf16[16,8704]{1,0:T(8,128)(2,1)S(1)}, u32[]{:S(2)}, u32[]{:S(2)}) %collective-permute-start) | collective-permute-done | bytes 278560 | tf_op jit(solution)/shard_map/ppermute | solution.py:885
  23.6 7.6 %all-to-all-start = ((bf16[16,64,512]{2,1,0:T(8,128)(2,1)}), bf16[16,64,512]{2,1,0:T(8,128)(2,1)S(1)}, u32[]{:S(2)}, u32[]{:S(2)}) async-start(bf16[16,64,512]{2,1,0:T(8,128)(2,1)} %broadcast_in_dim.56), calls=%async_computation | async-start | bytes 2097152 | tf_op jit(solution)/shard_map/all_to_all | solution.py:907
  48.8 7.2 %collective-permute-start.6 = (bf16[320,2048]{1,0:T(8,128)(2,1)}, bf16[320,2048]{1,0:T(8,128)(2,1)}, u32[]{:S(2)}, u32[]{:S(2)}) collective-permute-start(bf16[320,2048]{1,0:T(8,128)(2,1)} %get-tuple-element.267), channel_id=1, source_target_pairs={{0,32},{32,0},{1,33},{33,1},{2,34},{34,2},{3,35},{35,3},{4,36},{36... | collective-permute-start | bytes 3932168 | tf_op jit(solution)/shard_map/ppermute | solution.py:27
  77.1 3.1 collective-permute-start.12
  81.8 11.9 %shard_map.271 = (bf16[640,512]{1,0:T(8,128)(2,1)}, f32[2,512]{1,0:T(2,128)}, bf16[640,512]{1,0:T(8,128)(2,1)}, bf16[640,512]{1,0:T(8,128)(2,1)}) custom-call(f32[1]{0:T(128)} %bitcast.count_ref, s32[4]{0:T(128)} %add_multiply_fusion.1.at_ref, bf16[640,512]{1,0:T(8,128)(2,1)} %pad_maximum_fusion.6.value_ref, f32[2,512]{1,0:T(2,128)} %add.337.sums_ref.low_sums, ...), custom_call_target="tpu_custom_call" | custom-call | flops 3019898880 | bytes 7481876 | tf_op jit(solution)/shard_map/pallas_call | solution.py:172
  93.7 3.6 collective-permute-start.13
  113.5 6.3 %shard_map.272 = (bf16[640,512]{1,0:T(8,128)(2,1)}, bf16[640,2048]{1,0:T(8,128)(2,1)}, f32[2,2048]{1,0:T(2,128)}) custom-call(f32[1]{0:T(128)} %bitcast.count_ref, bf16[640,512]{1,0:T(8,128)(2,1)} %get-tuple-element.144.value_ref, f32[2,512]{1,0:T(2,128)} %add.342.sums_ref.low_sums, f32[1,512]{1,0:T(1,128)} %get-tuple-element.300.gain_ref.low_gain, ...), custom_call_target="tpu_custom_call" | custom-call | flops 1342177280 | bytes 7481860 | tf_op jit(solution)/shard_map/pallas_call | solution.py:172
  119.8 6.5 %collective-permute-start.18 = (f32[2,2048]{1,0:T(2,128)}, f32[2,2048]{1,0:T(2,128)S(1)}, u32[]{:S(2)}, u32[]{:S(2)}) collective-permute-start(f32[2,2048]{1,0:T(2,128)} %get-tuple-element.148), channel_id=1, source_target_pairs={{0,32},{32,0},{1,33},{33,1},{2,34},{34,2},{3,35},{35,3},{4,36},{36... | collective-permute-start | bytes 49160 | tf_op jit(solution)/shard_map/ppermute | solution.py:27
  128.8 8.3 %collective-permute-done.20 = bf16[160,1024]{1,0:T(8,128)(2,1)S(1)} collective-permute-done((bf16[160,1024]{1,0:T(8,128)(2,1)S(1)}, bf16[160,1024]{1,0:T(8,128)(2,1)S(1)}, u32[]{:S(2)}, u32[]{:S(2)}) %collective-permute-start.20) | collective-permute-done | bytes 327712 | tf_op jit(solution)/shard_map/ppermute | solution.py:27
  138.7 3.3 collective-permute-done.22
  150.7 3.3 collective-permute-done.26
  154.8 3.4 collective-permute-done.27
  160.4 30.3 %shard_map.273 = (f32[640,512]{1,0:T(8,128)}, f32[2,512]{1,0:T(2,128)}, bf16[640,2048]{1,0:T(8,128)(2,1)}, bf16[640,2048]{1,0:T(8,128)(2,1)}, bf16[640,2048]{1,0:T(8,128)(2,1)}, /*index=5*/bf16[640,2048]{1,0:T(8,128)(2,1)}) custom-call(f32[1]{0:T(128)} %bitcast.count_ref, s32[4]{0:T(128)} %add_multiply_fusion.1.at_ref, ...), custom_call_target="tpu_custom_call" | custom-call | flops 12079595520 | bytes 24152596 | tf_op jit(solution)/shard_map/pallas_call | solution.py:172
  210.6 20.7 %shard_map.274 = (bf16[640,512]{1,0:T(8,128)(2,1)}, bf16[160,1024]{1,0:T(8,128)(2,1)}, bf16[160,1024]{1,0:T(8,128)(2,1)}, bf16[160,1024]{1,0:T(8,128)(2,1)}, bf1...) custom-call(f32[1]{0:T(128)} %bitcast.count_ref, ...), custom_call_target="tpu_custom_call" | custom-call | flops 6710886400 | bytes 7875112 | tf_op jit(solution)/shard_map/pallas_call | solution.py:172
  231.2 9.8 %shard_map.275 = bf16[512,5120]{1,0:T(8,128)(2,1)} custom-call(bf16[640,512]{1,0:T(8,128)(2,1)} %get-tuple-element.169.x_ref, bf16[640,512]{1,0:T(8,128)(2,1)} %get-tuple-element.170.g_ref, bf16[640,512]{1,0:T(8,128)(2,1)} %get-tuple-element.171.rest_0_), custom_call_target="tpu_custom_call" | custom-call | flops 3355443200 | bytes 1966080 | tf_op jit(solution)/shard_map/pallas_call | solution.py:172
  260.8 21.0 %shard_map.276 = bf16[2048,4608]{1,0:T(8,128)(2,1)} custom-call(bf16[640,2048]{1,0:T(8,128)(2,1)} %get-tuple-element.162.x_ref, bf16[640,512]{1,0:T(8,128)(2,1)} %multiply_convert_fusion.1.g_ref), custom_call_target="tpu_custom_call" | custom-call | flops 12079595520 | bytes 3276800 | tf_op jit(solution)/shard_map/pallas_call | solution.py:172
  283.9 29.8 %shard_map.277 = (bf16[160,2048]{1,0:T(8,128)(2,1)}, bf16[160,2048]{1,0:T(8,128)(2,1)}, bf16[160,2048]{1,0:T(8,128)(2,1)}, bf16[160,2048]{1,0:T(8,128)(2,1)}, f32[2,2048]{1,0:T(2,128)}) custom-call(s32[4]{0:T(128)} %get-tuple-element.265.ring_ref.at_ref, bf16[640,512]{1,0:T(8,128)(2,1)} %multiply_convert_fusion.1.g_ref, ...), custom_call_target="tpu_custom_call" | custom-call | flops 12079595520 | bytes 24772624 | tf_op jit(solution)/shard_map/pallas_call | solution.py:172
  313.6 9.5 %reduce-scatter.3.cloned.1.call-done.refs_0_ = bf16[16,5120]{1,0:T(8,128)(2,1)} async-done(((bf16[512,5120]{1,0:T(8,128)(2,1)}), bf16[16,5120]{1,0:T(8,128)(2,1)}) %reduce-scatter.3.cloned.1.call-update) | async-done | bytes 163856 | tf_op jit(solution)/shard_map/reduce_scatter | solution.py:1003
  349.4 4.5 collective-permute-done.51.far_ref
  362.2 7.1 %shard_map.278 = (bf16[160,2048]{1,0:T(8,128)(2,1)}, bf16[160,512]{1,0:T(8,128)(2,1)}, bf16[160,512]{1,0:T(8,128)(2,1)}, bf16[160,512]{1,0:T(8,128)(2,1)}, bf16[...) custom-call(f32[1]{0:T(128)} %bitcast.count_ref, s32[4]{0:T(128)} %get-tuple-element.265.ring_ref.at_ref, ...), custom_call_target="tpu_custom_call" | custom-call | flops 335544320 | bytes 10314388 | tf_op jit(solution)/shard_map/pallas_call | solution.py:172
  372.6 5.4 %collective-permute-start.54 = (f32[2,512]{1,0:T(2,128)}, f32[2,512]{1,0:T(2,128)S(1)}, u32[]{:S(2)}, u32[]{:S(2)}) collective-permute-start(f32[2,512]{1,0:T(2,128)} %get-tuple-element.213), channel_id=1, source_target_pairs={{0,32},{32,0},{1,33},{33,1},{2,34},{34,2},{3,35},{35,3},{4,36},{36... | collective-permute-start | bytes 12296 | tf_op jit(solution)/shard_map/ppermute | solution.py:27
  403.4 6.9 %collective-permute-start.70 = (bf16[160,3072]{1,0:T(8,128)(2,1)S(1)}, bf16[160,3072]{1,0:T(8,128)(2,1)}, u32[]{:S(2)}, u32[]{:S(2)}) collective-permute-start(bf16[160,3072]{1,0:T(8,128)(2,1)S(1)} %pad_maximum_fusion.5), channel_id=1, source_target_pairs={{0,0},{1,64},{32,1},{33,65},{64,32},{65,96},{96,33},{97,97},{2,2},... | collective-permute-start | bytes 2949128 | tf_op jit(solution)/shard_map/ppermute | solution.py:69
  410.4 14.6 %shard_map.279 = (bf16[640,512]{1,0:T(8,128)(2,1)}, f32[2,512]{1,0:T(2,128)}, bf16[640,128]{1,0:T(8,128)(2,1)}) custom-call(f32[1]{0:T(128)} %bitcast.count_ref, s32[4]{0:T(128)} %get-tuple-element.265.ring_ref.at_ref, bf16[160,512]{1,0:T(8,128)(2,1)} %get-tuple-element.215.u0, bf16[160,512]{1,0:T(8,128)(2,1)} %copy-done.51, bf16[160,512]{1,0:T(8,128)(2,1)} %copy-done.50, ...), custom_call_target="tpu_custom_call" | custom-call | flops 3019898880 | bytes 8802836 | tf_op jit(solution)/shard_map/pallas_call | solution.py:172
  427.1 6.5 %shard_map.280 = bf16[512,1152]{1,0:T(8,128)(2,1)} custom-call(bf16[640,512]{1,0:T(8,128)(2,1)} %get-tuple-element.230.x_ref, bf16[640,128]{1,0:T(8,128)(2,1)} %get-tuple-element.231.g_ref), custom_call_target="tpu_custom_call" | custom-call | flops 754974720 | bytes 819200 | tf_op jit(solution)/shard_map/pallas_call | solution.py:172
  452.0 3.1 collective-permute-start.75
  458.6 10.0 %collective-permute-done.75.refs_3_ = bf16[64,4608]{1,0:T(8,128)(2,1)S(1)} collective-permute-done((bf16[64,4608]{1,0:T(8,128)(2,1)}, bf16[64,4608]{1,0:T(8,128)(2,1)S(1)}, u32[]{:S(2)}, u32[]{:S(2)}) %collective-permute-start.75) | collective-permute-done | bytes 589856 | tf_op jit(solution)/shard_map/ppermute | solution.py:1116
  469.5 3.2 pad_maximum_fusion
  474.0 10.8 %all-to-all-start.1 = ((bf16[32,16,2176]{2,1,0:T(8,128)(2,1)}), bf16[32,16,2176]{2,1,0:T(8,128)(2,1)S(1)}, u32[]{:S(2)}, u32[]{:S(2)}) async-start(bf16[32,16,2176]{2,1,0:T(8,128)(2,1)} %bitcast.42), calls=%async_computation.3 | async-start | bytes 4456448 | tf_op jit(solution)/shard_map/all_to_all | solution.py:825
  493.1 6.1 %collective-permute-start.81 = (bf16[160,512]{1,0:T(8,128)(2,1)S(1)}, bf16[160,512]{1,0:T(8,128)(2,1)S(1)}, u32[]{:S(2)}, u32[]{:S(2)}) collective-permute-start(bf16[160,512]{1,0:T(8,128)(2,1)S(1)} %constant_dynamic-slice_fusion), channel_id=1, source_target_pairs={{0,0},{1,64},{32,1},{33,65},{64,32},{65,96},{96,33},{97,97},{2,2},... | collective-permute-start | bytes 491528 | tf_op jit(solution)/shard_map/ppermute | solution.py:69
  499.3 3.6 collective-permute-done.81
  510.0 4.9 shard_map.281
  516.9 4.9 collective-permute-start.83
  (438 shorter events, 242.7 us)
Async XLA Ops:
  7.2 74.6 %all-gather.4.cloned.1.call-start = ((), (), s32[]{:S(2)}) async-start(), calls=%async_computation.4 | async-start | bytes 7028736 | tf_op jit(solution)/shard_map/all_gather | solution.py:911
  21.7 15.3 %collective-permute-start.3 = (bf16[160,2048]{1,0:T(8,128)(2,1)S(1)}, bf16[160,2048]{1,0:T(8,128)(2,1)S(1)}, u32[]{:S(2)}, u32[]{:S(2)}) collective-permute-start(bf16[160,2048]{1,0:T(8,128)(2,1)S(1)} %bitcast_multiply_fusion), channel_id=1, source_target_pairs={{0,65},{1,64},{64,1},{65,0},{2,67},{3,66},{66,3},{67,2},{4,69},{5,... | collective-permute-start | bytes 1966088 | tf_op jit(solution)/shard_map/ppermute | solution.py:27
  21.8 15.3 %collective-permute-start.2 = (bf16[160,2048]{1,0:T(8,128)(2,1)S(1)}, bf16[160,2048]{1,0:T(8,128)(2,1)S(1)}, u32[]{:S(2)}, u32[]{:S(2)}) collective-permute-start(bf16[160,2048]{1,0:T(8,128)(2,1)S(1)} %bitcast_multiply_fusion), channel_id=1, source_target_pairs={{0,64},{1,65},{64,0},{65,1},{2,66},{3,67},{66,2},{67,3},{4,68},{5,... | collective-permute-start | bytes 1966088 | tf_op jit(solution)/shard_map/ppermute | solution.py:27
  23.6 32.4 %all-to-all-start = ((bf16[16,64,512]{2,1,0:T(8,128)(2,1)}), bf16[16,64,512]{2,1,0:T(8,128)(2,1)S(1)}, u32[]{:S(2)}, u32[]{:S(2)}) async-start(bf16[16,64,512]{2,1,0:T(8,128)(2,1)} %broadcast_in_dim.56), calls=%async_computation | async-start | bytes 2097152 | tf_op jit(solution)/shard_map/all_to_all | solution.py:907
  31.2 129.2 %all-gather.6.cloned.1.call-start = ((), (), s32[]{:S(2)}) async-start(), calls=%async_computation.5 | async-start | bytes 19464192 | tf_op jit(solution)/shard_map/all_gather | solution.py:926
  41.2 14.8 %collective-permute-start.7 = (bf16[64,4608]{1,0:T(8,128)(2,1)}, bf16[64,4608]{1,0:T(8,128)(2,1)}, u32[]{:S(2)}, u32[]{:S(2)}) collective-permute-start(bf16[64,4608]{1,0:T(8,128)(2,1)} %dynamic-slice_bitcast_fusion), channel_id=1, source_target_pairs={{0,65},{33,96},{64,1},{97,32},{2,67},{35,98},{66,3},{99,34},{4,69}... | collective-permute-start | bytes 1769480 | tf_op jit(solution)/shard_map/ppermute | solution.py:885
  48.8 11.7 %collective-permute-start.6 = (bf16[320,2048]{1,0:T(8,128)(2,1)}, bf16[320,2048]{1,0:T(8,128)(2,1)}, u32[]{:S(2)}, u32[]{:S(2)}) collective-permute-start(bf16[320,2048]{1,0:T(8,128)(2,1)} %get-tuple-element.267), channel_id=1, source_target_pairs={{0,32},{32,0},{1,33},{33,1},{2,34},{34,2},{3,35},{35,3},{4,36},{36... | collective-permute-start | bytes 3932168 | tf_op jit(solution)/shard_map/ppermute | solution.py:27
  60.5 150.1 %all-gather.8.cloned.1.call-start = ((), (), s32[]{:S(2)}) async-start(), calls=%async_computation.6 | async-start | bytes 5406720 | tf_op jit(solution)/shard_map/all_gather | solution.py:963
  111.4 16.6 %collective-permute-start.21 = (bf16[16,5120]{1,0:T(8,128)(2,1)S(1)}, bf16[16,5120]{1,0:T(8,128)(2,1)S(1)}, u32[]{:S(2)}, u32[]{:S(2)}) collective-permute-start(bf16[16,5120]{1,0:T(8,128)(2,1)S(1)} %dynamic-slice_bitcast_fusion.1), channel_id=1, source_target_pairs={{0,65},{33,96},{64,1},{97,32},{2,67},{35,98},{66,3},{99,34},{4,69}... | collective-permute-start | bytes 491528 | tf_op jit(solution)/shard_map/ppermute | solution.py:885
  126.3 10.7 %collective-permute-start.20 = (bf16[160,1024]{1,0:T(8,128)(2,1)S(1)}, bf16[160,1024]{1,0:T(8,128)(2,1)S(1)}, u32[]{:S(2)}, u32[]{:S(2)}) collective-permute-start(bf16[160,1024]{1,0:T(8,128)(2,1)S(1)} %pad_maximum_fusion.12), channel_id=1, source_target_pairs={{0,65},{1,64},{64,1},{65,0},{2,67},{3,66},{66,3},{67,2},{4,69},{5,... | collective-permute-start | bytes 983048 | tf_op jit(solution)/shard_map/ppermute | solution.py:27
  126.4 10.6 %collective-permute-start.19 = (bf16[160,1024]{1,0:T(8,128)(2,1)S(1)}, bf16[160,1024]{1,0:T(8,128)(2,1)S(1)}, u32[]{:S(2)}, u32[]{:S(2)}) collective-permute-start(bf16[160,1024]{1,0:T(8,128)(2,1)S(1)} %pad_maximum_fusion.12), channel_id=1, source_target_pairs={{0,64},{1,65},{64,0},{65,1},{2,66},{3,67},{66,2},{67,3},{4,68},{5,... | collective-permute-start | bytes 983048 | tf_op jit(solution)/shard_map/ppermute | solution.py:27
  137.1 186.1 %reduce-scatter.3.cloned.1.call-start = ((), (), s32[]{:S(2)}) async-start(), calls=%async_computation.7 | async-start | bytes 5406720 | tf_op jit(solution)/shard_map/reduce_scatter | solution.py:1003
  147.9 11.0 %collective-permute-start.28 = (bf16[320,1024]{1,0:T(8,128)(2,1)S(1)}, bf16[320,1024]{1,0:T(8,128)(2,1)S(1)}, u32[]{:S(2)}, u32[]{:S(2)}) collective-permute-start(bf16[320,1024]{1,0:T(8,128)(2,1)S(1)} %get-tuple-element.271), channel_id=1, source_target_pairs={{0,32},{32,0},{1,33},{33,1},{2,34},{34,2},{3,35},{35,3},{4,36},{36... | collective-permute-start | bytes 1966088 | tf_op jit(solution)/shard_map/ppermute | solution.py:27
  241.1 211.0 %reduce-scatter.5.cloned.1.call-start = ((), (), s32[]{:S(2)}) async-start(), calls=%async_computation.8 | async-start | bytes 19464192 | tf_op jit(solution)/shard_map/reduce_scatter | solution.py:1018
  256.0 25.9 %collective-permute-start.40 = (bf16[80,1024]{1,0:T(8,128)(2,1)}, bf16[80,1024]{1,0:T(8,128)(2,1)S(1)}, u32[]{:S(2)}, u32[]{:S(2)}) collective-permute-start(bf16[80,1024]{1,0:T(8,128)(2,1)} %get-tuple-element.281), channel_id=1, source_target_pairs={{0,65},{1,64},{64,1},{65,0},{2,67},{3,66},{66,3},{67,2},{4,69},{5,... | collective-permute-start | bytes 491528 | tf_op jit(solution)/shard_map/ppermute | solution.py:27
  258.7 23.2 %collective-permute-start.39 = (bf16[80,1024]{1,0:T(8,128)(2,1)S(1)}, bf16[80,1024]{1,0:T(8,128)(2,1)S(1)}, u32[]{:S(2)}, u32[]{:S(2)}) collective-permute-start(bf16[80,1024]{1,0:T(8,128)(2,1)S(1)} %get-tuple-element.282), channel_id=1, source_target_pairs={{0,64},{1,65},{64,0},{65,1},{2,66},{3,67},{66,2},{67,3},{4,68},{5,... | collective-permute-start | bytes 491528 | tf_op jit(solution)/shard_map/ppermute | solution.py:27
  282.0 31.6 %collective-permute-start.41 = (bf16[160,1024]{1,0:T(8,128)(2,1)S(1)}, bf16[160,1024]{1,0:T(8,128)(2,1)S(1)}, u32[]{:S(2)}, u32[]{:S(2)}) collective-permute-start(bf16[160,1024]{1,0:T(8,128)(2,1)S(1)} %pad_maximum_fusion.13), channel_id=1, source_target_pairs={{0,64},{1,65},{64,0},{65,1},{2,66},{3,67},{66,2},{67,3},{4,68},{5,... | collective-permute-start | bytes 983048 | tf_op jit(solution)/shard_map/ppermute | solution.py:27
  283.6 30.0 %collective-permute-start.42 = (bf16[160,1024]{1,0:T(8,128)(2,1)S(1)}, bf16[160,1024]{1,0:T(8,128)(2,1)S(1)}, u32[]{:S(2)}, u32[]{:S(2)}) collective-permute-start(bf16[160,1024]{1,0:T(8,128)(2,1)S(1)} %pad_maximum_fusion.14), channel_id=1, source_target_pairs={{0,65},{1,64},{64,1},{65,0},{2,67},{3,66},{66,3},{67,2},{4,69},{5,... | collective-permute-start | bytes 983048 | tf_op jit(solution)/shard_map/ppermute | solution.py:27
  326.4 10.3 %collective-permute-start.47 = (bf16[80,2048]{1,0:T(8,128)(2,1)S(1)}, bf16[80,2048]{1,0:T(8,128)(2,1)S(1)}, u32[]{:S(2)}, u32[]{:S(2)}) collective-permute-start(bf16[80,2048]{1,0:T(8,128)(2,1)S(1)} %get-tuple-element.279), channel_id=1, source_target_pairs={{0,65},{1,64},{64,1},{65,0},{2,67},{3,66},{66,3},{67,2},{4,69},{5,... | collective-permute-start | bytes 983048 | tf_op jit(solution)/shard_map/ppermute | solution.py:27
  337.8 16.1 %collective-permute-start.51 = (bf16[160,2048]{1,0:T(8,128)(2,1)S(1)}, bf16[160,2048]{1,0:T(8,128)(2,1)S(1)}, u32[]{:S(2)}, u32[]{:S(2)}) collective-permute-start(bf16[160,2048]{1,0:T(8,128)(2,1)S(1)} %pad_maximum_fusion.9), channel_id=1, source_target_pairs={{0,65},{1,64},{64,1},{65,0},{2,67},{3,66},{66,3},{67,2},{4,69},{5,... | collective-permute-start | bytes 1966088 | tf_op jit(solution)/shard_map/ppermute | solution.py:27
  339.6 14.9 %collective-permute-start.50 = (bf16[160,2048]{1,0:T(8,128)(2,1)S(1)}, bf16[160,2048]{1,0:T(8,128)(2,1)S(1)}, u32[]{:S(2)}, u32[]{:S(2)}) collective-permute-start(bf16[160,2048]{1,0:T(8,128)(2,1)S(1)} %pad_maximum_fusion.8), channel_id=1, source_target_pairs={{0,64},{1,65},{64,0},{65,1},{2,66},{3,67},{66,2},{67,3},{4,68},{5,... | collective-permute-start | bytes 1966088 | tf_op jit(solution)/shard_map/ppermute | solution.py:27
  369.3 16.9 %collective-permute-start.59 = (bf16[160,512]{1,0:T(8,128)(2,1)}, bf16[160,512]{1,0:T(8,128)(2,1)S(1)}, u32[]{:S(2)}, u32[]{:S(2)}) collective-permute-start(bf16[160,512]{1,0:T(8,128)(2,1)} %get-tuple-element.215.u0), channel_id=1, source_target_pairs={{0,65},{1,64},{64,1},{65,0},{2,67},{3,66},{66,3},{67,2},{4,69},{5,... | collective-permute-start | bytes 491528 | tf_op jit(solution)/shard_map/ppermute | solution.py:27
  370.7 15.5 %collective-permute-start.58 = (bf16[160,512]{1,0:T(8,128)(2,1)}, bf16[160,512]{1,0:T(8,128)(2,1)S(1)}, u32[]{:S(2)}, u32[]{:S(2)}) collective-permute-start(bf16[160,512]{1,0:T(8,128)(2,1)} %get-tuple-element.215.u0), channel_id=1, source_target_pairs={{0,1},{1,0},{64,65},{65,64},{2,3},{3,2},{66,67},{67,66},{4,5},{5,4... | collective-permute-start | bytes 491528 | tf_op jit(solution)/shard_map/ppermute | solution.py:27
  370.7 15.5 %collective-permute-start.57 = (bf16[160,512]{1,0:T(8,128)(2,1)}, bf16[160,512]{1,0:T(8,128)(2,1)S(1)}, u32[]{:S(2)}, u32[]{:S(2)}) collective-permute-start(bf16[160,512]{1,0:T(8,128)(2,1)} %get-tuple-element.215.u0), channel_id=1, source_target_pairs={{0,64},{1,65},{64,0},{65,1},{2,66},{3,67},{66,2},{67,3},{4,68},{5,... | collective-permute-start | bytes 491528 | tf_op jit(solution)/shard_map/ppermute | solution.py:27
  403.4 34.0 %collective-permute-start.70 = (bf16[160,3072]{1,0:T(8,128)(2,1)S(1)}, bf16[160,3072]{1,0:T(8,128)(2,1)}, u32[]{:S(2)}, u32[]{:S(2)}) collective-permute-start(bf16[160,3072]{1,0:T(8,128)(2,1)S(1)} %pad_maximum_fusion.5), channel_id=1, source_target_pairs={{0,0},{1,64},{32,1},{33,65},{64,32},{65,96},{96,33},{97,97},{2,2},... | collective-permute-start | bytes 2949128 | tf_op jit(solution)/shard_map/ppermute | solution.py:69
  452.0 16.5 %collective-permute-start.75 = (bf16[64,4608]{1,0:T(8,128)(2,1)}, bf16[64,4608]{1,0:T(8,128)(2,1)S(1)}, u32[]{:S(2)}, u32[]{:S(2)}) collective-permute-start(bf16[64,4608]{1,0:T(8,128)(2,1)} %reduce-scatter.5.cloned.1.call-done.refs_0_), channel_id=1, source_target_pairs={{1,64},{32,97},{65,0},{96,33},{3,66},{34,99},{67,2},{98,35},{5,68}... | collective-permute-start | bytes 1769480 | tf_op jit(solution)/shard_map/ppermute | solution.py:1116
  455.1 14.3 %collective-permute-start.74 = (bf16[64,4608]{1,0:T(8,128)(2,1)}, bf16[64,4608]{1,0:T(8,128)(2,1)S(1)}, u32[]{:S(2)}, u32[]{:S(2)}) collective-permute-start(bf16[64,4608]{1,0:T(8,128)(2,1)} %reduce-scatter.5.cloned.1.call-done.refs_0_), channel_id=1, source_target_pairs={{1,0},{32,33},{65,64},{96,97},{3,2},{34,35},{67,66},{98,99},{5,4},... | collective-permute-start | bytes 1769480 | tf_op jit(solution)/shard_map/ppermute | solution.py:1116
  457.9 11.6 %collective-permute-start.73 = (bf16[64,4608]{1,0:T(8,128)(2,1)}, bf16[64,4608]{1,0:T(8,128)(2,1)S(1)}, u32[]{:S(2)}, u32[]{:S(2)}) collective-permute-start(bf16[64,4608]{1,0:T(8,128)(2,1)} %reduce-scatter.5.cloned.1.call-done.refs_0_), channel_id=1, source_target_pairs={{0,64},{33,97},{64,0},{97,33},{2,66},{35,99},{66,2},{99,35},{4,68}... | collective-permute-start | bytes 1769480 | tf_op jit(solution)/shard_map/ppermute | solution.py:1116
  472.7 37.3 %collective-permute-start.76 = (bf16[4,64,4608]{2,1,0:T(8,128)(2,1)}, bf16[4,64,4608]{2,1,0:T(8,128)(2,1)}, u32[]{:S(2)}, u32[]{:S(2)}) collective-permute-start(bf16[4,64,4608]{2,1,0:T(8,128)(2,1)} %pad_maximum_fusion), channel_id=1, source_target_pairs={{0,32},{33,1},{64,96},{97,65},{2,34},{35,3},{66,98},{99,67},{4,36}... | collective-permute-start | bytes 7077896 | tf_op jit(solution)/shard_map/ppermute | solution.py:1124
  474.0 40.9 %all-to-all-start.1 = ((bf16[32,16,2176]{2,1,0:T(8,128)(2,1)}), bf16[32,16,2176]{2,1,0:T(8,128)(2,1)S(1)}, u32[]{:S(2)}, u32[]{:S(2)}) async-start(bf16[32,16,2176]{2,1,0:T(8,128)(2,1)} %bitcast.42), calls=%async_computation.3 | async-start | bytes 4456448 | tf_op jit(solution)/shard_map/all_to_all | solution.py:825
  490.9 15.7 %collective-permute-start.80 = (bf16[4,16,5120]{2,1,0:T(8,128)(2,1)S(1)}, bf16[4,16,5120]{2,1,0:T(8,128)(2,1)S(1)}, u32[]{:S(2)}, u32[]{:S(2)}) collective-permute-start(bf16[4,16,5120]{2,1,0:T(8,128)(2,1)S(1)} %pad_maximum_fusion.11), channel_id=1, source_target_pairs={{0,32},{33,1},{64,96},{97,65},{2,34},{35,3},{66,98},{99,67},{4,36}... | collective-permute-start | bytes 1966088 | tf_op jit(solution)/shard_map/ppermute | solution.py:1124
  493.1 9.7 %collective-permute-start.81 = (bf16[160,512]{1,0:T(8,128)(2,1)S(1)}, bf16[160,512]{1,0:T(8,128)(2,1)S(1)}, u32[]{:S(2)}, u32[]{:S(2)}) collective-permute-start(bf16[160,512]{1,0:T(8,128)(2,1)S(1)} %constant_dynamic-slice_fusion), channel_id=1, source_target_pairs={{0,0},{1,64},{32,1},{33,65},{64,32},{65,96},{96,33},{97,97},{2,2},... | collective-permute-start | bytes 491528 | tf_op jit(solution)/shard_map/ppermute | solution.py:69
  (114 other events, 1047.7 us)
Sparse Core Ops, SparseCore 0:
  19.6 61.9 all-gather.3
  83.9 76.4 all-gather.5
  163.3 47.2 all-gather.7
  241.2 81.9 reduce-scatter.2
  327.5 121.5 reduce-scatter.4

commit v4 on v3

--- a/solution.py
+++ b/solution.py
@@ -168,7 +168,7 @@
 
 
 def call(kernel, grid, in_specs, out_specs, outs, scratch, flops, *operands):
-    moved = sum(a.size * a.dtype.itemsize for a in operands)
+    moved = sum(a.size * a.dtype.itemsize for a in operands) if flops else 0
     return pl.pallas_call(
         kernel,
         grid=grid,
@@ -293,41 +293,77 @@
     )
 
 
-def head_kernel(
-    count_ref, at_ref, value_ref, base_keep, base_got, sums_ref, gain_ref, bias_ref, inside_ref, w_ref,
-    out_ref, out_sums, trunk_ref, slope_ref, steep_ref, base_out, stack_ref,
+def trunk_kernel_forward(
+    count_ref, at_ref, value_ref, base_keep, base_got, sums_ref, gain_ref, bias_ref, inside_ref,
+    trunk_ref, slope_ref, steep_ref, base_out, turned_ref,
 ):
+    mean, inverse = moments(sums_ref, count_ref[0])
+    for k, bases in enumerate((base_keep, base_got)):
+
+        @pl.loop(0, 4)
+        def _(r):
+            source = pl.ds(pl.multiple_of(r * PITCH, 16), PITCH)
+            first = at_ref[2 * k + r // 2] + (r % 2) * PITCH
+            first = pl.multiple_of(first, 16)
+            rows = pl.ds(first, PITCH)
+            inside = inside_ref[rows, :]
+            for c in range(4):
+                columns = slice(c * 512, (c + 1) * 512)
+                centred = (value_ref[rows, columns].astype(F32) - mean[:, columns]) * inverse[:, columns]
+                base = bases[source, columns]
+                base_out[rows, columns] = base
+                joined = gain_ref[:, columns] * centred + bias_ref[:, columns] + base.astype(F32)
+                level, bend, squared = gelu_parts(joined)
+                trunk = joined * level * inside
+                slope = (
+                    level + 0.5 * joined * (1.0 - bend * bend) * ROOT * (1.0 + 3.0 * CUBE * squared)
+                ) * inside
+                trunk_ref[rows, columns] = trunk.astype(BF16)
+                slope_ref[rows, columns] = slope.astype(BF16)
+                steep_ref[rows, columns] = (slope * centred).astype(BF16)
+
+    for c in range(4):
+        columns = slice(c * 512, (c + 1) * 512)
+        turned_ref[columns, :] = trunk_ref[:, columns].T
+
+
+def trunk_forward(count, at, value, base_keep, base_got, sums, gain, bias, inside):
+    rows, deep = value.shape
+    operands = (value, base_keep, base_got, sums, gain, bias, inside)
+    return call(
+        trunk_kernel_forward,
+        (1,),
+        [SCALARS, SCALARS] + [whole(a.shape) for a in operands],
+        [whole((rows, deep))] * 4 + [whole((deep, rows))],
+        [((rows, deep), BF16)] * 4 + [((deep, rows), BF16)],
+        [],
+        40 * rows * deep,
+        count,
+        at,
+        *operands,
+    )
+
+
+def head_kernel(trunk_ref, inside_ref, w_ref, out_ref, out_sums, stack_ref):
     tap = pl.program_id(0)
     rows_all = out_ref.shape[0]
 
     @pl.when(tap == 0)
     def _():
         clear_ends(stack_ref, PITCH)
-        mean, inverse = moments(sums_ref, count_ref[0])
-        for k, bases in enumerate((base_keep, base_got)):
-
-            @pl.loop(0, 4)
-            def _(r):
-                source = pl.ds(pl.multiple_of(r * PITCH, 16), PITCH)
-                first = at_ref[2 * k + r // 2] + (r % 2) * PITCH
-                first = pl.multiple_of(first, 16)
-                rows = pl.ds(first, PITCH)
-                inside = inside_ref[rows, :]
-                for c in range(4):
-                    columns = slice(c * 512, (c + 1) * 512)
-                    centred = (value_ref[rows, columns].astype(F32) - mean[:, columns]) * inverse[:, columns]
-                    base = bases[source, columns]
-                    base_out[rows, columns] = base
-                    joined = gain_ref[:, columns] * centred + bias_ref[:, columns] + base.astype(F32)
-                    level, bend, squared = gelu_parts(joined)
-                    trunk = joined * level * inside
-                    slope = (
-                        level + 0.5 * joined * (1.0 - bend * bend) * ROOT * (1.0 + 3.0 * CUBE * squared)
-                    ) * inside
-                    trunk_ref[rows, columns] = trunk.astype(BF16)
-                    slope_ref[rows, columns] = slope.astype(BF16)
-                    steep_ref[rows, columns] = (slope * centred).astype(BF16)
-                    store_moved(stack_ref, pl.multiple_of(first + PITCH, 16), trunk, 1, columns)
+
+        @pl.loop(0, 8)
+        def _(r):
+            at = pl.multiple_of(r * PITCH, 16)
+            for c in range(4):
+                columns = slice(c * 512, (c + 1) * 512)
+                store_moved(
+                    stack_ref,
+                    pl.multiple_of(at + PITCH, 16),
+                    trunk_ref[pl.ds(at, PITCH), columns].astype(F32),
+                    1,
+                    columns,
+                )
 
         out_ref[...] = jnp.zeros_like(out_ref)
 
@@ -342,22 +378,18 @@
         store_sums(out_sums, value, value * out_ref[...])
 
 
-def head_forward(count, at, value, base_keep, base_got, sums, gain, bias, inside, weights):
-    rows, deep = value.shape
-    operands = (value, base_keep, base_got, sums, gain, bias, inside)
+def head_forward(trunk, inside, weights):
+    rows, deep = trunk.shape
     return call(
         head_kernel,
         (9,),
-        [SCALARS, SCALARS]
-        + [whole(a.shape) for a in operands]
-        + [pl.BlockSpec((deep, 512), lambda t: (0, t))],
-        [whole((rows, 512)), kept((2, 512))] + [whole((rows, deep))] * 4,
-        [((rows, 512), F32), ((2, 512), F32)] + [((rows, deep), BF16)] * 4,
+        [whole((rows, deep)), whole(inside.shape), pl.BlockSpec((deep, 512), lambda t: (0, t))],
+        [whole((rows, 512)), kept((2, 512))],
+        [((rows, 512), F32), ((2, 512), F32)],
         [pltpu.VMEM((3, rows + 2 * PITCH, deep), BF16)],
         18 * rows * deep * 512,
-        count,
-        at,
-        *operands,
+        trunk,
+        inside,
         weights,
     )
 
@@ -497,19 +529,20 @@
     )
 
 
-def weight_kernel(dilation, chunk, x_ref, g_ref, *rest):
+def weight_kernel(dilation, is_turned, x_ref, g_ref, *rest):
     *more, out_ref, turned_ref, stack_ref = rest
     tap = pl.program_id(0)
-    rows = x_ref.shape[0]
+    rows = g_ref.shape[0]
+    source_ref = x_ref if is_turned else turned_ref
 
     @pl.when(tap == 0)
     def _():
-        for c in range(0, x_ref.shape[1], chunk):
-            turned_ref[c : c + chunk, :] = x_ref[:, c : c + chunk].T
+        if not is_turned:
+            turned_ref[...] = x_ref[...].T
         move_map(stack_ref, g_ref, dilation)
 
     def product(g):
-        return jnp.dot(turned_ref[...], g, preferred_element_type=F32).astype(BF16)
+        return jnp.dot(source_ref[...], g, preferred_element_type=F32).astype(BF16)
 
     @pl.when(tap < 9)
     def _():
@@ -523,18 +556,18 @@
             out_ref[...] = product(more[0][...])
 
 
-def conv_weight(image, upstream, dilation, centre=()):
-    rows, deep = image.shape
-    wide = upstream.shape[1]
+def conv_weight(image, upstream, dilation, centre=(), is_turned=False):
+    rows, wide = upstream.shape
+    deep = image.size // rows
     blocks = 9 + len(centre)
     (out,) = call(
-        functools.partial(weight_kernel, dilation, 512),
+        functools.partial(weight_kernel, dilation, is_turned),
         (blocks,),
-        [whole((rows, deep)), whole((rows, wide))] + [whole((rows, wide)) for a in centre],
+        [whole(image.shape), whole((rows, wide))] + [whole((rows, wide)) for a in centre],
         [pl.BlockSpec((deep, wide), lambda t: (0, t))],
         [((deep, blocks * wide), BF16)],
         [
-            pltpu.VMEM((deep, rows), BF16),
+            pltpu.VMEM((16, 128) if is_turned else (deep, rows), BF16),
             pltpu.VMEM((3, rows + 2 * dilation * PITCH, wide), BF16),
         ],
         2 * blocks * rows * deep * wide,
@@ -959,20 +992,13 @@
         inside_whole,
         whole_trunk,
     )
-    sums_three, near, far, task_part = hold(fold(sums_three, CORE), near, far, task_part)
+    sums_three, task_part = hold(fold(sums_three, CORE, *LINE), task_part)
     whole_task = lax.all_gather(task_part, POOL, axis=0, tiled=True)
-    across_low, across_high = across_y(near, far)
-    sums_three = fold(sums_three, *LINE)
-    sums_three, near, far, across_low, across_high = hold(
-        sums_three, near, far, across_low, across_high
-    )
-    cots_keep, cots_got = spread(cots, near, across_low, across_high, far)
     sums_three = fold(sums_three, *PLANE)
-    sums_three, cots_keep, cots_got = hold(sums_three, cots_keep, cots_got)
 
     gain_here, bias_here = of_head(head_gain, y)[None], of_head(head_bias, y)[None]
     wide_gain, wide_bias = expand_gain[None], expand_bias[None]
-    pre_head, sums_head, trunk, slope, steep, base_image = head_forward(
+    trunk, slope, steep, base_image, trunk_turned = trunk_forward(
         count_here,
         head_at,
         pre_three,
@@ -982,8 +1008,14 @@
         wide_gain,
         wide_bias,
         inside_whole,
-        whole_head,
-    )
+    )
+    trunk, near, far = hold(trunk, near, far)
+    across_low, across_high = across_y(near, far)
+    pre_head, sums_head = head_forward(trunk, inside_whole, whole_head)
+    sums_head, near, far, across_low, across_high = hold(
+        sums_head, near, far, across_low, across_high
+    )
+    cots_keep, cots_got = spread(cots, near, across_low, across_high, far)
     sums_head = fold(sums_head, CORE, *LINE, *PLANE)
     task, *streams, d_message, d_logit, d_norm_head, back_here = message_stage(
         count_here,
@@ -999,8 +1031,6 @@
         cots_keep,
         cots_got,
     )
-    task_grad, back_here = hold(conv_weight(task, d_message, 1, (d_logit,)), back_here)
-    task_share = lax.psum_scatter(task_grad, POOL, scatter_dimension=0, tiled=True)
     back_head = fold(back_here, CORE, *LINE, *PLANE)
     back_head, streams = hold(back_head, streams)
     d_pre_head = norm_back(
@@ -1008,22 +1038,19 @@
     )
     own, near, across, far = streams
     from_near, from_far = half_way(across)
-    head_grad = conv_weight(trunk, d_pre_head, 1)
+    head_grad = conv_weight(trunk_turned, d_pre_head, 1, is_turned=True)
     head_grad, d_pre_head, from_near, from_far = hold(head_grad, d_pre_head, from_near, from_far)
+    head_share = lax.psum_scatter(head_grad, POOL, scatter_dimension=0, tiled=True)
     streams = last_way(own, near, far, from_near, from_far)
     *d_trunk, back_three = trunk_back(ring_at, d_pre_head, slope, steep, whole_head)
-    d_trunk, back_three, streams, head_grad, task_share = hold(
-        d_trunk, back_three, streams, head_grad, task_share
-    )
-    head_share = lax.psum_scatter(head_grad, POOL, scatter_dimension=0, tiled=True)
+    d_trunk, back_three, streams = hold(d_trunk, back_three, streams)
     placed = jnp.where(
         jnp.arange(4)[None, :, None] == y, back_here[:, None], jnp.zeros((1, 1, 1), F32)
     ).reshape(2, -1)
     back_wide = jnp.concatenate([back_three, placed], axis=1)
     own, near, across, far = d_trunk
     from_near, from_far = half_way(across)
-    back_wide = fold(back_wide, CORE, *LINE)
-    back_wide, from_near, from_far = hold(back_wide, from_near, from_far)
+    back_wide, from_near, from_far = hold(fold(back_wide, CORE, *LINE), from_near, from_far)
     pieces = last_way(own, near, far, from_near, from_far)
     back_wide = fold(back_wide, *PLANE)
     def strip_of(value):
@@ -1042,6 +1069,7 @@
         )
 
     act_two_ring = ring_order(act_two)
+    task_grad = conv_weight(task, d_message, 1, (d_logit,))
     (
         back_wide,
         pieces,
@@ -1050,6 +1078,7 @@
         base_strip,
         inside_strip,
         act_two_ring,
+        task_grad,
     ) = hold(
         back_wide,
         pieces,
@@ -1058,7 +1087,9 @@
         base_strip,
         inside_strip,
         act_two_ring,
-    )
+        task_grad,
+    )
+    task_share = lax.psum_scatter(task_grad, POOL, scatter_dimension=0, tiled=True)
     back_wide = fold(back_wide, *RIDGE)
     back_three, back_heads = back_wide[:, :deep], back_wide[:, deep:]
     d_joined, d_three_parts, d_norm_two, back_two = joined_back(
@@ -1127,7 +1158,8 @@
     back_one = fold(back_one, CORE, *LINE)
     grad_dilated = conv_weight(act_one_image, d_two_part, 2)
     trunk_grad = jnp.concatenate([grad_expand, grad_dilated], axis=1)
-    back_one, trunk_grad, homeward = hold(back_one, trunk_grad, homeward)
+    back_one, trunk_grad, homeward, head_share = hold(back_one, trunk_grad, homeward, head_share)
+    head_pieces = to_chips(head_share)
     back_one = fold(back_one, *PLANE)
     d_pre_one = norm_back(
         d_norm_one, pre_one_image, sums_one, bottleneck_gain[0], inside_whole, back_one, count
@@ -1138,21 +1170,19 @@
     trunk_grad = jnp.concatenate(
         [trunk_grad, grad_reduce.reshape(trunk_grad.shape[0], -1)], axis=1
     )
-    trunk_grad, head_share, task_share, d_pre_one = hold(
-        trunk_grad, head_share, task_share, d_pre_one
-    )
+    trunk_grad, head_pieces, d_pre_one = hold(trunk_grad, head_pieces, d_pre_one)
     trunk_parts = shares_sent(trunk_grad, POOL)
     wide = message_weight.shape[2]
-    (sum_head,) = to_cores(to_chips(head_share), wide)
-    sum_message, sum_gate = to_cores(to_chips(task_share), wide, gate_weight.shape[2])
+    (sum_head,) = to_cores(head_pieces, wide)
     d_pre_one = sent_home(strip_of(d_pre_one))
     d_base = homeward[:, :deep].astype(F32) + times_turned(d_pre_one, whole_reduce)
     input_grad = maps_of(d_base * inside, width)
-    trunk_parts, sum_head, sum_message, sum_gate, input_grad = hold(
-        trunk_parts, sum_head, sum_message, sum_gate, input_grad
-    )
-    all_trunk, all_reduce = to_cores(
-        to_chips(parts_summed(trunk_parts)), trunk_grad.shape[1] - 512, 512
+    trunk_parts, sum_head, input_grad, task_share = hold(
+        trunk_parts, sum_head, input_grad, task_share
+    )
+    small_share = jnp.concatenate([task_share, parts_summed(trunk_parts)], axis=1)
+    sum_message, sum_gate, all_trunk, all_reduce = to_cores(
+        to_chips(small_share), wide, gate_weight.shape[2], trunk_grad.shape[1] - 512, 512
     )
     sum_expand = jnp.moveaxis(all_trunk[:, :, :512], 0, 1).reshape(channels, -1)
     sum_dilated = jnp.moveaxis(

time: 553 us -> 549 us (level)
  starting transfers between devices: 153 us -> 147 us
    ppermute x69, waiting for transfers between devices: 88.7 us -> 77.9 us  [swap(): return lax.ppermute(value, axis, [(i, i ^ flip) for i in range(count)])]
    all_to_all x1, waiting for transfers between devices: 0.01 us -> 7.16 us  [shares_sent(): lax.all_to_all(value.reshape(count, value.shape[0] // count, value.shape[...]
    ppermute x9 -> x6, starting transfers between devices: 17.7 us -> 17 us  [to_chips(): pieces.append(lax.ppermute(share, GROUP, pairs))]
  transfers between devices with their start and end apart: 93 -> 89, of which waited for: 59 -> 53; matrix products, arithmetic and copies ran while one was open for 12% -> 13% of each run, Pallas kernels for 25% -> 27%
where the time goes in v4:
time: 549 us; the launch traced here: 539 us
  Pallas kernels  169 us (31%)
  starting transfers between devices  147 us (27%)
  waiting for transfers between devices  121 us (22%)
  other arithmetic  43.4 us (8%)
  local copies, waits for them, and re-layouts  36.1 us (7%)
  between operations  15.5 us (3%)
  matrix products  7.2 us (1%)
    pallas_call x13, Pallas kernels, call(): pl.pallas_call(kernel, grid=grid, in_specs=in_specs, out_specs=out_specs,...  169 us
    ppermute x69, starting transfers between devices, swap(): return lax.ppermute(value, axis, [(i, i ^ flip) for i in range(count)])  96 us
    ppermute x69, waiting for transfers between devices, swap(): return lax.ppermute(value, axis, [(i, i ^ flip) for i in range(count)])  77.9 us
    ppermute x6, starting transfers between devices, to_chips(): pieces.append(lax.ppermute(share, GROUP, pairs))  17 us
  transfers between devices with their start and end apart: 89, of which 53 were waited for; matrix products, arithmetic and copies ran while one was open for 13% of the time, Pallas kernels for 27%

profile of v4, /device:TPU:1, one launch (start us, length us, event | category | flops | bytes accessed | tf_op | source)
XLA Modules:
  0.0 538.8 jit_solution(9448654864333332978)
XLA Ops:
  11.3 7.5 %collective-permute-done = bf16[16,8704]{1,0:T(8,128)(2,1)S(1)} collective-permute-done((bf16[16,8704]{1,0:T(8,128)(2,1)S(1)}, bf16[16,8704]{1,0:T(8,128)(2,1)S(1)}, u32[]{:S(2)}, u32[]{:S(2)}) %collective-permute-start) | collective-permute-done | bytes 278560 | tf_op jit(solution)/shard_map/ppermute | solution.py:918
  23.7 7.6 %all-to-all-start = ((bf16[16,64,512]{2,1,0:T(8,128)(2,1)}), bf16[16,64,512]{2,1,0:T(8,128)(2,1)S(1)}, u32[]{:S(2)}, u32[]{:S(2)}) async-start(bf16[16,64,512]{2,1,0:T(8,128)(2,1)} %broadcast_in_dim.56), calls=%async_computation | async-start | bytes 2097152 | tf_op jit(solution)/shard_map/all_to_all | solution.py:940
  50.7 6.4 %collective-permute-start.6 = (bf16[320,2048]{1,0:T(8,128)(2,1)}, bf16[320,2048]{1,0:T(8,128)(2,1)}, u32[]{:S(2)}, u32[]{:S(2)}) collective-permute-start(bf16[320,2048]{1,0:T(8,128)(2,1)} %get-tuple-element.263), channel_id=1, source_target_pairs={{0,32},{32,0},{1,33},{33,1},{2,34},{34,2},{3,35},{35,3},{4,36},{36... | collective-permute-start | bytes 3932168 | tf_op jit(solution)/shard_map/ppermute | solution.py:27
  77.3 3.7 collective-permute-start.12
  83.4 11.9 %shard_map.271 = (bf16[640,512]{1,0:T(8,128)(2,1)}, f32[2,512]{1,0:T(2,128)}, bf16[640,512]{1,0:T(8,128)(2,1)}, bf16[640,512]{1,0:T(8,128)(2,1)}) custom-call(f32[1]{0:T(128)} %bitcast.count_ref, s32[4]{0:T(128)} %add_multiply_fusion.1.at_ref, bf16[640,512]{1,0:T(8,128)(2,1)} %pad_maximum_fusion.7.value_ref, f32[2,512]{1,0:T(2,128)} %add.337.sums_ref.low_sums, ...), custom_call_target="tpu_custom_call" | custom-call | flops 3019898880 | bytes 7481876 | tf_op jit(solution)/shard_map/pallas_call | solution.py:172
  95.4 3.3 collective-permute-start.13
  114.7 7.3 %shard_map.272 = (bf16[640,512]{1,0:T(8,128)(2,1)}, bf16[640,2048]{1,0:T(8,128)(2,1)}, f32[2,2048]{1,0:T(2,128)}) custom-call(f32[1]{0:T(128)} %bitcast.count_ref, bf16[640,512]{1,0:T(8,128)(2,1)} %get-tuple-element.142.value_ref, f32[2,512]{1,0:T(2,128)} %add.342.sums_ref.low_sums, f32[1,512]{1,0:T(1,128)} %get-tuple-element.298.gain_ref.low_gain, ...), custom_call_target="tpu_custom_call" | custom-call | flops 1342177280 | bytes 7481860 | tf_op jit(solution)/shard_map/pallas_call | solution.py:172
  121.9 3.8 collective-permute-start.18
  145.2 14.1 %shard_map.273 = (bf16[640,2048]{1,0:T(8,128)(2,1)}, bf16[640,2048]{1,0:T(8,128)(2,1)}, bf16[640,2048]{1,0:T(8,128)(2,1)}, bf16[640,2048]{1,0:T(8,128)(2,1)}, bf16[2048,640]{1,0:T(8,128)(2,1)}) custom-call(f32[1]{0:T(128)} %bitcast.count_ref, s32[4]{0:T(128)} %add_multiply_fusion.1.at_ref, bf16[640,2048]{1,0:T(8,128)(2,1)} %get-tuple-element.145.value_ref, ...), custom_call_target="tpu_custom_call" | custom-call | flops 52428800 | bytes 5278228 | tf_op jit(solution)/shard_map/pallas_call | solution.py:172
  162.8 19.2 %shard_map.274 = (f32[640,512]{1,0:T(8,128)}, f32[2,512]{1,0:T(2,128)}) custom-call(bf16[640,2048]{1,0:T(8,128)(2,1)} %get-tuple-element.153.trunk_ref, f32[640,1]{1,0:T(8,128)} %fusion.18.inside_ref, bf16[2048,4608]{1,0:T(8,128)(2,1)} %all-gather.6.cloned.1.call-done.w_ref), custom_call_target="tpu_custom_call" | custom-call | flops 12079595520 | bytes 21498368 | tf_op jit(solution)/shard_map/pallas_call | solution.py:172
  183.3 4.4 collective-permute-start.33
  203.5 6.4 %all-gather.8.cloned.1.call-done.w_ref = bf16[512,5120]{1,0:T(8,128)(2,1)} async-done(((bf16[16,5120]{1,0:T(8,128)(2,1)}), bf16[512,5120]{1,0:T(8,128)(2,1)}) %all-gather.8.cloned.1.call-update) | async-done | bytes 5242896 | tf_op jit(solution)/shard_map/all_gather | solution.py:996
  210.7 20.8 %shard_map.275 = (bf16[640,512]{1,0:T(8,128)(2,1)}, bf16[160,1024]{1,0:T(8,128)(2,1)}, bf16[160,1024]{1,0:T(8,128)(2,1)}, bf16[160,1024]{1,0:T(8,128)(2,1)}, bf1...) custom-call(f32[1]{0:T(128)} %bitcast.count_ref, ...), custom_call_target="tpu_custom_call" | custom-call | flops 6710886400 | bytes 7875112 | tf_op jit(solution)/shard_map/pallas_call | solution.py:172
  250.1 3.3 multiply_convert_fusion.1.g_ref
  253.4 20.1 %shard_map.276 = bf16[2048,4608]{1,0:T(8,128)(2,1)} custom-call(bf16[2048,640]{1,0:T(8,128)(2,1)} %get-tuple-element.149.x_ref, bf16[640,512]{1,0:T(8,128)(2,1)} %multiply_convert_fusion.1.g_ref), custom_call_target="tpu_custom_call" | custom-call | flops 12079595520 | bytes 3276800 | tf_op jit(solution)/shard_map/pallas_call | solution.py:172
  277.4 29.8 %shard_map.277 = (bf16[160,2048]{1,0:T(8,128)(2,1)}, bf16[160,2048]{1,0:T(8,128)(2,1)}, bf16[160,2048]{1,0:T(8,128)(2,1)}, bf16[160,2048]{1,0:T(8,128)(2,1)}, f32[2,2048]{1,0:T(2,128)}) custom-call(s32[4]{0:T(128)} %get-tuple-element.261.ring_ref.at_ref, bf16[640,512]{1,0:T(8,128)(2,1)} %multiply_convert_fusion.1.g_ref, ...), custom_call_target="tpu_custom_call" | custom-call | flops 12079595520 | bytes 24772624 | tf_op jit(solution)/shard_map/pallas_call | solution.py:172
  308.0 6.5 %collective-permute-start.43 = (f32[2,4096]{1,0:T(2,128)S(1)}, f32[2,4096]{1,0:T(2,128)S(1)}, u32[]{:S(2)}, u32[]{:S(2)}) collective-permute-start(f32[2,4096]{1,0:T(2,128)S(1)} %pad_maximum_fusion.16), channel_id=1, source_target_pairs={{0,32},{32,0},{1,33},{33,1},{2,34},{34,2},{3,35},{35,3},{4,36},{36... | collective-permute-start | bytes 98312 | tf_op jit(solution)/shard_map/ppermute | solution.py:27
  338.3 9.9 %shard_map.278 = bf16[512,5120]{1,0:T(8,128)(2,1)} custom-call(bf16[640,512]{1,0:T(8,128)(2,1)} %get-tuple-element.196.x_ref, bf16[640,512]{1,0:T(8,128)(2,1)} %get-tuple-element.197.g_ref, bf16[640,512]{1,0:T(8,128)(2,1)} %get-tuple-element.198.rest_0_), custom_call_target="tpu_custom_call" | custom-call | flops 3355443200 | bytes 1966080 | tf_op jit(solution)/shard_map/pallas_call | solution.py:172
  353.5 3.5 collective-permute-done.53
  357.6 6.7 %shard_map.279 = (bf16[160,2048]{1,0:T(8,128)(2,1)}, bf16[160,512]{1,0:T(8,128)(2,1)}, bf16[160,512]{1,0:T(8,128)(2,1)}, bf16[160,512]{1,0:T(8,128)(2,1)}, bf16[...) custom-call(f32[1]{0:T(128)} %bitcast.count_ref, s32[4]{0:T(128)} %get-tuple-element.261.ring_ref.at_ref, ...), custom_call_target="tpu_custom_call" | custom-call | flops 335544320 | bytes 10314388 | tf_op jit(solution)/shard_map/pallas_call | solution.py:172
  368.2 5.0 collective-permute-start.54
  377.8 3.5 collective-permute-done.56
  396.8 6.9 %collective-permute-start.70 = (bf16[160,3072]{1,0:T(8,128)(2,1)S(1)}, bf16[160,3072]{1,0:T(8,128)(2,1)}, u32[]{:S(2)}, u32[]{:S(2)}) collective-permute-start(bf16[160,3072]{1,0:T(8,128)(2,1)S(1)} %pad_maximum_fusion.5), channel_id=1, source_target_pairs={{0,0},{1,64},{32,1},{33,65},{64,32},{65,96},{96,33},{97,97},{2,2},... | collective-permute-start | bytes 2949128 | tf_op jit(solution)/shard_map/ppermute | solution.py:69
  403.8 14.6 %shard_map.280 = (bf16[640,512]{1,0:T(8,128)(2,1)}, f32[2,512]{1,0:T(2,128)}, bf16[640,128]{1,0:T(8,128)(2,1)}) custom-call(f32[1]{0:T(128)} %bitcast.count_ref, s32[4]{0:T(128)} %get-tuple-element.261.ring_ref.at_ref, bf16[160,512]{1,0:T(8,128)(2,1)} %get-tuple-element.209.u0, bf16[160,512]{1,0:T(8,128)(2,1)} %copy-done.50, bf16[160,512]{1,0:T(8,128)(2,1)} %copy-done.51, ...), custom_call_target="tpu_custom_call" | custom-call | flops 3019898880 | bytes 8802836 | tf_op jit(solution)/shard_map/pallas_call | solution.py:172
  420.5 6.5 %shard_map.281 = bf16[512,1152]{1,0:T(8,128)(2,1)} custom-call(bf16[640,512]{1,0:T(8,128)(2,1)} %get-tuple-element.224.x_ref, bf16[640,128]{1,0:T(8,128)(2,1)} %get-tuple-element.225.g_ref), custom_call_target="tpu_custom_call" | custom-call | flops 754974720 | bytes 819200 | tf_op jit(solution)/shard_map/pallas_call | solution.py:172
  438.0 5.9 %collective-permute-start.74 = (bf16[64,4608]{1,0:T(8,128)(2,1)}, bf16[64,4608]{1,0:T(8,128)(2,1)}, u32[]{:S(2)}, u32[]{:S(2)}) collective-permute-start(bf16[64,4608]{1,0:T(8,128)(2,1)} %reduce-scatter.3.cloned.1.call-done.refs_0_), channel_id=1, source_target_pairs={{1,0},{32,33},{65,64},{96,97},{3,2},{34,35},{67,66},{98,99},{5,4},... | collective-permute-start | bytes 1769480 | tf_op jit(solution)/shard_map/ppermute | solution.py:1147
  462.2 9.7 %all-to-all-start.1 = ((bf16[32,16,2176]{2,1,0:T(8,128)(2,1)}), bf16[32,16,2176]{2,1,0:T(8,128)(2,1)S(1)}, u32[]{:S(2)}, u32[]{:S(2)}) async-start(bf16[32,16,2176]{2,1,0:T(8,128)(2,1)} %bitcast.42), calls=%async_computation.2 | async-start | bytes 4456448 | tf_op jit(solution)/shard_map/all_to_all | solution.py:858
  476.1 3.8 collective-permute-done.77
  483.6 5.0 shard_map.282
  488.5 7.7 %reduce-scatter.5.cloned.1.call-done = bf16[16,5120]{1,0:T(8,128)(2,1)} async-done(((bf16[512,5120]{1,0:T(8,128)(2,1)}), bf16[16,5120]{1,0:T(8,128)(2,1)}) %reduce-scatter.5.cloned.1.call-update) | async-done | bytes 163856 | tf_op jit(solution)/shard_map/reduce_scatter | solution.py:1092
  496.2 7.2 %all-to-all-done.1 = bf16[32,16,2176]{2,1,0:T(8,128)(2,1)S(1)} async-done(((bf16[32,16,2176]{2,1,0:T(8,128)(2,1)}), bf16[32,16,2176]{2,1,0:T(8,128)(2,1)S(1)}, u32[]{:S(2)}, u32[]{:S(2)}) %all-to-all-start.1) | async-done | bytes 2228256 | tf_op jit(solution)/shard_map/all_to_all | solution.py:858
  504.4 5.3 collective-permute-start.79
  (432 shorter events, 246.3 us)
Async XLA Ops:
  7.2 76.2 %all-gather.4.cloned.1.call-start = ((), (), s32[]{:S(2)}) async-start(), calls=%async_computation.4 | async-start | bytes 7028736 | tf_op jit(solution)/shard_map/all_gather | solution.py:944
  21.7 14.6 %collective-permute-start.2 = (bf16[160,2048]{1,0:T(8,128)(2,1)S(1)}, bf16[160,2048]{1,0:T(8,128)(2,1)S(1)}, u32[]{:S(2)}, u32[]{:S(2)}) collective-permute-start(bf16[160,2048]{1,0:T(8,128)(2,1)S(1)} %bitcast_multiply_fusion), channel_id=1, source_target_pairs={{0,64},{1,65},{64,0},{65,1},{2,66},{3,67},{66,2},{67,3},{4,68},{5,... | collective-permute-start | bytes 1966088 | tf_op jit(solution)/shard_map/ppermute | solution.py:27
  22.4 15.8 %collective-permute-start.3 = (bf16[160,2048]{1,0:T(8,128)(2,1)S(1)}, bf16[160,2048]{1,0:T(8,128)(2,1)S(1)}, u32[]{:S(2)}, u32[]{:S(2)}) collective-permute-start(bf16[160,2048]{1,0:T(8,128)(2,1)S(1)} %bitcast_multiply_fusion), channel_id=1, source_target_pairs={{0,65},{1,64},{64,1},{65,0},{2,67},{3,66},{66,3},{67,2},{4,69},{5,... | collective-permute-start | bytes 1966088 | tf_op jit(solution)/shard_map/ppermute | solution.py:27
  23.7 33.4 %all-to-all-start = ((bf16[16,64,512]{2,1,0:T(8,128)(2,1)}), bf16[16,64,512]{2,1,0:T(8,128)(2,1)S(1)}, u32[]{:S(2)}, u32[]{:S(2)}) async-start(bf16[16,64,512]{2,1,0:T(8,128)(2,1)} %broadcast_in_dim.56), calls=%async_computation | async-start | bytes 2097152 | tf_op jit(solution)/shard_map/all_to_all | solution.py:940
  31.3 131.5 %all-gather.6.cloned.1.call-start = ((), (), s32[]{:S(2)}) async-start(), calls=%async_computation.5 | async-start | bytes 19464192 | tf_op jit(solution)/shard_map/all_gather | solution.py:959
  41.6 15.6 %collective-permute-start.7 = (bf16[64,4608]{1,0:T(8,128)(2,1)}, bf16[64,4608]{1,0:T(8,128)(2,1)}, u32[]{:S(2)}, u32[]{:S(2)}) collective-permute-start(bf16[64,4608]{1,0:T(8,128)(2,1)} %dynamic-slice_bitcast_fusion), channel_id=1, source_target_pairs={{0,65},{33,96},{64,1},{97,32},{2,67},{35,98},{66,3},{99,34},{4,69}... | collective-permute-start | bytes 1769480 | tf_op jit(solution)/shard_map/ppermute | solution.py:918
  61.7 148.2 %all-gather.8.cloned.1.call-start = ((), (), s32[]{:S(2)}) async-start(), calls=%async_computation.6 | async-start | bytes 5406720 | tf_op jit(solution)/shard_map/all_gather | solution.py:996
  112.5 23.0 %collective-permute-start.21 = (bf16[16,5120]{1,0:T(8,128)(2,1)S(1)}, bf16[16,5120]{1,0:T(8,128)(2,1)S(1)}, u32[]{:S(2)}, u32[]{:S(2)}) collective-permute-start(bf16[16,5120]{1,0:T(8,128)(2,1)S(1)} %dynamic-slice_bitcast_fusion.1), channel_id=1, source_target_pairs={{0,65},{33,96},{64,1},{97,32},{2,67},{35,98},{66,3},{99,34},{4,69}... | collective-permute-start | bytes 491528 | tf_op jit(solution)/shard_map/ppermute | solution.py:918
  136.2 295.5 %reduce-scatter.3.cloned.1.call-start = ((), (), s32[]{:S(2)}) async-start(), calls=%async_computation.7 | async-start | bytes 19464192 | tf_op jit(solution)/shard_map/reduce_scatter | solution.py:1043
  136.4 22.9 %collective-permute-start.24 = (bf16[160,1024]{1,0:T(8,128)(2,1)S(1)}, bf16[160,1024]{1,0:T(8,128)(2,1)S(1)}, u32[]{:S(2)}, u32[]{:S(2)}) collective-permute-start(bf16[160,1024]{1,0:T(8,128)(2,1)S(1)} %pad_maximum_fusion.12), channel_id=1, source_target_pairs={{0,64},{1,65},{64,0},{65,1},{2,66},{3,67},{66,2},{67,3},{4,68},{5,... | collective-permute-start | bytes 983048 | tf_op jit(solution)/shard_map/ppermute | solution.py:27
  136.5 22.8 %collective-permute-start.25 = (bf16[160,1024]{1,0:T(8,128)(2,1)S(1)}, bf16[160,1024]{1,0:T(8,128)(2,1)S(1)}, u32[]{:S(2)}, u32[]{:S(2)}) collective-permute-start(bf16[160,1024]{1,0:T(8,128)(2,1)S(1)} %pad_maximum_fusion.12), channel_id=1, source_target_pairs={{0,65},{1,64},{64,1},{65,0},{2,67},{3,66},{66,3},{67,2},{4,69},{5,... | collective-permute-start | bytes 983048 | tf_op jit(solution)/shard_map/ppermute | solution.py:27
  159.3 22.7 %collective-permute-start.26 = (bf16[80,1024]{1,0:T(8,128)(2,1)S(1)}, bf16[80,1024]{1,0:T(8,128)(2,1)S(1)}, u32[]{:S(2)}, u32[]{:S(2)}) collective-permute-start(bf16[80,1024]{1,0:T(8,128)(2,1)S(1)} %slice.178), channel_id=1, source_target_pairs={{0,64},{1,65},{64,0},{65,1},{2,66},{3,67},{66,2},{67,3},{4,68},{5,... | collective-permute-start | bytes 491528 | tf_op jit(solution)/shard_map/ppermute | solution.py:27
  160.7 21.3 %collective-permute-start.27 = (bf16[80,1024]{1,0:T(8,128)(2,1)S(1)}, bf16[80,1024]{1,0:T(8,128)(2,1)S(1)}, u32[]{:S(2)}, u32[]{:S(2)}) collective-permute-start(bf16[80,1024]{1,0:T(8,128)(2,1)S(1)} %slice.179), channel_id=1, source_target_pairs={{0,65},{1,64},{64,1},{65,0},{2,67},{3,66},{66,3},{67,2},{4,69},{5,... | collective-permute-start | bytes 491528 | tf_op jit(solution)/shard_map/ppermute | solution.py:27
  183.3 26.6 %collective-permute-start.33 = (bf16[320,1024]{1,0:T(8,128)(2,1)S(1)}, bf16[320,1024]{1,0:T(8,128)(2,1)S(1)}, u32[]{:S(2)}, u32[]{:S(2)}) collective-permute-start(bf16[320,1024]{1,0:T(8,128)(2,1)S(1)} %get-tuple-element.267), channel_id=1, source_target_pairs={{0,32},{32,0},{1,33},{33,1},{2,34},{34,2},{3,35},{35,3},{4,36},{36... | collective-permute-start | bytes 1966088 | tf_op jit(solution)/shard_map/ppermute | solution.py:27
  246.9 26.6 %collective-permute-start.39 = (bf16[80,1024]{1,0:T(8,128)(2,1)S(1)}, bf16[80,1024]{1,0:T(8,128)(2,1)S(1)}, u32[]{:S(2)}, u32[]{:S(2)}) collective-permute-start(bf16[80,1024]{1,0:T(8,128)(2,1)S(1)} %get-tuple-element.278), channel_id=1, source_target_pairs={{0,64},{1,65},{64,0},{65,1},{2,66},{3,67},{66,2},{67,3},{4,68},{5,... | collective-permute-start | bytes 491528 | tf_op jit(solution)/shard_map/ppermute | solution.py:27
  248.3 25.2 %collective-permute-start.40 = (bf16[80,1024]{1,0:T(8,128)(2,1)S(1)}, bf16[80,1024]{1,0:T(8,128)(2,1)S(1)}, u32[]{:S(2)}, u32[]{:S(2)}) collective-permute-start(bf16[80,1024]{1,0:T(8,128)(2,1)S(1)} %get-tuple-element.277), channel_id=1, source_target_pairs={{0,65},{1,64},{64,1},{65,0},{2,67},{3,66},{66,3},{67,2},{4,69},{5,... | collective-permute-start | bytes 491528 | tf_op jit(solution)/shard_map/ppermute | solution.py:27
  273.5 222.7 %reduce-scatter.5.cloned.1.call-start = ((), (), s32[]{:S(2)}) async-start(), calls=%async_computation.8 | async-start | bytes 5406720 | tf_op jit(solution)/shard_map/reduce_scatter | solution.py:1092
  276.1 31.1 %collective-permute-start.42 = (bf16[160,1024]{1,0:T(8,128)(2,1)S(1)}, bf16[160,1024]{1,0:T(8,128)(2,1)S(1)}, u32[]{:S(2)}, u32[]{:S(2)}) collective-permute-start(bf16[160,1024]{1,0:T(8,128)(2,1)S(1)} %pad_maximum_fusion.14), channel_id=1, source_target_pairs={{0,65},{1,64},{64,1},{65,0},{2,67},{3,66},{66,3},{67,2},{4,69},{5,... | collective-permute-start | bytes 983048 | tf_op jit(solution)/shard_map/ppermute | solution.py:27
  277.2 30.1 %collective-permute-start.41 = (bf16[160,1024]{1,0:T(8,128)(2,1)S(1)}, bf16[160,1024]{1,0:T(8,128)(2,1)S(1)}, u32[]{:S(2)}, u32[]{:S(2)}) collective-permute-start(bf16[160,1024]{1,0:T(8,128)(2,1)S(1)} %pad_maximum_fusion.13), channel_id=1, source_target_pairs={{0,64},{1,65},{64,0},{65,1},{2,66},{3,67},{66,2},{67,3},{4,68},{5,... | collective-permute-start | bytes 983048 | tf_op jit(solution)/shard_map/ppermute | solution.py:27
  328.4 19.8 %collective-permute-start.51 = (bf16[160,2048]{1,0:T(8,128)(2,1)}, bf16[160,2048]{1,0:T(8,128)(2,1)S(1)}, u32[]{:S(2)}, u32[]{:S(2)}) collective-permute-start(bf16[160,2048]{1,0:T(8,128)(2,1)} %pad_maximum_fusion.10), channel_id=1, source_target_pairs={{0,65},{1,64},{64,1},{65,0},{2,67},{3,66},{66,3},{67,2},{4,69},{5,... | collective-permute-start | bytes 1966088 | tf_op jit(solution)/shard_map/ppermute | solution.py:27
  331.3 17.0 %collective-permute-start.50 = (bf16[160,2048]{1,0:T(8,128)(2,1)}, bf16[160,2048]{1,0:T(8,128)(2,1)}, u32[]{:S(2)}, u32[]{:S(2)}) collective-permute-start(bf16[160,2048]{1,0:T(8,128)(2,1)} %pad_maximum_fusion.9), channel_id=1, source_target_pairs={{0,64},{1,65},{64,0},{65,1},{2,66},{3,67},{66,2},{67,3},{4,68},{5,... | collective-permute-start | bytes 1966088 | tf_op jit(solution)/shard_map/ppermute | solution.py:27
  336.0 12.2 %collective-permute-start.49 = (f32[2,4096]{1,0:T(2,128)S(1)}, f32[2,4096]{1,0:T(2,128)S(1)}, u32[]{:S(2)}, u32[]{:S(2)}) collective-permute-start(f32[2,4096]{1,0:T(2,128)S(1)} %add.370), channel_id=1, source_target_pairs={{0,6},{2,4},{4,2},{6,0},{1,7},{3,5},{5,3},{7,1},{8,14},{10,12},{12... | collective-permute-start | bytes 98312 | tf_op jit(solution)/shard_map/ppermute | solution.py:27
  364.2 17.1 %collective-permute-start.57 = (bf16[160,512]{1,0:T(8,128)(2,1)}, bf16[160,512]{1,0:T(8,128)(2,1)S(1)}, u32[]{:S(2)}, u32[]{:S(2)}) collective-permute-start(bf16[160,512]{1,0:T(8,128)(2,1)} %get-tuple-element.209.u0), channel_id=1, source_target_pairs={{0,64},{1,65},{64,0},{65,1},{2,66},{3,67},{66,2},{67,3},{4,68},{5,... | collective-permute-start | bytes 491528 | tf_op jit(solution)/shard_map/ppermute | solution.py:27
  364.6 16.8 %collective-permute-start.58 = (bf16[160,512]{1,0:T(8,128)(2,1)}, bf16[160,512]{1,0:T(8,128)(2,1)S(1)}, u32[]{:S(2)}, u32[]{:S(2)}) collective-permute-start(bf16[160,512]{1,0:T(8,128)(2,1)} %get-tuple-element.209.u0), channel_id=1, source_target_pairs={{0,1},{1,0},{64,65},{65,64},{2,3},{3,2},{66,67},{67,66},{4,5},{5,4... | collective-permute-start | bytes 491528 | tf_op jit(solution)/shard_map/ppermute | solution.py:27
  366.4 14.9 %collective-permute-start.59 = (bf16[160,512]{1,0:T(8,128)(2,1)}, bf16[160,512]{1,0:T(8,128)(2,1)S(1)}, u32[]{:S(2)}, u32[]{:S(2)}) collective-permute-start(bf16[160,512]{1,0:T(8,128)(2,1)} %get-tuple-element.209.u0), channel_id=1, source_target_pairs={{0,65},{1,64},{64,1},{65,0},{2,67},{3,66},{66,3},{67,2},{4,69},{5,... | collective-permute-start | bytes 491528 | tf_op jit(solution)/shard_map/ppermute | solution.py:27
  396.8 34.8 %collective-permute-start.70 = (bf16[160,3072]{1,0:T(8,128)(2,1)S(1)}, bf16[160,3072]{1,0:T(8,128)(2,1)}, u32[]{:S(2)}, u32[]{:S(2)}) collective-permute-start(bf16[160,3072]{1,0:T(8,128)(2,1)S(1)} %pad_maximum_fusion.5), channel_id=1, source_target_pairs={{0,0},{1,64},{32,1},{33,65},{64,32},{65,96},{96,33},{97,97},{2,2},... | collective-permute-start | bytes 2949128 | tf_op jit(solution)/shard_map/ppermute | solution.py:69
  434.5 11.4 %collective-permute-start.72 = (f32[2,512]{1,0:T(2,128)S(1)}, f32[2,512]{1,0:T(2,128)S(1)}, u32[]{:S(2)}, u32[]{:S(2)}) collective-permute-start(f32[2,512]{1,0:T(2,128)S(1)} %add.393), channel_id=1, source_target_pairs={{0,6},{2,4},{4,2},{6,0},{1,7},{3,5},{5,3},{7,1},{8,14},{10,12},{12... | collective-permute-start | bytes 12296 | tf_op jit(solution)/shard_map/ppermute | solution.py:27
  436.5 17.0 %collective-permute-start.73 = (bf16[64,4608]{1,0:T(8,128)(2,1)}, bf16[64,4608]{1,0:T(8,128)(2,1)}, u32[]{:S(2)}, u32[]{:S(2)}) collective-permute-start(bf16[64,4608]{1,0:T(8,128)(2,1)} %reduce-scatter.3.cloned.1.call-done.refs_0_), channel_id=1, source_target_pairs={{0,64},{33,97},{64,0},{97,33},{2,66},{35,99},{66,2},{99,35},{4,68}... | collective-permute-start | bytes 1769480 | tf_op jit(solution)/shard_map/ppermute | solution.py:1147
  438.0 16.8 %collective-permute-start.74 = (bf16[64,4608]{1,0:T(8,128)(2,1)}, bf16[64,4608]{1,0:T(8,128)(2,1)}, u32[]{:S(2)}, u32[]{:S(2)}) collective-permute-start(bf16[64,4608]{1,0:T(8,128)(2,1)} %reduce-scatter.3.cloned.1.call-done.refs_0_), channel_id=1, source_target_pairs={{1,0},{32,33},{65,64},{96,97},{3,2},{34,35},{67,66},{98,99},{5,4},... | collective-permute-start | bytes 1769480 | tf_op jit(solution)/shard_map/ppermute | solution.py:1147
  443.9 13.9 %collective-permute-start.75 = (bf16[64,4608]{1,0:T(8,128)(2,1)}, bf16[64,4608]{1,0:T(8,128)(2,1)}, u32[]{:S(2)}, u32[]{:S(2)}) collective-permute-start(bf16[64,4608]{1,0:T(8,128)(2,1)} %reduce-scatter.3.cloned.1.call-done.refs_0_), channel_id=1, source_target_pairs={{1,64},{32,97},{65,0},{96,33},{3,66},{34,99},{67,2},{98,35},{5,68}... | collective-permute-start | bytes 1769480 | tf_op jit(solution)/shard_map/ppermute | solution.py:1147
  461.0 22.6 %collective-permute-start.76 = (bf16[4,64,4608]{2,1,0:T(8,128)(2,1)}, bf16[4,64,4608]{2,1,0:T(8,128)(2,1)}, u32[]{:S(2)}, u32[]{:S(2)}) collective-permute-start(bf16[4,64,4608]{2,1,0:T(8,128)(2,1)} %pad_maximum_fusion), channel_id=1, source_target_pairs={{0,32},{33,1},{64,96},{97,65},{2,34},{35,3},{66,98},{99,67},{4,36}... | collective-permute-start | bytes 7077896 | tf_op jit(solution)/shard_map/ppermute | solution.py:1155
  462.2 41.1 %all-to-all-start.1 = ((bf16[32,16,2176]{2,1,0:T(8,128)(2,1)}), bf16[32,16,2176]{2,1,0:T(8,128)(2,1)S(1)}, u32[]{:S(2)}, u32[]{:S(2)}) async-start(bf16[32,16,2176]{2,1,0:T(8,128)(2,1)} %bitcast.42), calls=%async_computation.2 | async-start | bytes 4456448 | tf_op jit(solution)/shard_map/all_to_all | solution.py:858
  (111 other events, 1144.0 us)
Sparse Core Ops, SparseCore 0:
  19.6 61.2 all-gather.3
  83.2 76.8 all-gather.5
  162.9 46.9 all-gather.7
  273.6 122.2 reduce-scatter.2
  400.0 96.1 reduce-scatter.4

commit v5 on v4

--- a/solution.py
+++ b/solution.py
@@ -1170,16 +1170,14 @@
     trunk_grad = jnp.concatenate(
         [trunk_grad, grad_reduce.reshape(trunk_grad.shape[0], -1)], axis=1
     )
-    trunk_grad, head_pieces, d_pre_one = hold(trunk_grad, head_pieces, d_pre_one)
+    trunk_grad, d_pre_one = hold(trunk_grad, d_pre_one)
     trunk_parts = shares_sent(trunk_grad, POOL)
     wide = message_weight.shape[2]
-    (sum_head,) = to_cores(head_pieces, wide)
     d_pre_one = sent_home(strip_of(d_pre_one))
     d_base = homeward[:, :deep].astype(F32) + times_turned(d_pre_one, whole_reduce)
     input_grad = maps_of(d_base * inside, width)
-    trunk_parts, sum_head, input_grad, task_share = hold(
-        trunk_parts, sum_head, input_grad, task_share
-    )
+    trunk_parts, head_pieces, input_grad = hold(trunk_parts, head_pieces, input_grad)
+    (sum_head,) = to_cores(head_pieces, wide)
     small_share = jnp.concatenate([task_share, parts_summed(trunk_parts)], axis=1)
     sum_message, sum_gate, all_trunk, all_reduce = to_cores(
         to_chips(small_share), wide, gate_weight.shape[2], trunk_grad.shape[1] - 512, 512

time: 549 us -> 562 us (1.024)
  waiting for transfers between devices: 121 us -> 129 us
    reduce_scatter x1, waiting for transfers between devices: 7.67 us -> 18.3 us  [shards(): lax.psum_scatter(task_grad, POOL, scatter_dimension=0, tiled=True)]
    ppermute x6, waiting for transfers between devices: 7.49 us -> 0.02 us  [to_chips(): pieces.append(lax.ppermute(share, GROUP, pairs))]
  transfers between devices with their start and end apart: 89 -> 89, of which waited for: 53 -> 50; matrix products, arithmetic and copies ran while one was open for 13% -> 14% of each run, Pallas kernels for 27% -> 26%
where the time goes in v5:
time: 562 us; the launch traced here: 552 us
  Pallas kernels  168 us (30%)
  starting transfers between devices  147 us (26%)
  waiting for transfers between devices  129 us (23%)
  other arithmetic  46.5 us (8%)
  local copies, waits for them, and re-layouts  37.3 us (7%)
  between operations  15.5 us (3%)
  matrix products  8.15 us (1%)
    pallas_call x13, Pallas kernels, call(): pl.pallas_call(kernel, grid=grid, in_specs=in_specs, out_specs=out_specs,...  168 us
    ppermute x69, starting transfers between devices, swap(): return lax.ppermute(value, axis, [(i, i ^ flip) for i in range(count)])  95.5 us
    ppermute x69, waiting for transfers between devices, swap(): return lax.ppermute(value, axis, [(i, i ^ flip) for i in range(count)])  80.2 us
    ppermute x6, starting transfers between devices, to_chips(): pieces.append(lax.ppermute(share, GROUP, pairs))  19.6 us
    reduce_scatter x1, waiting for transfers between devices, shards(): lax.psum_scatter(task_grad, POOL, scatter_dimension=0, tiled=True)  18.3 us
  transfers between devices with their start and end apart: 89, of which 50 were waited for; matrix products, arithmetic and copies ran while one was open for 14% of the time, Pallas kernels for 26%

profile of v5, /device:TPU:1, one launch (start us, length us, event | category | flops | bytes accessed | tf_op | source)
XLA Modules:
  0.0 552.1 jit_solution(7891506469039375237)
XLA Ops:
  11.3 7.5 %collective-permute-done = bf16[16,8704]{1,0:T(8,128)(2,1)S(1)} collective-permute-done((bf16[16,8704]{1,0:T(8,128)(2,1)S(1)}, bf16[16,8704]{1,0:T(8,128)(2,1)S(1)}, u32[]{:S(2)}, u32[]{:S(2)}) %collective-permute-start) | collective-permute-done | bytes 278560 | tf_op jit(solution)/shard_map/ppermute | solution.py:918
  23.7 7.6 %all-to-all-start = ((bf16[16,64,512]{2,1,0:T(8,128)(2,1)}), bf16[16,64,512]{2,1,0:T(8,128)(2,1)S(1)}, u32[]{:S(2)}, u32[]{:S(2)}) async-start(bf16[16,64,512]{2,1,0:T(8,128)(2,1)} %broadcast_in_dim.56), calls=%async_computation | async-start | bytes 2097152 | tf_op jit(solution)/shard_map/all_to_all | solution.py:940
  50.7 6.4 %collective-permute-start.6 = (bf16[320,2048]{1,0:T(8,128)(2,1)}, bf16[320,2048]{1,0:T(8,128)(2,1)}, u32[]{:S(2)}, u32[]{:S(2)}) collective-permute-start(bf16[320,2048]{1,0:T(8,128)(2,1)} %get-tuple-element.259), channel_id=1, source_target_pairs={{0,32},{32,0},{1,33},{33,1},{2,34},{34,2},{3,35},{35,3},{4,36},{36... | collective-permute-start | bytes 3932168 | tf_op jit(solution)/shard_map/ppermute | solution.py:27
  77.3 3.7 collective-permute-start.12
  83.4 11.9 %shard_map.271 = (bf16[640,512]{1,0:T(8,128)(2,1)}, f32[2,512]{1,0:T(2,128)}, bf16[640,512]{1,0:T(8,128)(2,1)}, bf16[640,512]{1,0:T(8,128)(2,1)}) custom-call(f32[1]{0:T(128)} %bitcast.count_ref, s32[4]{0:T(128)} %add_multiply_fusion.1.at_ref, bf16[640,512]{1,0:T(8,128)(2,1)} %pad_maximum_fusion.7.value_ref, f32[2,512]{1,0:T(2,128)} %add.337.sums_ref.low_sums, ...), custom_call_target="tpu_custom_call" | custom-call | flops 3019898880 | bytes 7481876 | tf_op jit(solution)/shard_map/pallas_call | solution.py:172
  95.3 3.3 collective-permute-start.13
  114.6 7.2 %shard_map.272 = (bf16[640,512]{1,0:T(8,128)(2,1)}, bf16[640,2048]{1,0:T(8,128)(2,1)}, f32[2,2048]{1,0:T(2,128)}) custom-call(f32[1]{0:T(128)} %bitcast.count_ref, bf16[640,512]{1,0:T(8,128)(2,1)} %get-tuple-element.140.value_ref, f32[2,512]{1,0:T(2,128)} %add.342.sums_ref.low_sums, f32[1,512]{1,0:T(1,128)} %get-tuple-element.294.gain_ref.low_gain, ...), custom_call_target="tpu_custom_call" | custom-call | flops 1342177280 | bytes 7481860 | tf_op jit(solution)/shard_map/pallas_call | solution.py:172
  121.8 3.8 collective-permute-start.18
  136.6 3.3 collective-permute-done.22
  145.1 14.1 %shard_map.273 = (bf16[640,2048]{1,0:T(8,128)(2,1)}, bf16[640,2048]{1,0:T(8,128)(2,1)}, bf16[640,2048]{1,0:T(8,128)(2,1)}, bf16[640,2048]{1,0:T(8,128)(2,1)}, bf16[2048,640]{1,0:T(8,128)(2,1)}) custom-call(f32[1]{0:T(128)} %bitcast.count_ref, s32[4]{0:T(128)} %add_multiply_fusion.1.at_ref, bf16[640,2048]{1,0:T(8,128)(2,1)} %get-tuple-element.143.value_ref, ...), custom_call_target="tpu_custom_call" | custom-call | flops 52428800 | bytes 5278228 | tf_op jit(solution)/shard_map/pallas_call | solution.py:172
  162.7 19.2 %shard_map.274 = (f32[640,512]{1,0:T(8,128)}, f32[2,512]{1,0:T(2,128)}) custom-call(bf16[640,2048]{1,0:T(8,128)(2,1)} %get-tuple-element.151.trunk_ref, f32[640,1]{1,0:T(8,128)} %fusion.18.inside_ref, bf16[2048,4608]{1,0:T(8,128)(2,1)} %all-gather.6.cloned.1.call-done.w_ref), custom_call_target="tpu_custom_call" | custom-call | flops 12079595520 | bytes 21498368 | tf_op jit(solution)/shard_map/pallas_call | solution.py:172
  183.1 4.3 collective-permute-start.33
  203.3 6.8 %all-gather.8.cloned.1.call-done.w_ref = bf16[512,5120]{1,0:T(8,128)(2,1)} async-done(((bf16[16,5120]{1,0:T(8,128)(2,1)}), bf16[512,5120]{1,0:T(8,128)(2,1)}) %all-gather.8.cloned.1.call-update) | async-done | bytes 5242896 | tf_op jit(solution)/shard_map/all_gather | solution.py:996
  210.9 20.8 %shard_map.275 = (bf16[640,512]{1,0:T(8,128)(2,1)}, bf16[160,1024]{1,0:T(8,128)(2,1)}, bf16[160,1024]{1,0:T(8,128)(2,1)}, bf16[160,1024]{1,0:T(8,128)(2,1)}, bf1...) custom-call(f32[1]{0:T(128)} %bitcast.count_ref, ...), custom_call_target="tpu_custom_call" | custom-call | flops 6710886400 | bytes 7875112 | tf_op jit(solution)/shard_map/pallas_call | solution.py:172
  253.3 20.1 %shard_map.276 = bf16[2048,4608]{1,0:T(8,128)(2,1)} custom-call(bf16[2048,640]{1,0:T(8,128)(2,1)} %get-tuple-element.147.x_ref, bf16[640,512]{1,0:T(8,128)(2,1)} %multiply_convert_fusion.1.g_ref), custom_call_target="tpu_custom_call" | custom-call | flops 12079595520 | bytes 3276800 | tf_op jit(solution)/shard_map/pallas_call | solution.py:172
  277.4 29.8 %shard_map.277 = (bf16[160,2048]{1,0:T(8,128)(2,1)}, bf16[160,2048]{1,0:T(8,128)(2,1)}, bf16[160,2048]{1,0:T(8,128)(2,1)}, bf16[160,2048]{1,0:T(8,128)(2,1)}, f32[2,2048]{1,0:T(2,128)}) custom-call(s32[4]{0:T(128)} %get-tuple-element.257.ring_ref.at_ref, bf16[640,512]{1,0:T(8,128)(2,1)} %multiply_convert_fusion.1.g_ref, ...), custom_call_target="tpu_custom_call" | custom-call | flops 12079595520 | bytes 24772624 | tf_op jit(solution)/shard_map/pallas_call | solution.py:172
  308.0 6.5 %collective-permute-start.43 = (f32[2,4096]{1,0:T(2,128)S(1)}, f32[2,4096]{1,0:T(2,128)S(1)}, u32[]{:S(2)}, u32[]{:S(2)}) collective-permute-start(f32[2,4096]{1,0:T(2,128)S(1)} %pad_maximum_fusion.16), channel_id=1, source_target_pairs={{0,32},{32,0},{1,33},{33,1},{2,34},{34,2},{3,35},{35,3},{4,36},{36... | collective-permute-start | bytes 98312 | tf_op jit(solution)/shard_map/ppermute | solution.py:27
  338.3 9.8 %shard_map.278 = bf16[512,5120]{1,0:T(8,128)(2,1)} custom-call(bf16[640,512]{1,0:T(8,128)(2,1)} %get-tuple-element.194.x_ref, bf16[640,512]{1,0:T(8,128)(2,1)} %get-tuple-element.195.g_ref, bf16[640,512]{1,0:T(8,128)(2,1)} %get-tuple-element.196.rest_0_), custom_call_target="tpu_custom_call" | custom-call | flops 3355443200 | bytes 1966080 | tf_op jit(solution)/shard_map/pallas_call | solution.py:172
  353.4 3.5 collective-permute-done.53
  357.5 6.6 %shard_map.279 = (bf16[160,2048]{1,0:T(8,128)(2,1)}, bf16[160,512]{1,0:T(8,128)(2,1)}, bf16[160,512]{1,0:T(8,128)(2,1)}, bf16[160,512]{1,0:T(8,128)(2,1)}, bf16[...) custom-call(f32[1]{0:T(128)} %bitcast.count_ref, s32[4]{0:T(128)} %get-tuple-element.257.ring_ref.at_ref, ...), custom_call_target="tpu_custom_call" | custom-call | flops 335544320 | bytes 10314388 | tf_op jit(solution)/shard_map/pallas_call | solution.py:172
  368.0 5.0 collective-permute-start.54
  377.6 3.5 collective-permute-done.56
  396.6 6.9 %collective-permute-start.70 = (bf16[160,3072]{1,0:T(8,128)(2,1)S(1)}, bf16[160,3072]{1,0:T(8,128)(2,1)}, u32[]{:S(2)}, u32[]{:S(2)}) collective-permute-start(bf16[160,3072]{1,0:T(8,128)(2,1)S(1)} %pad_maximum_fusion.5), channel_id=1, source_target_pairs={{0,0},{1,64},{32,1},{33,65},{64,32},{65,96},{96,33},{97,97},{2,2},... | collective-permute-start | bytes 2949128 | tf_op jit(solution)/shard_map/ppermute | solution.py:69
  403.6 14.5 %shard_map.280 = (bf16[640,512]{1,0:T(8,128)(2,1)}, f32[2,512]{1,0:T(2,128)}, bf16[640,128]{1,0:T(8,128)(2,1)}) custom-call(f32[1]{0:T(128)} %bitcast.count_ref, s32[4]{0:T(128)} %get-tuple-element.257.ring_ref.at_ref, bf16[160,512]{1,0:T(8,128)(2,1)} %get-tuple-element.207.u0, bf16[160,512]{1,0:T(8,128)(2,1)} %copy-done.46, bf16[160,512]{1,0:T(8,128)(2,1)} %copy-done.47, ...), custom_call_target="tpu_custom_call" | custom-call | flops 3019898880 | bytes 8802836 | tf_op jit(solution)/shard_map/pallas_call | solution.py:172
  420.2 6.5 %shard_map.281 = bf16[512,1152]{1,0:T(8,128)(2,1)} custom-call(bf16[640,512]{1,0:T(8,128)(2,1)} %get-tuple-element.222.x_ref, bf16[640,128]{1,0:T(8,128)(2,1)} %get-tuple-element.223.g_ref), custom_call_target="tpu_custom_call" | custom-call | flops 754974720 | bytes 819200 | tf_op jit(solution)/shard_map/pallas_call | solution.py:172
  446.2 8.0 %all-to-all-start.1 = ((bf16[32,16,2176]{2,1,0:T(8,128)(2,1)}), bf16[32,16,2176]{2,1,0:T(8,128)(2,1)S(1)}, u32[]{:S(2)}, u32[]{:S(2)}) async-start(bf16[32,16,2176]{2,1,0:T(8,128)(2,1)} %bitcast.89), calls=%async_computation.2 | async-start | bytes 4456448 | tf_op jit(solution)/shard_map/all_to_all | solution.py:858
  455.0 6.7 %collective-permute-start.74 = (bf16[64,4608]{1,0:T(8,128)(2,1)S(1)}, bf16[64,4608]{1,0:T(8,128)(2,1)}, u32[]{:S(2)}, u32[]{:S(2)}) collective-permute-start(bf16[64,4608]{1,0:T(8,128)(2,1)S(1)} %copy-done.6), channel_id=1, source_target_pairs={{1,0},{32,33},{65,64},{96,97},{3,2},{34,35},{67,66},{98,99},{5,4},... | collective-permute-start | bytes 1769480 | tf_op jit(solution)/shard_map/ppermute | solution.py:1147
  467.9 6.2 %collective-permute-done.76 = bf16[160,512]{1,0:T(8,128)(2,1)} collective-permute-done((bf16[160,512]{1,0:T(8,128)(2,1)}, bf16[160,512]{1,0:T(8,128)(2,1)}, u32[]{:S(2)}, u32[]{:S(2)}) %collective-permute-start.76) | collective-permute-done | bytes 163872 | tf_op jit(solution)/shard_map/ppermute | solution.py:69
  477.8 9.6 %all-to-all-done.1 = bf16[32,16,2176]{2,1,0:T(8,128)(2,1)S(1)} async-done(((bf16[32,16,2176]{2,1,0:T(8,128)(2,1)}), bf16[32,16,2176]{2,1,0:T(8,128)(2,1)S(1)}, u32[]{:S(2)}, u32[]{:S(2)}) %all-to-all-start.1) | async-done | bytes 2228256 | tf_op jit(solution)/shard_map/all_to_all | solution.py:858
  487.8 18.3 %reduce-scatter.5.cloned.1.call-done = bf16[16,5120]{1,0:T(8,128)(2,1)} async-done(((bf16[512,5120]{1,0:T(8,128)(2,1)}), bf16[16,5120]{1,0:T(8,128)(2,1)}) %reduce-scatter.5.cloned.1.call-update) | async-done | bytes 163856 | tf_op jit(solution)/shard_map/reduce_scatter | solution.py:1092
  509.2 6.8 %collective-permute-start.78 = (bf16[16,7296]{1,0:T(8,128)(2,1)}, bf16[16,7296]{1,0:T(8,128)(2,1)}, u32[]{:S(2)}, u32[]{:S(2)}) collective-permute-start(bf16[16,7296]{1,0:T(8,128)(2,1)} %get-tuple-element.276.refs_0_), channel_id=1, source_target_pairs={{1,0},{32,33},{65,64},{96,97},{3,2},{34,35},{67,66},{98,99},{5,4},... | collective-permute-start | bytes 700424 | tf_op jit(solution)/shard_map/ppermute | solution.py:1147
  540.2 4.9 shard_map.283
  (424 shorter events, 243.6 us)
Async XLA Ops:
  7.2 76.2 %all-gather.4.cloned.1.call-start = ((), (), s32[]{:S(2)}) async-start(), calls=%async_computation.4 | async-start | bytes 7028736 | tf_op jit(solution)/shard_map/all_gather | solution.py:944
  21.7 14.6 %collective-permute-start.2 = (bf16[160,2048]{1,0:T(8,128)(2,1)S(1)}, bf16[160,2048]{1,0:T(8,128)(2,1)S(1)}, u32[]{:S(2)}, u32[]{:S(2)}) collective-permute-start(bf16[160,2048]{1,0:T(8,128)(2,1)S(1)} %bitcast_multiply_fusion), channel_id=1, source_target_pairs={{0,64},{1,65},{64,0},{65,1},{2,66},{3,67},{66,2},{67,3},{4,68},{5,... | collective-permute-start | bytes 1966088 | tf_op jit(solution)/shard_map/ppermute | solution.py:27
  22.4 15.8 %collective-permute-start.3 = (bf16[160,2048]{1,0:T(8,128)(2,1)S(1)}, bf16[160,2048]{1,0:T(8,128)(2,1)S(1)}, u32[]{:S(2)}, u32[]{:S(2)}) collective-permute-start(bf16[160,2048]{1,0:T(8,128)(2,1)S(1)} %bitcast_multiply_fusion), channel_id=1, source_target_pairs={{0,65},{1,64},{64,1},{65,0},{2,67},{3,66},{66,3},{67,2},{4,69},{5,... | collective-permute-start | bytes 1966088 | tf_op jit(solution)/shard_map/ppermute | solution.py:27
  23.7 33.4 %all-to-all-start = ((bf16[16,64,512]{2,1,0:T(8,128)(2,1)}), bf16[16,64,512]{2,1,0:T(8,128)(2,1)S(1)}, u32[]{:S(2)}, u32[]{:S(2)}) async-start(bf16[16,64,512]{2,1,0:T(8,128)(2,1)} %broadcast_in_dim.56), calls=%async_computation | async-start | bytes 2097152 | tf_op jit(solution)/shard_map/all_to_all | solution.py:940
  31.3 131.4 %all-gather.6.cloned.1.call-start = ((), (), s32[]{:S(2)}) async-start(), calls=%async_computation.5 | async-start | bytes 19464192 | tf_op jit(solution)/shard_map/all_gather | solution.py:959
  41.6 15.6 %collective-permute-start.7 = (bf16[64,4608]{1,0:T(8,128)(2,1)}, bf16[64,4608]{1,0:T(8,128)(2,1)}, u32[]{:S(2)}, u32[]{:S(2)}) collective-permute-start(bf16[64,4608]{1,0:T(8,128)(2,1)} %dynamic-slice_bitcast_fusion), channel_id=1, source_target_pairs={{0,65},{33,96},{64,1},{97,32},{2,67},{35,98},{66,3},{99,34},{4,69}... | collective-permute-start | bytes 1769480 | tf_op jit(solution)/shard_map/ppermute | solution.py:918
  61.7 148.4 %all-gather.8.cloned.1.call-start = ((), (), s32[]{:S(2)}) async-start(), calls=%async_computation.6 | async-start | bytes 5406720 | tf_op jit(solution)/shard_map/all_gather | solution.py:996
  112.5 22.9 %collective-permute-start.21 = (bf16[16,5120]{1,0:T(8,128)(2,1)S(1)}, bf16[16,5120]{1,0:T(8,128)(2,1)S(1)}, u32[]{:S(2)}, u32[]{:S(2)}) collective-permute-start(bf16[16,5120]{1,0:T(8,128)(2,1)S(1)} %dynamic-slice_bitcast_fusion.1), channel_id=1, source_target_pairs={{0,65},{33,96},{64,1},{97,32},{2,67},{35,98},{66,3},{99,34},{4,69}... | collective-permute-start | bytes 491528 | tf_op jit(solution)/shard_map/ppermute | solution.py:918
  136.1 295.4 %reduce-scatter.3.cloned.1.call-start = ((), (), s32[]{:S(2)}) async-start(), calls=%async_computation.7 | async-start | bytes 19464192 | tf_op jit(solution)/shard_map/reduce_scatter | solution.py:1043
  136.3 22.9 %collective-permute-start.24 = (bf16[160,1024]{1,0:T(8,128)(2,1)S(1)}, bf16[160,1024]{1,0:T(8,128)(2,1)S(1)}, u32[]{:S(2)}, u32[]{:S(2)}) collective-permute-start(bf16[160,1024]{1,0:T(8,128)(2,1)S(1)} %pad_maximum_fusion.12), channel_id=1, source_target_pairs={{0,64},{1,65},{64,0},{65,1},{2,66},{3,67},{66,2},{67,3},{4,68},{5,... | collective-permute-start | bytes 983048 | tf_op jit(solution)/shard_map/ppermute | solution.py:27
  136.4 22.8 %collective-permute-start.25 = (bf16[160,1024]{1,0:T(8,128)(2,1)S(1)}, bf16[160,1024]{1,0:T(8,128)(2,1)S(1)}, u32[]{:S(2)}, u32[]{:S(2)}) collective-permute-start(bf16[160,1024]{1,0:T(8,128)(2,1)S(1)} %pad_maximum_fusion.12), channel_id=1, source_target_pairs={{0,65},{1,64},{64,1},{65,0},{2,67},{3,66},{66,3},{67,2},{4,69},{5,... | collective-permute-start | bytes 983048 | tf_op jit(solution)/shard_map/ppermute | solution.py:27
  159.2 22.7 %collective-permute-start.26 = (bf16[80,1024]{1,0:T(8,128)(2,1)S(1)}, bf16[80,1024]{1,0:T(8,128)(2,1)S(1)}, u32[]{:S(2)}, u32[]{:S(2)}) collective-permute-start(bf16[80,1024]{1,0:T(8,128)(2,1)S(1)} %slice.178), channel_id=1, source_target_pairs={{0,64},{1,65},{64,0},{65,1},{2,66},{3,67},{66,2},{67,3},{4,68},{5,... | collective-permute-start | bytes 491528 | tf_op jit(solution)/shard_map/ppermute | solution.py:27
  160.6 21.3 %collective-permute-start.27 = (bf16[80,1024]{1,0:T(8,128)(2,1)S(1)}, bf16[80,1024]{1,0:T(8,128)(2,1)S(1)}, u32[]{:S(2)}, u32[]{:S(2)}) collective-permute-start(bf16[80,1024]{1,0:T(8,128)(2,1)S(1)} %slice.179), channel_id=1, source_target_pairs={{0,65},{1,64},{64,1},{65,0},{2,67},{3,66},{66,3},{67,2},{4,69},{5,... | collective-permute-start | bytes 491528 | tf_op jit(solution)/shard_map/ppermute | solution.py:27
  183.1 26.9 %collective-permute-start.33 = (bf16[320,1024]{1,0:T(8,128)(2,1)S(1)}, bf16[320,1024]{1,0:T(8,128)(2,1)S(1)}, u32[]{:S(2)}, u32[]{:S(2)}) collective-permute-start(bf16[320,1024]{1,0:T(8,128)(2,1)S(1)} %get-tuple-element.263), channel_id=1, source_target_pairs={{0,32},{32,0},{1,33},{33,1},{2,34},{34,2},{3,35},{35,3},{4,36},{36... | collective-permute-start | bytes 1966088 | tf_op jit(solution)/shard_map/ppermute | solution.py:27
  247.1 26.4 %collective-permute-start.39 = (bf16[80,1024]{1,0:T(8,128)(2,1)S(1)}, bf16[80,1024]{1,0:T(8,128)(2,1)S(1)}, u32[]{:S(2)}, u32[]{:S(2)}) collective-permute-start(bf16[80,1024]{1,0:T(8,128)(2,1)S(1)} %get-tuple-element.274), channel_id=1, source_target_pairs={{0,64},{1,65},{64,0},{65,1},{2,66},{3,67},{66,2},{67,3},{4,68},{5,... | collective-permute-start | bytes 491528 | tf_op jit(solution)/shard_map/ppermute | solution.py:27
  248.3 25.2 %collective-permute-start.40 = (bf16[80,1024]{1,0:T(8,128)(2,1)S(1)}, bf16[80,1024]{1,0:T(8,128)(2,1)S(1)}, u32[]{:S(2)}, u32[]{:S(2)}) collective-permute-start(bf16[80,1024]{1,0:T(8,128)(2,1)S(1)} %get-tuple-element.273), channel_id=1, source_target_pairs={{0,65},{1,64},{64,1},{65,0},{2,67},{3,66},{66,3},{67,2},{4,69},{5,... | collective-permute-start | bytes 491528 | tf_op jit(solution)/shard_map/ppermute | solution.py:27
  273.5 232.6 %reduce-scatter.5.cloned.1.call-start = ((), (), s32[]{:S(2)}) async-start(), calls=%async_computation.8 | async-start | bytes 5406720 | tf_op jit(solution)/shard_map/reduce_scatter | solution.py:1092
  276.1 31.1 %collective-permute-start.42 = (bf16[160,1024]{1,0:T(8,128)(2,1)S(1)}, bf16[160,1024]{1,0:T(8,128)(2,1)S(1)}, u32[]{:S(2)}, u32[]{:S(2)}) collective-permute-start(bf16[160,1024]{1,0:T(8,128)(2,1)S(1)} %pad_maximum_fusion.14), channel_id=1, source_target_pairs={{0,65},{1,64},{64,1},{65,0},{2,67},{3,66},{66,3},{67,2},{4,69},{5,... | collective-permute-start | bytes 983048 | tf_op jit(solution)/shard_map/ppermute | solution.py:27
  277.1 30.0 %collective-permute-start.41 = (bf16[160,1024]{1,0:T(8,128)(2,1)S(1)}, bf16[160,1024]{1,0:T(8,128)(2,1)S(1)}, u32[]{:S(2)}, u32[]{:S(2)}) collective-permute-start(bf16[160,1024]{1,0:T(8,128)(2,1)S(1)} %pad_maximum_fusion.13), channel_id=1, source_target_pairs={{0,64},{1,65},{64,0},{65,1},{2,66},{3,67},{66,2},{67,3},{4,68},{5,... | collective-permute-start | bytes 983048 | tf_op jit(solution)/shard_map/ppermute | solution.py:27
  328.4 19.7 %collective-permute-start.51 = (bf16[160,2048]{1,0:T(8,128)(2,1)}, bf16[160,2048]{1,0:T(8,128)(2,1)S(1)}, u32[]{:S(2)}, u32[]{:S(2)}) collective-permute-start(bf16[160,2048]{1,0:T(8,128)(2,1)} %pad_maximum_fusion.10), channel_id=1, source_target_pairs={{0,65},{1,64},{64,1},{65,0},{2,67},{3,66},{66,3},{67,2},{4,69},{5,... | collective-permute-start | bytes 1966088 | tf_op jit(solution)/shard_map/ppermute | solution.py:27
  331.2 17.0 %collective-permute-start.50 = (bf16[160,2048]{1,0:T(8,128)(2,1)}, bf16[160,2048]{1,0:T(8,128)(2,1)}, u32[]{:S(2)}, u32[]{:S(2)}) collective-permute-start(bf16[160,2048]{1,0:T(8,128)(2,1)} %pad_maximum_fusion.9), channel_id=1, source_target_pairs={{0,64},{1,65},{64,0},{65,1},{2,66},{3,67},{66,2},{67,3},{4,68},{5,... | collective-permute-start | bytes 1966088 | tf_op jit(solution)/shard_map/ppermute | solution.py:27
  364.1 17.1 %collective-permute-start.57 = (bf16[160,512]{1,0:T(8,128)(2,1)}, bf16[160,512]{1,0:T(8,128)(2,1)S(1)}, u32[]{:S(2)}, u32[]{:S(2)}) collective-permute-start(bf16[160,512]{1,0:T(8,128)(2,1)} %get-tuple-element.207.u0), channel_id=1, source_target_pairs={{0,64},{1,65},{64,0},{65,1},{2,66},{3,67},{66,2},{67,3},{4,68},{5,... | collective-permute-start | bytes 491528 | tf_op jit(solution)/shard_map/ppermute | solution.py:27
  364.4 16.8 %collective-permute-start.58 = (bf16[160,512]{1,0:T(8,128)(2,1)}, bf16[160,512]{1,0:T(8,128)(2,1)S(1)}, u32[]{:S(2)}, u32[]{:S(2)}) collective-permute-start(bf16[160,512]{1,0:T(8,128)(2,1)} %get-tuple-element.207.u0), channel_id=1, source_target_pairs={{0,1},{1,0},{64,65},{65,64},{2,3},{3,2},{66,67},{67,66},{4,5},{5,4... | collective-permute-start | bytes 491528 | tf_op jit(solution)/shard_map/ppermute | solution.py:27
  366.3 15.0 %collective-permute-start.59 = (bf16[160,512]{1,0:T(8,128)(2,1)}, bf16[160,512]{1,0:T(8,128)(2,1)S(1)}, u32[]{:S(2)}, u32[]{:S(2)}) collective-permute-start(bf16[160,512]{1,0:T(8,128)(2,1)} %get-tuple-element.207.u0), channel_id=1, source_target_pairs={{0,65},{1,64},{64,1},{65,0},{2,67},{3,66},{66,3},{67,2},{4,69},{5,... | collective-permute-start | bytes 491528 | tf_op jit(solution)/shard_map/ppermute | solution.py:27
  396.6 34.9 %collective-permute-start.70 = (bf16[160,3072]{1,0:T(8,128)(2,1)S(1)}, bf16[160,3072]{1,0:T(8,128)(2,1)}, u32[]{:S(2)}, u32[]{:S(2)}) collective-permute-start(bf16[160,3072]{1,0:T(8,128)(2,1)S(1)} %pad_maximum_fusion.5), channel_id=1, source_target_pairs={{0,0},{1,64},{32,1},{33,65},{64,32},{65,96},{96,33},{97,97},{2,2},... | collective-permute-start | bytes 2949128 | tf_op jit(solution)/shard_map/ppermute | solution.py:69
  446.2 41.2 %all-to-all-start.1 = ((bf16[32,16,2176]{2,1,0:T(8,128)(2,1)}), bf16[32,16,2176]{2,1,0:T(8,128)(2,1)S(1)}, u32[]{:S(2)}, u32[]{:S(2)}) async-start(bf16[32,16,2176]{2,1,0:T(8,128)(2,1)} %bitcast.89), calls=%async_computation.2 | async-start | bytes 4456448 | tf_op jit(solution)/shard_map/all_to_all | solution.py:858
  454.3 23.5 %collective-permute-start.73 = (bf16[64,4608]{1,0:T(8,128)(2,1)S(1)}, bf16[64,4608]{1,0:T(8,128)(2,1)S(1)}, u32[]{:S(2)}, u32[]{:S(2)}) collective-permute-start(bf16[64,4608]{1,0:T(8,128)(2,1)S(1)} %copy-done.6), channel_id=1, source_target_pairs={{0,64},{33,97},{64,0},{97,33},{2,66},{35,99},{66,2},{99,35},{4,68}... | collective-permute-start | bytes 1769480 | tf_op jit(solution)/shard_map/ppermute | solution.py:1147
  455.0 22.8 %collective-permute-start.74 = (bf16[64,4608]{1,0:T(8,128)(2,1)S(1)}, bf16[64,4608]{1,0:T(8,128)(2,1)}, u32[]{:S(2)}, u32[]{:S(2)}) collective-permute-start(bf16[64,4608]{1,0:T(8,128)(2,1)S(1)} %copy-done.6), channel_id=1, source_target_pairs={{1,0},{32,33},{65,64},{96,97},{3,2},{34,35},{67,66},{98,99},{5,4},... | collective-permute-start | bytes 1769480 | tf_op jit(solution)/shard_map/ppermute | solution.py:1147
  461.7 16.2 %collective-permute-start.75 = (bf16[64,4608]{1,0:T(8,128)(2,1)S(1)}, bf16[64,4608]{1,0:T(8,128)(2,1)}, u32[]{:S(2)}, u32[]{:S(2)}) collective-permute-start(bf16[64,4608]{1,0:T(8,128)(2,1)S(1)} %copy-done.6), channel_id=1, source_target_pairs={{1,64},{32,97},{65,0},{96,33},{3,66},{34,99},{67,2},{98,35},{5,68}... | collective-permute-start | bytes 1769480 | tf_op jit(solution)/shard_map/ppermute | solution.py:1147
  507.8 16.3 %collective-permute-start.77 = (bf16[16,7296]{1,0:T(8,128)(2,1)}, bf16[16,7296]{1,0:T(8,128)(2,1)}, u32[]{:S(2)}, u32[]{:S(2)}) collective-permute-start(bf16[16,7296]{1,0:T(8,128)(2,1)} %get-tuple-element.276.refs_0_), channel_id=1, source_target_pairs={{0,64},{33,97},{64,0},{97,33},{2,66},{35,99},{66,2},{99,35},{4,68}... | collective-permute-start | bytes 700424 | tf_op jit(solution)/shard_map/ppermute | solution.py:1147
  509.2 15.0 %collective-permute-start.78 = (bf16[16,7296]{1,0:T(8,128)(2,1)}, bf16[16,7296]{1,0:T(8,128)(2,1)}, u32[]{:S(2)}, u32[]{:S(2)}) collective-permute-start(bf16[16,7296]{1,0:T(8,128)(2,1)} %get-tuple-element.276.refs_0_), channel_id=1, source_target_pairs={{1,0},{32,33},{65,64},{96,97},{3,2},{34,35},{67,66},{98,99},{5,4},... | collective-permute-start | bytes 700424 | tf_op jit(solution)/shard_map/ppermute | solution.py:1147
  520.9 17.9 %collective-permute-start.81 = (bf16[4,64,4608]{2,1,0:T(8,128)(2,1)}, bf16[4,64,4608]{2,1,0:T(8,128)(2,1)S(1)}, u32[]{:S(2)}, u32[]{:S(2)}) collective-permute-start(bf16[4,64,4608]{2,1,0:T(8,128)(2,1)} %pad_maximum_fusion), channel_id=1, source_target_pairs={{0,32},{33,1},{64,96},{97,65},{2,34},{35,3},{66,98},{99,67},{4,36}... | collective-permute-start | bytes 7077896 | tf_op jit(solution)/shard_map/ppermute | solution.py:1155
  (107 other events, 1125.8 us)
Sparse Core Ops, SparseCore 0:
  19.6 61.2 all-gather.3
  83.2 76.8 all-gather.5
  162.9 47.0 all-gather.7
  273.6 122.0 reduce-scatter.2
  399.8 106.2 reduce-scatter.4

commit v6 on v4

--- a/solution.py
+++ b/solution.py
@@ -1170,7 +1170,7 @@
     trunk_grad = jnp.concatenate(
         [trunk_grad, grad_reduce.reshape(trunk_grad.shape[0], -1)], axis=1
     )
-    trunk_grad, head_pieces, d_pre_one = hold(trunk_grad, head_pieces, d_pre_one)
+    trunk_grad, d_pre_one = hold(trunk_grad, d_pre_one)
     trunk_parts = shares_sent(trunk_grad, POOL)
     wide = message_weight.shape[2]
     (sum_head,) = to_cores(head_pieces, wide)

time: 549 us -> 549 us (level)
  no operation moved by 1% of the time
where the time goes in v6:
time: 549 us; the launch traced here: 539 us
  Pallas kernels  168 us (31%)
  starting transfers between devices  148 us (27%)
  waiting for transfers between devices  124 us (23%)
  other arithmetic  41.4 us (8%)
  local copies, waits for them, and re-layouts  36.1 us (7%)
  between operations  15.6 us (3%)
  matrix products  7.19 us (1%)
    pallas_call x13, Pallas kernels, call(): pl.pallas_call(kernel, grid=grid, in_specs=in_specs, out_specs=out_specs,...  168 us
    ppermute x69, starting transfers between devices, swap(): return lax.ppermute(value, axis, [(i, i ^ flip) for i in range(count)])  96.5 us
    ppermute x69, waiting for transfers between devices, swap(): return lax.ppermute(value, axis, [(i, i ^ flip) for i in range(count)])  77.9 us
    ppermute x6, starting transfers between devices, to_chips(): pieces.append(lax.ppermute(share, GROUP, pairs))  16.7 us
    all_to_all x1, waiting for transfers between devices, shares_sent(): lax.all_to_all(value.reshape(count, value.shape[0] // count, value.shape[...  12.6 us
  transfers between devices with their start and end apart: 89, of which 53 were waited for; matrix products, arithmetic and copies ran while one was open for 13% of the time, Pallas kernels for 27%

profile of v6, /device:TPU:1, one launch (start us, length us, event | category | flops | bytes accessed | tf_op | source)
XLA Modules:
  0.0 539.5 jit_solution(493939289695848254)
XLA Ops:
  11.3 7.5 %collective-permute-done = bf16[16,8704]{1,0:T(8,128)(2,1)S(1)} collective-permute-done((bf16[16,8704]{1,0:T(8,128)(2,1)S(1)}, bf16[16,8704]{1,0:T(8,128)(2,1)S(1)}, u32[]{:S(2)}, u32[]{:S(2)}) %collective-permute-start) | collective-permute-done | bytes 278560 | tf_op jit(solution)/shard_map/ppermute | solution.py:918
  23.7 7.6 %all-to-all-start = ((bf16[16,64,512]{2,1,0:T(8,128)(2,1)}), bf16[16,64,512]{2,1,0:T(8,128)(2,1)S(1)}, u32[]{:S(2)}, u32[]{:S(2)}) async-start(bf16[16,64,512]{2,1,0:T(8,128)(2,1)} %broadcast_in_dim.56), calls=%async_computation | async-start | bytes 2097152 | tf_op jit(solution)/shard_map/all_to_all | solution.py:940
  50.7 6.4 %collective-permute-start.6 = (bf16[320,2048]{1,0:T(8,128)(2,1)}, bf16[320,2048]{1,0:T(8,128)(2,1)}, u32[]{:S(2)}, u32[]{:S(2)}) collective-permute-start(bf16[320,2048]{1,0:T(8,128)(2,1)} %get-tuple-element.255), channel_id=1, source_target_pairs={{0,32},{32,0},{1,33},{33,1},{2,34},{34,2},{3,35},{35,3},{4,36},{36... | collective-permute-start | bytes 3932168 | tf_op jit(solution)/shard_map/ppermute | solution.py:27
  77.3 3.7 collective-permute-start.12
  83.4 11.8 %shard_map.271 = (bf16[640,512]{1,0:T(8,128)(2,1)}, f32[2,512]{1,0:T(2,128)}, bf16[640,512]{1,0:T(8,128)(2,1)}, bf16[640,512]{1,0:T(8,128)(2,1)}) custom-call(f32[1]{0:T(128)} %bitcast.count_ref, s32[4]{0:T(128)} %add_multiply_fusion.1.at_ref, bf16[640,512]{1,0:T(8,128)(2,1)} %pad_maximum_fusion.7.value_ref, f32[2,512]{1,0:T(2,128)} %add.337.sums_ref.low_sums, ...), custom_call_target="tpu_custom_call" | custom-call | flops 3019898880 | bytes 7481876 | tf_op jit(solution)/shard_map/pallas_call | solution.py:172
  95.3 3.3 collective-permute-start.13
  114.3 6.8 %shard_map.272 = (bf16[640,512]{1,0:T(8,128)(2,1)}, bf16[640,2048]{1,0:T(8,128)(2,1)}, f32[2,2048]{1,0:T(2,128)}) custom-call(f32[1]{0:T(128)} %bitcast.count_ref, bf16[640,512]{1,0:T(8,128)(2,1)} %get-tuple-element.138.value_ref, f32[2,512]{1,0:T(2,128)} %add.342.sums_ref.low_sums, f32[1,512]{1,0:T(1,128)} %get-tuple-element.290.gain_ref.low_gain, ...), custom_call_target="tpu_custom_call" | custom-call | flops 1342177280 | bytes 7481860 | tf_op jit(solution)/shard_map/pallas_call | solution.py:172
  121.2 4.4 collective-permute-start.18
  136.5 3.3 collective-permute-done.22
  145.0 14.0 %shard_map.273 = (bf16[640,2048]{1,0:T(8,128)(2,1)}, bf16[640,2048]{1,0:T(8,128)(2,1)}, bf16[640,2048]{1,0:T(8,128)(2,1)}, bf16[640,2048]{1,0:T(8,128)(2,1)}, bf16[2048,640]{1,0:T(8,128)(2,1)}) custom-call(f32[1]{0:T(128)} %bitcast.count_ref, s32[4]{0:T(128)} %add_multiply_fusion.1.at_ref, bf16[640,2048]{1,0:T(8,128)(2,1)} %get-tuple-element.141.value_ref, ...), custom_call_target="tpu_custom_call" | custom-call | flops 52428800 | bytes 5278228 | tf_op jit(solution)/shard_map/pallas_call | solution.py:172
  162.5 19.2 %shard_map.274 = (f32[640,512]{1,0:T(8,128)}, f32[2,512]{1,0:T(2,128)}) custom-call(bf16[640,2048]{1,0:T(8,128)(2,1)} %get-tuple-element.149.trunk_ref, f32[640,1]{1,0:T(8,128)} %fusion.18.inside_ref, bf16[2048,4608]{1,0:T(8,128)(2,1)} %all-gather.6.cloned.1.call-done.w_ref), custom_call_target="tpu_custom_call" | custom-call | flops 12079595520 | bytes 21498368 | tf_op jit(solution)/shard_map/pallas_call | solution.py:172
  183.0 4.4 collective-permute-start.33
  203.2 6.7 %all-gather.8.cloned.1.call-done.w_ref = bf16[512,5120]{1,0:T(8,128)(2,1)} async-done(((bf16[16,5120]{1,0:T(8,128)(2,1)}), bf16[512,5120]{1,0:T(8,128)(2,1)}) %all-gather.8.cloned.1.call-update) | async-done | bytes 5242896 | tf_op jit(solution)/shard_map/all_gather | solution.py:996
  210.8 20.7 %shard_map.275 = (bf16[640,512]{1,0:T(8,128)(2,1)}, bf16[160,1024]{1,0:T(8,128)(2,1)}, bf16[160,1024]{1,0:T(8,128)(2,1)}, bf16[160,1024]{1,0:T(8,128)(2,1)}, bf1...) custom-call(f32[1]{0:T(128)} %bitcast.count_ref, ...), custom_call_target="tpu_custom_call" | custom-call | flops 6710886400 | bytes 7875112 | tf_op jit(solution)/shard_map/pallas_call | solution.py:172
  253.2 20.1 %shard_map.276 = bf16[2048,4608]{1,0:T(8,128)(2,1)} custom-call(bf16[2048,640]{1,0:T(8,128)(2,1)} %get-tuple-element.145.x_ref, bf16[640,512]{1,0:T(8,128)(2,1)} %multiply_convert_fusion.1.g_ref), custom_call_target="tpu_custom_call" | custom-call | flops 12079595520 | bytes 3276800 | tf_op jit(solution)/shard_map/pallas_call | solution.py:172
  277.2 29.8 %shard_map.277 = (bf16[160,2048]{1,0:T(8,128)(2,1)}, bf16[160,2048]{1,0:T(8,128)(2,1)}, bf16[160,2048]{1,0:T(8,128)(2,1)}, bf16[160,2048]{1,0:T(8,128)(2,1)}, f32[2,2048]{1,0:T(2,128)}) custom-call(s32[4]{0:T(128)} %get-tuple-element.253.ring_ref.at_ref, bf16[640,512]{1,0:T(8,128)(2,1)} %multiply_convert_fusion.1.g_ref, ...), custom_call_target="tpu_custom_call" | custom-call | flops 12079595520 | bytes 24772624 | tf_op jit(solution)/shard_map/pallas_call | solution.py:172
  307.8 6.5 %collective-permute-start.43 = (f32[2,4096]{1,0:T(2,128)S(1)}, f32[2,4096]{1,0:T(2,128)S(1)}, u32[]{:S(2)}, u32[]{:S(2)}) collective-permute-start(f32[2,4096]{1,0:T(2,128)S(1)} %pad_maximum_fusion.16), channel_id=1, source_target_pairs={{0,32},{32,0},{1,33},{33,1},{2,34},{34,2},{3,35},{35,3},{4,36},{36... | collective-permute-start | bytes 98312 | tf_op jit(solution)/shard_map/ppermute | solution.py:27
  338.1 9.8 %shard_map.278 = bf16[512,5120]{1,0:T(8,128)(2,1)} custom-call(bf16[640,512]{1,0:T(8,128)(2,1)} %get-tuple-element.192.x_ref, bf16[640,512]{1,0:T(8,128)(2,1)} %get-tuple-element.193.g_ref, bf16[640,512]{1,0:T(8,128)(2,1)} %get-tuple-element.194.rest_0_), custom_call_target="tpu_custom_call" | custom-call | flops 3355443200 | bytes 1966080 | tf_op jit(solution)/shard_map/pallas_call | solution.py:172
  353.2 3.5 collective-permute-done.53
  357.4 6.5 %shard_map.279 = (bf16[160,2048]{1,0:T(8,128)(2,1)}, bf16[160,512]{1,0:T(8,128)(2,1)}, bf16[160,512]{1,0:T(8,128)(2,1)}, bf16[160,512]{1,0:T(8,128)(2,1)}, bf16[...) custom-call(f32[1]{0:T(128)} %bitcast.count_ref, s32[4]{0:T(128)} %get-tuple-element.253.ring_ref.at_ref, ...), custom_call_target="tpu_custom_call" | custom-call | flops 335544320 | bytes 10314388 | tf_op jit(solution)/shard_map/pallas_call | solution.py:172
  367.8 5.0 collective-permute-start.54
  377.4 3.5 collective-permute-done.56
  396.5 6.9 %collective-permute-start.70 = (bf16[160,3072]{1,0:T(8,128)(2,1)S(1)}, bf16[160,3072]{1,0:T(8,128)(2,1)}, u32[]{:S(2)}, u32[]{:S(2)}) collective-permute-start(bf16[160,3072]{1,0:T(8,128)(2,1)S(1)} %pad_maximum_fusion.5), channel_id=1, source_target_pairs={{0,0},{1,64},{32,1},{33,65},{64,32},{65,96},{96,33},{97,97},{2,2},... | collective-permute-start | bytes 2949128 | tf_op jit(solution)/shard_map/ppermute | solution.py:69
  403.4 14.4 %shard_map.280 = (bf16[640,512]{1,0:T(8,128)(2,1)}, f32[2,512]{1,0:T(2,128)}, bf16[640,128]{1,0:T(8,128)(2,1)}) custom-call(f32[1]{0:T(128)} %bitcast.count_ref, s32[4]{0:T(128)} %get-tuple-element.253.ring_ref.at_ref, bf16[160,512]{1,0:T(8,128)(2,1)} %get-tuple-element.205.u0, bf16[160,512]{1,0:T(8,128)(2,1)} %copy-done.51, bf16[160,512]{1,0:T(8,128)(2,1)} %copy-done.52, ...), custom_call_target="tpu_custom_call" | custom-call | flops 3019898880 | bytes 8802836 | tf_op jit(solution)/shard_map/pallas_call | solution.py:172
  420.0 6.5 %shard_map.281 = bf16[512,1152]{1,0:T(8,128)(2,1)} custom-call(bf16[640,512]{1,0:T(8,128)(2,1)} %get-tuple-element.220.x_ref, bf16[640,128]{1,0:T(8,128)(2,1)} %get-tuple-element.221.g_ref), custom_call_target="tpu_custom_call" | custom-call | flops 754974720 | bytes 819200 | tf_op jit(solution)/shard_map/pallas_call | solution.py:172
  437.4 5.9 %collective-permute-start.74 = (bf16[64,4608]{1,0:T(8,128)(2,1)}, bf16[64,4608]{1,0:T(8,128)(2,1)}, u32[]{:S(2)}, u32[]{:S(2)}) collective-permute-start(bf16[64,4608]{1,0:T(8,128)(2,1)} %reduce-scatter.3.cloned.1.call-done.refs_0_), channel_id=1, source_target_pairs={{1,0},{32,33},{65,64},{96,97},{3,2},{34,35},{67,66},{98,99},{5,4},... | collective-permute-start | bytes 1769480 | tf_op jit(solution)/shard_map/ppermute | solution.py:1147
  449.7 4.5 collective-permute-done.74.refs_2_
  463.3 9.7 %all-to-all-start.1 = ((bf16[32,16,2176]{2,1,0:T(8,128)(2,1)}), bf16[32,16,2176]{2,1,0:T(8,128)(2,1)S(1)}, u32[]{:S(2)}, u32[]{:S(2)}) async-start(bf16[32,16,2176]{2,1,0:T(8,128)(2,1)} %bitcast.89), calls=%async_computation.2 | async-start | bytes 4456448 | tf_op jit(solution)/shard_map/all_to_all | solution.py:858
  477.2 3.8 collective-permute-done.77
  484.7 4.9 shard_map.282
  491.9 12.6 %all-to-all-done.1 = bf16[32,16,2176]{2,1,0:T(8,128)(2,1)S(1)} async-done(((bf16[32,16,2176]{2,1,0:T(8,128)(2,1)}), bf16[32,16,2176]{2,1,0:T(8,128)(2,1)S(1)}, u32[]{:S(2)}, u32[]{:S(2)}) %all-to-all-start.1) | async-done | bytes 2228256 | tf_op jit(solution)/shard_map/all_to_all | solution.py:858
  505.6 5.2 collective-permute-start.79
  (434 shorter events, 244.8 us)
Async XLA Ops:
  7.2 76.2 %all-gather.4.cloned.1.call-start = ((), (), s32[]{:S(2)}) async-start(), calls=%async_computation.4 | async-start | bytes 7028736 | tf_op jit(solution)/shard_map/all_gather | solution.py:944
  21.7 14.6 %collective-permute-start.2 = (bf16[160,2048]{1,0:T(8,128)(2,1)S(1)}, bf16[160,2048]{1,0:T(8,128)(2,1)S(1)}, u32[]{:S(2)}, u32[]{:S(2)}) collective-permute-start(bf16[160,2048]{1,0:T(8,128)(2,1)S(1)} %bitcast_multiply_fusion), channel_id=1, source_target_pairs={{0,64},{1,65},{64,0},{65,1},{2,66},{3,67},{66,2},{67,3},{4,68},{5,... | collective-permute-start | bytes 1966088 | tf_op jit(solution)/shard_map/ppermute | solution.py:27
  22.4 15.8 %collective-permute-start.3 = (bf16[160,2048]{1,0:T(8,128)(2,1)S(1)}, bf16[160,2048]{1,0:T(8,128)(2,1)S(1)}, u32[]{:S(2)}, u32[]{:S(2)}) collective-permute-start(bf16[160,2048]{1,0:T(8,128)(2,1)S(1)} %bitcast_multiply_fusion), channel_id=1, source_target_pairs={{0,65},{1,64},{64,1},{65,0},{2,67},{3,66},{66,3},{67,2},{4,69},{5,... | collective-permute-start | bytes 1966088 | tf_op jit(solution)/shard_map/ppermute | solution.py:27
  23.7 33.4 %all-to-all-start = ((bf16[16,64,512]{2,1,0:T(8,128)(2,1)}), bf16[16,64,512]{2,1,0:T(8,128)(2,1)S(1)}, u32[]{:S(2)}, u32[]{:S(2)}) async-start(bf16[16,64,512]{2,1,0:T(8,128)(2,1)} %broadcast_in_dim.56), calls=%async_computation | async-start | bytes 2097152 | tf_op jit(solution)/shard_map/all_to_all | solution.py:940
  31.3 131.2 %all-gather.6.cloned.1.call-start = ((), (), s32[]{:S(2)}) async-start(), calls=%async_computation.5 | async-start | bytes 19464192 | tf_op jit(solution)/shard_map/all_gather | solution.py:959
  41.6 15.6 %collective-permute-start.7 = (bf16[64,4608]{1,0:T(8,128)(2,1)}, bf16[64,4608]{1,0:T(8,128)(2,1)}, u32[]{:S(2)}, u32[]{:S(2)}) collective-permute-start(bf16[64,4608]{1,0:T(8,128)(2,1)} %dynamic-slice_bitcast_fusion), channel_id=1, source_target_pairs={{0,65},{33,96},{64,1},{97,32},{2,67},{35,98},{66,3},{99,34},{4,69}... | collective-permute-start | bytes 1769480 | tf_op jit(solution)/shard_map/ppermute | solution.py:918
  61.7 148.2 %all-gather.8.cloned.1.call-start = ((), (), s32[]{:S(2)}) async-start(), calls=%async_computation.6 | async-start | bytes 5406720 | tf_op jit(solution)/shard_map/all_gather | solution.py:996
  112.2 23.1 %collective-permute-start.21 = (bf16[16,5120]{1,0:T(8,128)(2,1)S(1)}, bf16[16,5120]{1,0:T(8,128)(2,1)S(1)}, u32[]{:S(2)}, u32[]{:S(2)}) collective-permute-start(bf16[16,5120]{1,0:T(8,128)(2,1)S(1)} %dynamic-slice_bitcast_fusion.1), channel_id=1, source_target_pairs={{0,65},{33,96},{64,1},{97,32},{2,67},{35,98},{66,3},{99,34},{4,69}... | collective-permute-start | bytes 491528 | tf_op jit(solution)/shard_map/ppermute | solution.py:918
  136.0 295.2 %reduce-scatter.3.cloned.1.call-start = ((), (), s32[]{:S(2)}) async-start(), calls=%async_computation.7 | async-start | bytes 19464192 | tf_op jit(solution)/shard_map/reduce_scatter | solution.py:1043
  136.2 22.8 %collective-permute-start.24 = (bf16[160,1024]{1,0:T(8,128)(2,1)S(1)}, bf16[160,1024]{1,0:T(8,128)(2,1)S(1)}, u32[]{:S(2)}, u32[]{:S(2)}) collective-permute-start(bf16[160,1024]{1,0:T(8,128)(2,1)S(1)} %pad_maximum_fusion.12), channel_id=1, source_target_pairs={{0,64},{1,65},{64,0},{65,1},{2,66},{3,67},{66,2},{67,3},{4,68},{5,... | collective-permute-start | bytes 983048 | tf_op jit(solution)/shard_map/ppermute | solution.py:27
  136.3 22.8 %collective-permute-start.25 = (bf16[160,1024]{1,0:T(8,128)(2,1)S(1)}, bf16[160,1024]{1,0:T(8,128)(2,1)S(1)}, u32[]{:S(2)}, u32[]{:S(2)}) collective-permute-start(bf16[160,1024]{1,0:T(8,128)(2,1)S(1)} %pad_maximum_fusion.12), channel_id=1, source_target_pairs={{0,65},{1,64},{64,1},{65,0},{2,67},{3,66},{66,3},{67,2},{4,69},{5,... | collective-permute-start | bytes 983048 | tf_op jit(solution)/shard_map/ppermute | solution.py:27
  159.1 22.7 %collective-permute-start.26 = (bf16[80,1024]{1,0:T(8,128)(2,1)S(1)}, bf16[80,1024]{1,0:T(8,128)(2,1)S(1)}, u32[]{:S(2)}, u32[]{:S(2)}) collective-permute-start(bf16[80,1024]{1,0:T(8,128)(2,1)S(1)} %slice.178), channel_id=1, source_target_pairs={{0,64},{1,65},{64,0},{65,1},{2,66},{3,67},{66,2},{67,3},{4,68},{5,... | collective-permute-start | bytes 491528 | tf_op jit(solution)/shard_map/ppermute | solution.py:27
  160.4 21.3 %collective-permute-start.27 = (bf16[80,1024]{1,0:T(8,128)(2,1)S(1)}, bf16[80,1024]{1,0:T(8,128)(2,1)S(1)}, u32[]{:S(2)}, u32[]{:S(2)}) collective-permute-start(bf16[80,1024]{1,0:T(8,128)(2,1)S(1)} %slice.179), channel_id=1, source_target_pairs={{0,65},{1,64},{64,1},{65,0},{2,67},{3,66},{66,3},{67,2},{4,69},{5,... | collective-permute-start | bytes 491528 | tf_op jit(solution)/shard_map/ppermute | solution.py:27
  183.0 26.9 %collective-permute-start.33 = (bf16[320,1024]{1,0:T(8,128)(2,1)S(1)}, bf16[320,1024]{1,0:T(8,128)(2,1)S(1)}, u32[]{:S(2)}, u32[]{:S(2)}) collective-permute-start(bf16[320,1024]{1,0:T(8,128)(2,1)S(1)} %get-tuple-element.259), channel_id=1, source_target_pairs={{0,32},{32,0},{1,33},{33,1},{2,34},{34,2},{3,35},{35,3},{4,36},{36... | collective-permute-start | bytes 1966088 | tf_op jit(solution)/shard_map/ppermute | solution.py:27
  246.9 26.4 %collective-permute-start.39 = (bf16[80,1024]{1,0:T(8,128)(2,1)S(1)}, bf16[80,1024]{1,0:T(8,128)(2,1)S(1)}, u32[]{:S(2)}, u32[]{:S(2)}) collective-permute-start(bf16[80,1024]{1,0:T(8,128)(2,1)S(1)} %get-tuple-element.270), channel_id=1, source_target_pairs={{0,64},{1,65},{64,0},{65,1},{2,66},{3,67},{66,2},{67,3},{4,68},{5,... | collective-permute-start | bytes 491528 | tf_op jit(solution)/shard_map/ppermute | solution.py:27
  248.2 25.1 %collective-permute-start.40 = (bf16[80,1024]{1,0:T(8,128)(2,1)S(1)}, bf16[80,1024]{1,0:T(8,128)(2,1)S(1)}, u32[]{:S(2)}, u32[]{:S(2)}) collective-permute-start(bf16[80,1024]{1,0:T(8,128)(2,1)S(1)} %get-tuple-element.269), channel_id=1, source_target_pairs={{0,65},{1,64},{64,1},{65,0},{2,67},{3,66},{66,3},{67,2},{4,69},{5,... | collective-permute-start | bytes 491528 | tf_op jit(solution)/shard_map/ppermute | solution.py:27
  273.3 218.5 %reduce-scatter.5.cloned.1.call-start = ((), (), s32[]{:S(2)}) async-start(), calls=%async_computation.8 | async-start | bytes 5406720 | tf_op jit(solution)/shard_map/reduce_scatter | solution.py:1092
  275.9 31.1 %collective-permute-start.42 = (bf16[160,1024]{1,0:T(8,128)(2,1)S(1)}, bf16[160,1024]{1,0:T(8,128)(2,1)S(1)}, u32[]{:S(2)}, u32[]{:S(2)}) collective-permute-start(bf16[160,1024]{1,0:T(8,128)(2,1)S(1)} %pad_maximum_fusion.14), channel_id=1, source_target_pairs={{0,65},{1,64},{64,1},{65,0},{2,67},{3,66},{66,3},{67,2},{4,69},{5,... | collective-permute-start | bytes 983048 | tf_op jit(solution)/shard_map/ppermute | solution.py:27
  277.0 30.1 %collective-permute-start.41 = (bf16[160,1024]{1,0:T(8,128)(2,1)S(1)}, bf16[160,1024]{1,0:T(8,128)(2,1)S(1)}, u32[]{:S(2)}, u32[]{:S(2)}) collective-permute-start(bf16[160,1024]{1,0:T(8,128)(2,1)S(1)} %pad_maximum_fusion.13), channel_id=1, source_target_pairs={{0,64},{1,65},{64,0},{65,1},{2,66},{3,67},{66,2},{67,3},{4,68},{5,... | collective-permute-start | bytes 983048 | tf_op jit(solution)/shard_map/ppermute | solution.py:27
  328.2 19.7 %collective-permute-start.51 = (bf16[160,2048]{1,0:T(8,128)(2,1)}, bf16[160,2048]{1,0:T(8,128)(2,1)S(1)}, u32[]{:S(2)}, u32[]{:S(2)}) collective-permute-start(bf16[160,2048]{1,0:T(8,128)(2,1)} %pad_maximum_fusion.10), channel_id=1, source_target_pairs={{0,65},{1,64},{64,1},{65,0},{2,67},{3,66},{66,3},{67,2},{4,69},{5,... | collective-permute-start | bytes 1966088 | tf_op jit(solution)/shard_map/ppermute | solution.py:27
  331.1 17.0 %collective-permute-start.50 = (bf16[160,2048]{1,0:T(8,128)(2,1)}, bf16[160,2048]{1,0:T(8,128)(2,1)}, u32[]{:S(2)}, u32[]{:S(2)}) collective-permute-start(bf16[160,2048]{1,0:T(8,128)(2,1)} %pad_maximum_fusion.9), channel_id=1, source_target_pairs={{0,64},{1,65},{64,0},{65,1},{2,66},{3,67},{66,2},{67,3},{4,68},{5,... | collective-permute-start | bytes 1966088 | tf_op jit(solution)/shard_map/ppermute | solution.py:27
  335.8 12.2 %collective-permute-start.49 = (f32[2,4096]{1,0:T(2,128)S(1)}, f32[2,4096]{1,0:T(2,128)S(1)}, u32[]{:S(2)}, u32[]{:S(2)}) collective-permute-start(f32[2,4096]{1,0:T(2,128)S(1)} %add.370), channel_id=1, source_target_pairs={{0,6},{2,4},{4,2},{6,0},{1,7},{3,5},{5,3},{7,1},{8,14},{10,12},{12... | collective-permute-start | bytes 98312 | tf_op jit(solution)/shard_map/ppermute | solution.py:27
  363.9 17.1 %collective-permute-start.57 = (bf16[160,512]{1,0:T(8,128)(2,1)}, bf16[160,512]{1,0:T(8,128)(2,1)S(1)}, u32[]{:S(2)}, u32[]{:S(2)}) collective-permute-start(bf16[160,512]{1,0:T(8,128)(2,1)} %get-tuple-element.205.u0), channel_id=1, source_target_pairs={{0,64},{1,65},{64,0},{65,1},{2,66},{3,67},{66,2},{67,3},{4,68},{5,... | collective-permute-start | bytes 491528 | tf_op jit(solution)/shard_map/ppermute | solution.py:27
  364.2 16.7 %collective-permute-start.58 = (bf16[160,512]{1,0:T(8,128)(2,1)}, bf16[160,512]{1,0:T(8,128)(2,1)S(1)}, u32[]{:S(2)}, u32[]{:S(2)}) collective-permute-start(bf16[160,512]{1,0:T(8,128)(2,1)} %get-tuple-element.205.u0), channel_id=1, source_target_pairs={{0,1},{1,0},{64,65},{65,64},{2,3},{3,2},{66,67},{67,66},{4,5},{5,4... | collective-permute-start | bytes 491528 | tf_op jit(solution)/shard_map/ppermute | solution.py:27
  366.0 15.0 %collective-permute-start.59 = (bf16[160,512]{1,0:T(8,128)(2,1)}, bf16[160,512]{1,0:T(8,128)(2,1)S(1)}, u32[]{:S(2)}, u32[]{:S(2)}) collective-permute-start(bf16[160,512]{1,0:T(8,128)(2,1)} %get-tuple-element.205.u0), channel_id=1, source_target_pairs={{0,65},{1,64},{64,1},{65,0},{2,67},{3,66},{66,3},{67,2},{4,69},{5,... | collective-permute-start | bytes 491528 | tf_op jit(solution)/shard_map/ppermute | solution.py:27
  396.5 34.7 %collective-permute-start.70 = (bf16[160,3072]{1,0:T(8,128)(2,1)S(1)}, bf16[160,3072]{1,0:T(8,128)(2,1)}, u32[]{:S(2)}, u32[]{:S(2)}) collective-permute-start(bf16[160,3072]{1,0:T(8,128)(2,1)S(1)} %pad_maximum_fusion.5), channel_id=1, source_target_pairs={{0,0},{1,64},{32,1},{33,65},{64,32},{65,96},{96,33},{97,97},{2,2},... | collective-permute-start | bytes 2949128 | tf_op jit(solution)/shard_map/ppermute | solution.py:69
  434.0 11.3 %collective-permute-start.72 = (f32[2,512]{1,0:T(2,128)S(1)}, f32[2,512]{1,0:T(2,128)S(1)}, u32[]{:S(2)}, u32[]{:S(2)}) collective-permute-start(f32[2,512]{1,0:T(2,128)S(1)} %add.393), channel_id=1, source_target_pairs={{0,6},{2,4},{4,2},{6,0},{1,7},{3,5},{5,3},{7,1},{8,14},{10,12},{12... | collective-permute-start | bytes 12296 | tf_op jit(solution)/shard_map/ppermute | solution.py:27
  435.9 13.8 %collective-permute-start.73 = (bf16[64,4608]{1,0:T(8,128)(2,1)}, bf16[64,4608]{1,0:T(8,128)(2,1)}, u32[]{:S(2)}, u32[]{:S(2)}) collective-permute-start(bf16[64,4608]{1,0:T(8,128)(2,1)} %reduce-scatter.3.cloned.1.call-done.refs_0_), channel_id=1, source_target_pairs={{0,64},{33,97},{64,0},{97,33},{2,66},{35,99},{66,2},{99,35},{4,68}... | collective-permute-start | bytes 1769480 | tf_op jit(solution)/shard_map/ppermute | solution.py:1147
  437.4 16.8 %collective-permute-start.74 = (bf16[64,4608]{1,0:T(8,128)(2,1)}, bf16[64,4608]{1,0:T(8,128)(2,1)}, u32[]{:S(2)}, u32[]{:S(2)}) collective-permute-start(bf16[64,4608]{1,0:T(8,128)(2,1)} %reduce-scatter.3.cloned.1.call-done.refs_0_), channel_id=1, source_target_pairs={{1,0},{32,33},{65,64},{96,97},{3,2},{34,35},{67,66},{98,99},{5,4},... | collective-permute-start | bytes 1769480 | tf_op jit(solution)/shard_map/ppermute | solution.py:1147
  443.3 13.9 %collective-permute-start.75 = (bf16[64,4608]{1,0:T(8,128)(2,1)}, bf16[64,4608]{1,0:T(8,128)(2,1)}, u32[]{:S(2)}, u32[]{:S(2)}) collective-permute-start(bf16[64,4608]{1,0:T(8,128)(2,1)} %reduce-scatter.3.cloned.1.call-done.refs_0_), channel_id=1, source_target_pairs={{1,64},{32,97},{65,0},{96,33},{3,66},{34,99},{67,2},{98,35},{5,68}... | collective-permute-start | bytes 1769480 | tf_op jit(solution)/shard_map/ppermute | solution.py:1147
  460.5 24.2 %collective-permute-start.76 = (bf16[4,64,4608]{2,1,0:T(8,128)(2,1)}, bf16[4,64,4608]{2,1,0:T(8,128)(2,1)}, u32[]{:S(2)}, u32[]{:S(2)}) collective-permute-start(bf16[4,64,4608]{2,1,0:T(8,128)(2,1)} %pad_maximum_fusion), channel_id=1, source_target_pairs={{0,32},{33,1},{64,96},{97,65},{2,34},{35,3},{66,98},{99,67},{4,36}... | collective-permute-start | bytes 7077896 | tf_op jit(solution)/shard_map/ppermute | solution.py:1155
  463.3 41.2 %all-to-all-start.1 = ((bf16[32,16,2176]{2,1,0:T(8,128)(2,1)}), bf16[32,16,2176]{2,1,0:T(8,128)(2,1)S(1)}, u32[]{:S(2)}, u32[]{:S(2)}) async-start(bf16[32,16,2176]{2,1,0:T(8,128)(2,1)} %bitcast.89), calls=%async_computation.2 | async-start | bytes 4456448 | tf_op jit(solution)/shard_map/all_to_all | solution.py:858
  (112 other events, 1151.3 us)
Sparse Core Ops, SparseCore 0:
  19.6 61.2 all-gather.3
  83.2 76.8 all-gather.5
  162.9 46.9 all-gather.7
  273.4 122.1 reduce-scatter.2
  399.7 92.1 reduce-scatter.4
